TPU v7x, 32 devices: a whole 2x2x4 slice. The times are simulated.
32 devices in a mesh: ens: 2 (over y), dom: 16 (over z, x, core).
Axes of the slice: x: 2, y: 2, z: 4, core: 2. Of those that a mesh axis runs over, the one named last changes fastest.
Arguments:
- grid_feat: bfloat16 [32768, 227], P(('ens', 'dom')), parts along dimension 0, may hold values from -6 to 6
- mesh_latent: bfloat16 [16384, 512], P(('ens', 'dom')), parts along dimension 0, may hold values from -6 to 6
- cotangent: bfloat16 [16384, 512], P(('ens', 'dom')), parts along dimension 0, may hold values from -0.15625 to 0.15625
- row_pack: int32 [1024], P('dom'), may hold values from -1 to 1023, as said below
- edge_src: int32 [64, 1024], P('dom'), may hold values from 0 to 1087, as said below
- edge_dst: int32 [64, 1024], P('dom'), may hold values from 0 to 127
- edge_count: int32 [64], P('dom'), may hold values from 512 to 1024
- w_embed: bfloat16 [227, 512], replicated, may hold values from -0.375 to 0.375
- b_embed: bfloat16 [512], replicated, may hold values from -4 to 4
- w_src: bfloat16 [512, 512], replicated, may hold values from -0.25 to 0.25
- w_dst: bfloat16 [512, 512], replicated, may hold values from -0.25 to 0.25
- b_hidden: bfloat16 [512], replicated, may hold values from -4 to 4
- w_out: bfloat16 [512, 512], replicated, may hold values from -0.25 to 0.25
Outputs:
- mesh_out: bfloat16 [16384, 512], P(('ens', 'dom')), parts along dimension 0
- grad_embed: float32 [454, 512], P('ens'), parts along dimension 0
- grad_src: float32 [1024, 512], P('ens'), parts along dimension 0
- grad_dst: float32 [1024, 512], P('ens'), parts along dimension 0
- grad_out: float32 [1024, 512], P('ens'), parts along dimension 0
- grad_biases: float32 [4, 512], P('ens'), parts along dimension 0
There are 2 independent parts, one for each index of `ens`. A program takes and returns all parts, laid end to end along the dimension named above; an argument that names none is the same for every part. Nothing has to cross between parts.
Inputs may be any that keep to these rules, and one draw needn't show every extreme that they name: `row_pack`: entries of band s, in order of partition d and slot k: the local row of s that goes to d, or -1; filled slots of a pair come first; no row is named twice; a band sends nothing to itself. `edge_src`: edges name only filled buffer rows, and never a home row that its band sends away.
All inputs are finite; a program needn't handle non-finite values.
Results may differ from a plain program's by a relative error of at most 0.0062.
Values may be sent and summed in bfloat16 or wider, within the bound.
No kernel may reach another device: no remote copies, remote signals or barrier semaphores. Data moves between devices by JAX's collectives and lax.ppermute only.
A program may use at most 128 MiB of HBM per device.

v0:
```python
import jax
import jax.numpy as jnp
from jax import lax
from jax.sharding import PartitionSpec as P


def silu_slope(values):
    sig = jax.nn.sigmoid(values)
    return sig * (1.0 + values * (1.0 - sig))


def rows_product(left, right):
    return lax.dot_general(
        left, right, (((0,), (0,)), ((), ())), preferred_element_type=jnp.float32
    )


def shards(
    grid_feat,
    mesh_latent,
    cotangent,
    row_pack,
    edge_src,
    edge_dst,
    edge_count,
    w_embed,
    b_embed,
    w_src,
    w_dst,
    b_hidden,
    w_out,
):
    device_count = lax.axis_size("dom")
    grid_rows, channels = grid_feat.shape
    latent_width = w_src.shape[1]
    peer_slots = row_pack.shape[0] // device_count
    block_count, edge_slots = edge_src.shape
    block_nodes = mesh_latent.shape[0] // block_count
    filled = row_pack >= 0
    pick_rows = jnp.maximum(row_pack, 0)
    embed_bias = b_embed.astype(jnp.float32)
    pre_own = jnp.dot(grid_feat, w_embed, preferred_element_type=jnp.float32) + embed_bias
    latent_own = jax.nn.silu(pre_own).astype(jnp.bfloat16)
    send_rows = latent_own[pick_rows].reshape(device_count, peer_slots, latent_width)
    latent_in = lax.all_to_all(send_rows, "dom", split_axis=0, concat_axis=0, tiled=True).reshape(
        device_count * peer_slots, latent_width
    )
    buffer = jnp.concatenate([latent_own, latent_in], axis=0)
    proj_src = jnp.dot(buffer, w_src, preferred_element_type=jnp.float32).astype(jnp.bfloat16)
    proj_dst = jnp.dot(mesh_latent, w_dst, preferred_element_type=jnp.float32).astype(jnp.bfloat16)
    proj_dst = proj_dst.reshape(block_count, block_nodes, latent_width)
    live_edge = lax.broadcasted_iota(jnp.int32, (block_count, edge_slots), 1) < edge_count[:, None]
    node_iota = lax.broadcasted_iota(jnp.int32, (1, 1, block_nodes), 2)
    one_hot = ((edge_dst[:, :, None] == node_iota) & live_edge[:, :, None]).astype(jnp.bfloat16)
    flat_src = edge_src.reshape(-1)
    near_terms = jnp.einsum("ben,bnl->bel", one_hot, proj_dst, preferred_element_type=jnp.float32)
    pre_edge = (
        proj_src[flat_src].astype(jnp.float32).reshape(block_count, edge_slots, latent_width)
        + near_terms
        + b_hidden.astype(jnp.float32)
    )
    hidden = jax.nn.silu(pre_edge).astype(jnp.bfloat16)
    message = jnp.einsum("bel,lm->bem", hidden, w_out, preferred_element_type=jnp.float32)
    message_high = message.astype(jnp.bfloat16)
    message_low = (message - message_high.astype(jnp.float32)).astype(jnp.bfloat16)
    gathered = jnp.einsum(
        "ben,bem->bnm", one_hot, message_high, preferred_element_type=jnp.float32
    ) + jnp.einsum("ben,bem->bnm", one_hot, message_low, preferred_element_type=jnp.float32)
    mesh_out = (mesh_latent.astype(jnp.float32) + gathered.reshape(-1, latent_width)).astype(
        jnp.bfloat16
    )
    cot_rows = cotangent.reshape(block_count, block_nodes, latent_width)
    msg_grad = jnp.einsum(
        "ben,bnl->bel", one_hot, cot_rows, preferred_element_type=jnp.float32
    ).astype(jnp.bfloat16)
    grad_out = jnp.einsum("bel,bem->lm", hidden, msg_grad, preferred_element_type=jnp.float32)
    hidden_grad = jnp.einsum("bem,lm->bel", msg_grad, w_out, preferred_element_type=jnp.float32)
    pre_grad = (hidden_grad * silu_slope(pre_edge)).astype(jnp.bfloat16)
    bias_hidden = jnp.sum(pre_grad, axis=(0, 1), dtype=jnp.float32)
    node_grad = jnp.einsum(
        "ben,bel->bnl", one_hot, pre_grad, preferred_element_type=jnp.float32
    ).astype(jnp.bfloat16)
    grad_dst = rows_product(mesh_latent, node_grad.reshape(-1, latent_width))
    slot_grad = jax.ops.segment_sum(
        pre_grad.reshape(-1, latent_width).astype(jnp.float32),
        flat_src,
        num_segments=buffer.shape[0],
    ).astype(jnp.bfloat16)
    grad_src = rows_product(buffer, slot_grad)
    buffer_grad = lax.dot_general(
        slot_grad, w_src, (((1,), (1,)), ((), ())), preferred_element_type=jnp.float32
    )
    back_rows = buffer_grad[grid_rows:].reshape(device_count, peer_slots, latent_width)
    returned = (
        lax.all_to_all(
            back_rows.astype(jnp.bfloat16), "dom", split_axis=0, concat_axis=0, tiled=True
        )
        .astype(back_rows.dtype)
        .reshape(-1, latent_width)
    )
    latent_grad = (
        buffer_grad[:grid_rows]
        .at[pick_rows]
        .add(jnp.where(filled[:, None], returned, jnp.float32(0.0)))
    )
    embed_own = (latent_grad * silu_slope(pre_own)).astype(jnp.bfloat16)
    grad_embed = rows_product(grid_feat, embed_own)
    bias_embed = jnp.sum(embed_own, axis=0, dtype=jnp.float32)
    bias_stack = jnp.stack([bias_embed, bias_hidden])
    totals = lax.psum((grad_embed, grad_src, grad_dst, grad_out, bias_stack), "dom")
    return (mesh_out, totals[0], totals[1], totals[2], totals[3], totals[4])


def solution(mesh):
    return jax.shard_map(
        shards,
        mesh=mesh,
        in_specs=(
            P(("ens", "dom"), None),
            P(("ens", "dom"), None),
            P(("ens", "dom"), None),
            P("dom"),
            P("dom", None),
            P("dom", None),
            P("dom"),
            P(),
            P(),
            P(),
            P(),
            P(),
            P(),
        ),
        out_specs=(
            P(("ens", "dom"), None),
            P("ens", None),
            P("ens", None),
            P("ens", None),
            P("ens", None),
            P("ens", None),
        ),
        check_vma=False,
    )
```

profile of v0, /device:TPU:0, one launch (start us, length us, event | category | flops | bytes accessed | tf_op | source)
XLA Modules:
  0.0 236.4 jit_solution(10630594701099004073)
XLA Ops:
  7.2 0.7 convert_element_type.74
  7.9 0.7 broadcast_maximum_fusion
  8.7 3.6 %multiply_convert_fusion.3 = (bf16[1024,512]{1,0:T(8,128)(2,1)}, f32[1024,512]{1,0:T(8,128)}) fusion(f32[512]{0:T(512)S(1)} %convert_element_type.74, bf16[1024,227]{0,1:T(8,128)(2,1)} %param.13, bf16[227,512]{1,0:T(8,128)(2,1)} %param.20), kind=kOutput, calls=%fused_computation.19 | convolution fusion | flops 241172480 | bytes 3845120 | tf_op jit(solution)/shard_map/dot_general | solution.py:42
  12.2 2.1 gather_fusion
  14.4 0.7 reshape.99
  15.0 7.4 %all-to-all-start = ((bf16[16,4,512]{2,1,0:T(4,128)(2,1)}), bf16[16,4,512]{2,1,0:T(4,128)(2,1)S(1)}, u32[]{:S(2)}, u32[]{:S(2)}) async-start(bf16[16,4,512]{2,1,0:T(4,128)(2,1)} %reshape.99), calls=%async_computation | async-start | bytes 131072 | tf_op jit(solution)/shard_map/all_to_all | solution.py:45
  23.0 3.3 %convolution_convert_fusion.1 = bf16[4,1024,512]{2,1,0:T(8,128)(2,1)} fusion(bf16[4,128,512]{2,1,0:T(8,128)(2,1)S(1)} %bitcast.57, s32[4,1024]{1,0:T(4,128)S(1)} %copy-done.12, pred[4,1024]{1,0:T(4,128)(4,1)S(1)} %iota_compare_fusion.1), kind=kOutput, calls=%fused_computation.12 | convolution fusion | flops 540016640 | bytes 4739072 | tf_op jit(solution)/shard_map/ben,bnl->bel/dot_general | solution.py:73
  26.3 2.9 %all-to-all-done = bf16[16,4,512]{2,1,0:T(4,128)(2,1)S(1)} async-done(((bf16[16,4,512]{2,1,0:T(4,128)(2,1)}), bf16[16,4,512]{2,1,0:T(4,128)(2,1)S(1)}, u32[]{:S(2)}, u32[]{:S(2)}) %all-to-all-start) | async-done | bytes 65568 | tf_op jit(solution)/shard_map/all_to_all | solution.py:45
  29.3 2.0 convolution_convert_fusion
  31.3 17.4 %gather_fusion.1 = bf16[4096,512]{1,0:T(8,128)(2,1)} fusion(bf16[1088,512]{1,0:T(8,128)(2,1)S(1)} %convolution_convert_fusion, s32[4096]{0:T(1024)S(1)} %broadcast_clamp_fusion), kind=kCustom, calls=%fused_computation.1 | custom fusion | bytes 8404992 | tf_op jit(solution)/shard_map/gather | solution.py:58
  48.6 6.2 %multiply_convert_fusion.1 = (bf16[4,1024,512]{2,1,0:T(8,128)(2,1)}, f32[4,1024,512]{2,1,0:T(8,128)S(1)}) fusion(bf16[4,1024,512]{2,1,0:T(8,128)(2,1)} %bitcast.52, f32[512]{0:T(512)S(1)} %convert_element_type.80, bf16[4,128,512]{2,1,0:T(8,128)(2,1)S(1)} %bitcast.55, s32[4,1024]{1,0:T(4,128)S(1)} %copy-done.12, pred[4,1024]{1,0:T(4,128)(4,1)S(1)} %iota_compare_fusion.1), kind=kOutput, calls=%fused_computation.8 | convolution fusion | flops 554696704 | bytes 17324032 | tf_op jit(solution)/shard_map/ben,bnl->bel/dot_general | solution.py:56
  54.8 6.1 %convert_reduce_fusion = (f32[512]{0:T(512)S(1)}, bf16[4,1024,512]{2,1,0:T(8,128)(2,1)}) fusion(f32[512]{0:T(512)S(1)} %convert_element_type.80, f32[4,1024,512]{2,1,0:T(8,128)S(1)} %get-tuple-element.21, bf16[4,1024,512]{2,1,0:T(8,128)(2,1)S(1)} %bitcast.53, bf16[4,1024,512]{2,1,0:T(8,128)(2,1)S(1)} %copy-done.1, bf16[512,512]{1,0:T(8,128)(2,1)S(1)} %copy-done), kind=kOutput, calls=%fused_computation.13 | convolution fusion | flops 2176843264 | bytes 21499904 | tf_op jit(solution)/shard_map/bem,lm->bel/dot_general | solution.py:77
  60.9 26.3 %scatter_custom_fusion = f32[1088,512]{1,0:T(8,128)S(1)} fusion(s32[4096]{0:T(1024)S(1)} %bitcast.62, f32[]{:T(128)} %constant.7.clone.1, bf16[4096,512]{1,0:T(8,128)(2,1)} %bitcast.54), kind=kCustom, calls=%fused_computation.32 | custom fusion | flops 4194304 | bytes 6422532 | tf_op jit(solution)/shard_map/scatter-add | solution.py:84
  87.2 2.0 fusion.36
  89.1 3.8 %fusion.34 = f32[512,512]{1,0:T(8,128)} fusion(bf16[64,512]{1,0:T(8,128)(2,1)S(1)} %reshape.100, bf16[1024,512]{1,0:T(8,128)(2,1)} %get-tuple-element.18, f32[1088,512]{1,0:T(8,128)S(1)} %scatter_custom_fusion), kind=kOutput, calls=%fused_computation.46 | convolution fusion | flops 573210624 | bytes 4390912 | tf_op jit(solution)/shard_map/dot_general | solution.py:13
  93.0 1.6 fusion.18
  95.2 3.5 %all-to-all-start.1 = ((bf16[16,4,512]{2,1,0:T(4,128)(2,1)}), bf16[16,4,512]{2,1,0:T(4,128)(2,1)S(1)}, u32[]{:S(2)}, u32[]{:S(2)}) async-start(bf16[16,4,512]{2,1,0:T(4,128)(2,1)} %convert_element_type.91), calls=%async_computation.1 | async-start | bytes 131072 | tf_op jit(solution)/shard_map/all_to_all | solution.py:95
  98.8 6.8 %convolution_bitcast_fusion = f32[512,512]{1,0:T(8,128)} fusion(bf16[4,1024,512]{2,1,0:T(8,128)(2,1)} %get-tuple-element.20, bf16[4,1024,512]{2,1,0:T(8,128)(2,1)} %convolution_convert_fusion.1), kind=kOutput, calls=%fused_computation.25 | convolution fusion | flops 2147483648 | bytes 9437184 | tf_op jit(solution)/shard_map/bel,bem->lm/dot_general | solution.py:76
  105.6 1.4 convolution_bitcast_fusion.1
  107.6 1.8 scatter_custom_fusion.1
  109.4 2.5 %convert_reduce_fusion.1 = (f32[512]{0:T(512)S(1)}, bf16[1024,512]{1,0:T(8,128)(2,1)S(1)}) fusion(f32[1024,512]{1,0:T(8,128)S(1)} %scatter_custom_fusion.1, f32[1024,512]{1,0:T(8,128)} %get-tuple-element.19, f32[512]{0:T(512)S(1)} %convert_element_type.74), kind=kLoop, calls=%fused_computation.14 | loop fusion | flops 6290944 | bytes 5246976 | tf_op jit(solution)/shard_map/reduce_sum | solution.py:108
  111.9 1.2 convolution_bitcast_fusion.2
  113.1 4.5 %fusion.39 = f32[4,1024,512]{2,1,0:T(8,128)S(1)} fusion(bf16[4,1024,512]{2,1,0:T(8,128)(2,1)} %get-tuple-element.20, bf16[512,512]{1,0:T(8,128)(2,1)S(1)} %copy-done), kind=kOutput, calls=%fused_computation.51 | convolution fusion | flops 2147483648 | bytes 13107200 | tf_op jit(solution)/shard_map/bel,lm->bem/dot_general | solution.py:63
  117.6 0.9 fusion.1
  118.6 0.8 fusion.13
  119.3 1.0 fusion.23
  120.3 35.1 %psum.39 = f32[2,512]{1,0:T(2,128)} all-reduce(f32[2,512]{1,0:T(2,128)S(1)} %pad_maximum_fusion.3), channel_id=1, replica_groups=mesh['ens'=2,'dom'=16] {'dom'}, use_global_device_ids=true, to_apply=%region_8.9 | all-reduce | flops 1024 | bytes 8192 | tf_op jit(solution)/shard_map/psum | solution.py:110
  155.5 66.4 %all-reduce.3.cloned.1.call-done = (f32[227,512]{1,0:T(8,128)}, f32[512,512]{1,0:T(8,128)}, f32[512,512]{0,1:T(8,128)}, f32[512,512]{1,0:T(8,128)}) async-done(((f32[227,512]{1,0:T(8,128)}, f32[512,512]{1,0:T(8,128)}, f32[512,512]{0,1:T(8,128)}, f32[512,512]{1,0:T(8,128)}), (f32[227,512]{1,0:T(8,128)}, f32[512,512]{1,0:T(8,128)}, f32[512,512]{0,1:T(8,128)}, ...) | async-done | bytes 3610640 | tf_op jit(solution)/shard_map/psum | solution.py:110
  221.9 2.6 %copy.22 = f32[512,512]{1,0:T(8,128)} copy(f32[512,512]{0,1:T(8,128)} %get-tuple-element.14) | data formatting | bytes 2097152
  224.5 1.8 copy.35
  226.3 2.3 copy.36
  228.6 1.0 copy.37
  (53 shorter events, 1.9 us)
Async XLA Ops:
  7.2 47.6 %copy-start = (bf16[512,512]{1,0:T(8,128)(2,1)S(1)}, bf16[512,512]{1,0:T(8,128)(2,1)}, u32[]{:S(2)}) copy-start(bf16[512,512]{1,0:T(8,128)(2,1)} %param.25) | copy-start | bytes 1572868
  8.6 13.8 %copy-start.13 = (s32[4,1024]{1,0:T(4,128)S(1)}, s32[4,1024]{1,0:T(4,128)}, u32[]{:S(2)}) copy-start(s32[4,1024]{1,0:T(4,128)} %param.17) | copy-start | bytes 49156
  8.6 13.9 %copy-start.15 = (s32[4]{0:T(128)S(1)}, s32[4]{0:T(128)}, u32[]{:S(2)}) copy-start(s32[4]{0:T(128)} %param.19) | copy-start | bytes 52
  8.6 13.9 %copy-start.14 = (bf16[512]{0:T(512)(128)(2,1)S(1)}, bf16[512]{0:T(512)(128)(2,1)}, u32[]{:S(2)}) copy-start(bf16[512]{0:T(512)(128)(2,1)} %param.24) | copy-start | bytes 3076
  8.6 13.9 %copy-start.3 = (bf16[512,512]{1,0:T(8,128)(2,1)S(1)}, bf16[512,512]{1,0:T(8,128)(2,1)}, u32[]{:S(2)}) copy-start(bf16[512,512]{1,0:T(8,128)(2,1)} %param.14) | copy-start | bytes 1572868
  8.6 13.9 %copy-start.7 = (bf16[512,512]{1,0:T(8,128)(2,1)S(1)}, bf16[512,512]{1,0:T(8,128)(2,1)}, u32[]{:S(2)}) copy-start(bf16[512,512]{1,0:T(8,128)(2,1)} %param.23) | copy-start | bytes 1572868
  8.6 14.4 %copy-start.10 = (bf16[512,512]{1,0:T(8,128)(2,1)S(1)}, bf16[512,512]{1,0:T(8,128)(2,1)}, u32[]{:S(2)}) copy-start(bf16[512,512]{1,0:T(8,128)(2,1)} %param.15) | copy-start | bytes 1572868
  8.7 14.4 %copy-start.12 = (s32[4,1024]{1,0:T(4,128)S(1)}, s32[4,1024]{1,0:T(4,128)}, u32[]{:S(2)}) copy-start(s32[4,1024]{1,0:T(4,128)} %param.18) | copy-start | bytes 49156
  12.2 14.1 %copy-start.16 = (s32[64]{0:T(128)S(1)}, s32[64]{0:T(128)}, u32[]{:S(2)}) copy-start(s32[64]{0:T(128)} %param.16) | copy-start | bytes 772
  12.2 17.1 %copy-start.8 = (bf16[512,512]{1,0:T(8,128)(2,1)S(1)}, bf16[512,512]{1,0:T(8,128)(2,1)}, u32[]{:S(2)}) copy-start(bf16[512,512]{1,0:T(8,128)(2,1)} %param.22) | copy-start | bytes 1572868
  15.0 14.3 %all-to-all-start = ((bf16[16,4,512]{2,1,0:T(4,128)(2,1)}), bf16[16,4,512]{2,1,0:T(4,128)(2,1)S(1)}, u32[]{:S(2)}, u32[]{:S(2)}) async-start(bf16[16,4,512]{2,1,0:T(4,128)(2,1)} %reshape.99), calls=%async_computation | async-start | bytes 131072 | tf_op jit(solution)/shard_map/all_to_all | solution.py:45
  48.6 6.2 %copy-start.1 = (bf16[4,1024,512]{2,1,0:T(8,128)(2,1)S(1)}, bf16[4,1024,512]{2,1,0:T(8,128)(2,1)}, u32[]{:S(2)}) copy-start(bf16[4,1024,512]{2,1,0:T(8,128)(2,1)} %convolution_convert_fusion.1) | copy-start | bytes 12582916
  48.6 6.2 %copy-start.4 = (bf16[4096,512]{1,0:T(8,128)(2,1)S(1)}, bf16[4096,512]{1,0:T(8,128)(2,1)}, u32[]{:S(2)}) copy-start(bf16[4096,512]{1,0:T(8,128)(2,1)} %gather_fusion.1) | copy-start | bytes 12582916
  87.1 5.8 %copy-start.5 = (bf16[4,1024,512]{2,1,0:T(8,128)(2,1)S(1)}, bf16[4,1024,512]{2,1,0:T(8,128)(2,1)}, u32[]{:S(2)}) copy-start(bf16[4,1024,512]{2,1,0:T(8,128)(2,1)} %get-tuple-element.23) | copy-start | bytes 12582916
  89.1 5.4 %copy-start.2 = (f32[1088,512]{1,0:T(8,128)}, f32[1088,512]{1,0:T(8,128)S(1)}, u32[]{:S(2)}) copy-start(f32[1088,512]{1,0:T(8,128)S(1)} %fusion.36) | copy-start | bytes 6684676
  95.2 11.8 %all-to-all-start.1 = ((bf16[16,4,512]{2,1,0:T(4,128)(2,1)}), bf16[16,4,512]{2,1,0:T(4,128)(2,1)S(1)}, u32[]{:S(2)}, u32[]{:S(2)}) async-start(bf16[16,4,512]{2,1,0:T(4,128)(2,1)} %convert_element_type.91), calls=%async_computation.1 | async-start | bytes 131072 | tf_op jit(solution)/shard_map/all_to_all | solution.py:95
  98.7 123.1 %all-reduce.3.cloned.1.call-start = ((), (), s32[]{:S(2)}) async-start(), calls=%async_computation.2 | async-start | bytes 7241728 | tf_op jit(solution)/shard_map/psum | solution.py:110
  98.8 6.8 %copy-start.9 = (bf16[4,128,512]{2,1,0:T(8,128)(2,1)S(1)}, bf16[4,128,512]{2,1,0:T(8,128)(2,1)}, u32[]{:S(2)}) copy-start(bf16[4,128,512]{2,1,0:T(8,128)(2,1)} %fusion.18) | copy-start | bytes 1572868
  105.6 2.0 slice-start
  109.4 2.5 %copy-start.11 = (bf16[1024,227]{0,1:T(8,128)(2,1)S(1)}, bf16[1024,227]{0,1:T(8,128)(2,1)}, u32[]{:S(2)}) copy-start(bf16[1024,227]{0,1:T(8,128)(2,1)} %param.13) | copy-start | bytes 1394692
  221.9 6.7 %copy-start.6 = (f32[512,512]{1,0:T(8,128)S(1)}, f32[512,512]{1,0:T(8,128)}, u32[]{:S(2)}) copy-start(f32[512,512]{1,0:T(8,128)} %get-tuple-element.28) | copy-start | bytes 3145732
Sparse Core Ops, SparseCore 0:
  113.2 108.5 all-reduce.2
where the time goes:
time: 237 us; the launch traced here: 236 us
  waiting for transfers between devices  69.4 us (29%)
  matrix products  44.5 us (19%)
  blocking collectives  35.1 us (15%)
  other arithmetic  33 us (14%)
  local copies, waits for them, and re-layouts  29.1 us (12%)
  between operations  14.3 us (6%)
  starting transfers between devices  10.9 us (5%)
    psum x1, waiting for transfers between devices, shards(): lax.psum((grad_embed, grad_src, grad_dst, grad_out, bias_stack), 'dom')  66.4 us
    psum x1, blocking collectives, shards(): lax.psum((grad_embed, grad_src, grad_dst, grad_out, bias_stack), 'dom')  35.1 us
    scatter-add x1, other arithmetic, shards(): jax.ops.segment_sum(pre_grad.reshape(-1, latent_width).astype(jnp.float32...  26.3 us
    gather x1, local copies, waits for them, and re-layouts, shards(): proj_src[flat_src].astype(jnp.float32)  17.4 us
    unnamed x40, local copies, waits for them, and re-layouts  7.79 us
    all_to_all x1, starting transfers between devices, shards(): lax.all_to_all(send_rows, 'dom', split_axis=0, concat_axis=0, tiled=True)  7.36 us
    dot_general x1, matrix products, shards(): jnp.einsum('bel,bem->lm', hidden, msg_grad, preferred_element_type=jnp.fl...  6.83 us
    dot_general x3, matrix products, rows_product(): lax.dot_general(left, right, (((0,), (0,)), ((), ())), preferred_element_...  6.46 us
  transfers between devices with their start and end apart: 3, of which 2 were waited for; matrix products, arithmetic and copies ran while one was open for 8% of the time, Pallas kernels for 0%

commit v1 on v0

v1 whole, which is shorter than its diff:
```python
import functools

import jax
import jax.numpy as jnp
from jax import lax
from jax.experimental import pallas as pl
from jax.experimental.pallas import tpu as pltpu
from jax.sharding import PartitionSpec as P

BF16 = jnp.bfloat16
F32 = jnp.float32
VMEM_BYTES = 60 * 1024 * 1024


def mm(left, right, left_dim=1, right_dim=0):
    return lax.dot_general(
        left, right, (((left_dim,), (right_dim,)), ((), ())), preferred_element_type=F32
    )


def sigmoid(values):
    return 0.5 * jnp.tanh(0.5 * values) + 0.5


def round_up(value, step):
    return -(-value // step) * step


def own_kernel(feat, w_embed, w_src, mesh, w_dst, cot, w_out, latent, proj, near, back):
    rows = feat.shape[0]
    step = 256

    def body(i, carry):
        part = pl.ds(pl.multiple_of(i * step, step), step)
        pre = mm(feat[part, :], w_embed[...])
        lat = (pre * sigmoid(pre)).astype(BF16)
        latent[part, :] = lat
        proj[part, :] = mm(lat, w_src[...]).astype(BF16)
        return carry

    lax.fori_loop(0, rows // step, body, 0)
    near[...] = mm(mesh[...], w_dst[...]).astype(BF16)
    back[...] = mm(cot[...], w_out[...], 1, 1).astype(BF16)


def edge_kernel(
    channels,
    count,
    src,
    dst,
    feat_in,
    feat_own,
    w_embed,
    w_src,
    w_out,
    b_hidden,
    latent_own,
    proj_own,
    near,
    back,
    mesh,
    cot,
    mesh_out,
    grads,
    table,
    latent,
    feat,
    one_hot,
    one_hot_t,
    hid,
    pgrad,
    slot_sum,
    node_sum,
    hid_sum,
    bias_sum,
):
    own = feat_own.shape[0]
    more = feat_in.shape[0]
    slots = own + more
    blocks, edges = src.shape
    width = w_src.shape[0]
    block = mesh.shape[0] // blocks
    depth = table.shape[0]
    step = 256

    feat[0:own, :] = feat_own[...]
    feat[own:slots, :] = feat_in[...]
    latent[0:own, :] = latent_own[...]
    pre_in = mm(feat_in[...], w_embed[...])
    lat_in = (pre_in * sigmoid(pre_in)).astype(BF16)
    latent[own:slots, :] = lat_in
    table[0:own, :] = proj_own[...]
    table[own:slots, :] = mm(lat_in, w_src[...]).astype(BF16)
    tail = depth - slots - block
    tail_row = lax.broadcasted_iota(jnp.int32, (tail, width), 0)
    table[slots + block : depth, :] = jnp.where(
        tail_row == 0, jnp.broadcast_to(b_hidden[...], (tail, width)).astype(F32), 0.0
    ).astype(BF16)
    slot_sum[...] = jnp.zeros_like(slot_sum)
    bias_sum[...] = jnp.zeros_like(bias_sum)

    edge_lane = lax.broadcasted_iota(jnp.int32, (blocks, edges), 1)
    block_row = lax.broadcasted_iota(jnp.int32, (blocks, 1), 0)
    counts = jnp.zeros((blocks, 1), jnp.int32)
    for b in range(blocks):
        counts = jnp.where(block_row == b, count[b], counts)
    src_all = src[...]
    dst_all = jnp.where(edge_lane < counts, dst[...] + slots, -1)
    columns = jnp.transpose(jnp.concatenate([src_all, dst_all], axis=0))

    for b in range(blocks):
        rows = slice(b * block, (b + 1) * block)
        table[slots : slots + block, :] = near[rows, :]
        src_row = src_all[b : b + 1, :]
        dst_row = dst_all[b : b + 1, :]
        back_b = back[rows, :]
        for e in range(0, edges, step):
            src_col = columns[e : e + step, b : b + 1]
            dst_col = columns[e : e + step, blocks + b : blocks + b + 1]
            lane = lax.broadcasted_iota(jnp.int32, (step, depth), 1)
            hot = (lane == src_col) | (lane == dst_col) | (lane == slots + block)
            hot = jnp.where(hot, 1.0, 0.0).astype(BF16)
            one_hot[e : e + step, :] = hot
            pre = mm(hot, table[...])
            grad = mm(hot[:, slots : slots + block], back_b)
            sig = sigmoid(pre)
            act = pre * sig
            hid[e : e + step, :] = act.astype(BF16)
            pgrad[e : e + step, :] = (grad * (sig + act * (1.0 - sig))).astype(BF16)
        for r in range(0, depth, 128):
            sub = lax.broadcasted_iota(jnp.int32, (128, edges), 0) + r
            hot_t = (sub == src_row) | (sub == dst_row) | (sub == slots + block)
            one_hot_t[r : r + 128, :] = jnp.where(hot_t, 1.0, 0.0).astype(BF16)
        slot_sum[...] += mm(one_hot_t[0:slots, :], pgrad[...])
        node = mm(one_hot_t[slots:depth, :], pgrad[...])
        node_sum[rows, :] = node[0:block, :].astype(BF16)
        bias_sum[...] += node[block : block + 8, :]
        hid_sum[rows, :] = mm(one_hot_t[slots : slots + block, :], hid[...]).astype(BF16)

    total = hid_sum[...]
    mesh_out[...] = (mesh[...].astype(F32) + mm(total, w_out[...])).astype(BF16)
    grads[0:width, :] = mm(total, cot[...], 0, 0).astype(BF16)
    grads[width : 2 * width, :] = mm(mesh[...], node_sum[...], 0, 0).astype(BF16)
    slot_grad = slot_sum[...].astype(BF16)
    grads[2 * width : 3 * width, :] = mm(latent[...], slot_grad, 0, 0).astype(BF16)
    buffer_grad = mm(slot_grad, w_src[...], 1, 1)
    pre = mm(feat[...], w_embed[...])
    sig = sigmoid(pre)
    embed = (buffer_grad * (sig * (1.0 + pre * (1.0 - sig)))).astype(BF16)
    padded = feat.shape[1]
    grad_embed = mm(feat[...], embed, 0, 0)
    bias_row = lax.broadcasted_iota(jnp.int32, (padded, width), 0)
    grad_embed = jnp.where(bias_row == channels + 1, bias_sum[0:1, :], grad_embed)
    grads[3 * width : 3 * width + padded, :] = grad_embed.astype(BF16)
    if grads.shape[0] > 3 * width + padded:
        rest = grads.shape[0] - 3 * width - padded
        grads[3 * width + padded :, :] = jnp.zeros((rest, width), BF16)


def shards(
    grid_feat,
    mesh_latent,
    cotangent,
    row_pack,
    edge_src,
    edge_dst,
    edge_count,
    w_embed,
    b_embed,
    w_src,
    w_dst,
    b_hidden,
    w_out,
):
    device_count = lax.axis_size("dom")
    me = lax.axis_index("dom")
    own, channels = grid_feat.shape
    width = w_src.shape[0]
    peer_slots = row_pack.shape[0] // device_count
    more = device_count * peer_slots
    slots = own + more
    blocks, edges = edge_src.shape
    nodes = mesh_latent.shape[0]
    block = nodes // blocks
    padded = round_up(channels + 2, 128)
    depth = round_up(slots + block + 1, 256)
    grad_rows = round_up(3 * width + padded, 16 * device_count)

    feat = jnp.concatenate(
        [grid_feat, jnp.ones((own, 1), BF16), jnp.zeros((own, padded - channels - 1), BF16)], axis=1
    )
    w_pad = jnp.concatenate(
        [w_embed, b_embed[None, :], jnp.zeros((padded - channels - 1, width), BF16)], axis=0
    )
    pick = (row_pack[:, None] == lax.broadcasted_iota(jnp.int32, (1, own), 1)).astype(BF16)
    send = jnp.dot(pick, feat, preferred_element_type=F32).astype(BF16)
    feat_in = lax.all_to_all(
        send.reshape(device_count, peer_slots, padded), "dom", split_axis=0, concat_axis=0, tiled=True
    ).reshape(more, padded)

    vmem = pl.BlockSpec(memory_space=pltpu.VMEM)
    smem = pl.BlockSpec(memory_space=pltpu.SMEM)
    params = pltpu.CompilerParams(vmem_limit_bytes=VMEM_BYTES)
    own_macs = own * width * (padded + width) + 2 * nodes * width * width
    latent, proj, near, back = pl.pallas_call(
        own_kernel,
        out_shape=(
            jax.ShapeDtypeStruct((own, width), BF16),
            jax.ShapeDtypeStruct((own, width), BF16),
            jax.ShapeDtypeStruct((nodes, width), BF16),
            jax.ShapeDtypeStruct((nodes, width), BF16),
        ),
        in_specs=[vmem] * 7,
        out_specs=(vmem,) * 4,
        compiler_params=params,
        cost_estimate=pl.CostEstimate(
            flops=2 * own_macs, bytes_accessed=8 * own * width, transcendentals=own * width
        ),
        name="own_rows",
    )(feat, w_pad, w_src, mesh_latent, w_dst, cotangent, w_out)

    edge_macs = blocks * edges * width * (2 * depth + 2 * block)
    mesh_out, grads = pl.pallas_call(
        functools.partial(edge_kernel, channels),
        out_shape=(
            jax.ShapeDtypeStruct((nodes, width), BF16),
            jax.ShapeDtypeStruct((grad_rows, width), BF16),
        ),
        in_specs=[smem] + [vmem] * 14,
        out_specs=(vmem,) * 2,
        scratch_shapes=[
            pltpu.VMEM((depth, width), BF16),
            pltpu.VMEM((slots, width), BF16),
            pltpu.VMEM((slots, padded), BF16),
            pltpu.VMEM((edges, depth), BF16),
            pltpu.VMEM((depth, edges), BF16),
            pltpu.VMEM((edges, width), BF16),
            pltpu.VMEM((edges, width), BF16),
            pltpu.VMEM((slots, width), F32),
            pltpu.VMEM((nodes, width), BF16),
            pltpu.VMEM((nodes, width), BF16),
            pltpu.VMEM((8, width), F32),
        ],
        compiler_params=params,
        cost_estimate=pl.CostEstimate(
            flops=2 * edge_macs, bytes_accessed=8 * own * width, transcendentals=blocks * edges * width
        ),
        name="edge_rows",
    )(
        edge_count,
        edge_src,
        edge_dst,
        feat_in,
        feat,
        w_pad,
        w_src,
        w_out,
        b_hidden[None, :],
        latent,
        proj,
        near,
        back,
        mesh_latent,
        cotangent,
    )

    core = me % 2
    swap = [(i, i ^ 1) for i in range(device_count)]
    half = grad_rows // 2
    chips = device_count // 2
    groups = [[2 * c + k for c in range(chips)] for k in range(2)]
    kept = lax.dynamic_slice_in_dim(grads, core * half, half, 0)
    sent = lax.dynamic_slice_in_dim(grads, (1 - core) * half, half, 0)
    got = lax.ppermute(sent, "dom", swap)
    pair = (kept.astype(F32) + got.astype(F32)).astype(BF16)
    parts = lax.all_to_all(
        pair.reshape(chips, half // chips, width),
        "dom",
        split_axis=0,
        concat_axis=0,
        axis_index_groups=groups,
        tiled=True,
    )
    mine = jnp.sum(parts.astype(F32), axis=0).astype(BF16)
    spread = lax.all_to_all(
        jnp.broadcast_to(mine[None], parts.shape),
        "dom",
        split_axis=0,
        concat_axis=0,
        axis_index_groups=groups,
        tiled=True,
    ).reshape(half, width)
    other = lax.ppermute(spread, "dom", swap)
    low = jnp.where(core == 0, spread, other)
    high = jnp.where(core == 0, other, spread)
    total = jnp.concatenate([low, high], axis=0).astype(F32)
    base = 3 * width
    return (
        mesh_out,
        total[base : base + channels],
        total[2 * width : base],
        total[width : 2 * width],
        total[0:width],
        total[base + channels : base + channels + 2],
    )


def solution(mesh):
    return jax.shard_map(
        shards,
        mesh=mesh,
        in_specs=(
            P(("ens", "dom"), None),
            P(("ens", "dom"), None),
            P(("ens", "dom"), None),
            P("dom"),
            P("dom", None),
            P("dom", None),
            P("dom"),
            P(),
            P(),
            P(),
            P(),
            P(),
            P(),
        ),
        out_specs=(
            P(("ens", "dom"), None),
            P("ens", None),
            P("ens", None),
            P("ens", None),
            P("ens", None),
            P("ens", None),
        ),
        check_vma=False,
    )
```

time: 237 us -> 108 us (0.46)
  waiting for transfers between devices: 69.4 us -> 4.78 us
  matrix products: 44.5 us -> 0.24 us
  other arithmetic: 33 us -> 3.45 us
  Pallas kernels: 0 us -> 28.1 us
  local copies, waits for them, and re-layouts: 29.1 us -> 7.34 us
  blocking collectives: 35.1 us -> 55.5 us
  between operations: 14.3 us -> 0.76 us
  starting transfers between devices: 10.9 us -> 7.76 us
    psum x1 -> x0, waiting for transfers between devices: 66.4 us -> none  [shards(): lax.psum((grad_embed, grad_src, grad_dst, grad_out, bias_stack), 'dom')]
    all_to_all x0 -> x2, blocking collectives: none -> 55.5 us  [the longest x1 29.3 us: shards(): lax.all_to_all(pair.reshape(chips, half // chips, width), 'dom', split_ax...]
    dot_general x15 -> x1, matrix products: 44.5 us -> 0.24 us  [shards(): send = jnp.dot(pick, feat, preferred_element_type=F32).astype(BF16)]
    psum x1 -> x0, blocking collectives: 35.1 us -> none  [shards(): lax.psum((grad_embed, grad_src, grad_dst, grad_out, bias_stack), 'dom')]
    pallas_call x0 -> x2, Pallas kernels: none -> 28.1 us  [the longest x1 22.9 us: shards(): pl.pallas_call(functools.partial(edge_kernel, channels), out_shape=(jax.S...]
    scatter-add x2 -> x0, other arithmetic: 28.1 us -> none  [the longest x1 26.3 us: shards(): jax.ops.segment_sum(pre_grad.reshape(-1, latent_width).astype(jnp.float32...]
    gather x2 -> x0, local copies, waits for them, and re-layouts: 19.5 us -> none  [the longest x1 17.4 us: shards(): proj_src[flat_src].astype(jnp.float32)]
    unnamed x40 -> x13, local copies, waits for them, and re-layouts: 7.79 us -> 1.25 us
  transfers between devices with their start and end apart: 3 -> 3, of which waited for: 2 -> 2; matrix products, arithmetic and copies ran while one was open for 8% -> 1% of each run, Pallas kernels for 0% -> 5%
where the time goes in v1:
time: 108 us
  blocking collectives  55.5 us (51%)
  Pallas kernels  28.1 us (26%)
  starting transfers between devices  7.76 us (7%)
  local copies, waits for them, and re-layouts  7.34 us (7%)
  waiting for transfers between devices  4.78 us (4%)
  other arithmetic  3.45 us (3%)
    all_to_all x1, blocking collectives, shards(): lax.all_to_all(pair.reshape(chips, half // chips, width), 'dom', split_ax...  29.3 us
    all_to_all x1, blocking collectives, shards(): lax.all_to_all(jnp.broadcast_to(mine[None], parts.shape), 'dom', split_ax...  26.2 us
    pallas_call x1, Pallas kernels, shards(): pl.pallas_call(functools.partial(edge_kernel, channels), out_shape=(jax.S...  22.9 us
    all_to_all x1, starting transfers between devices, shards(): lax.all_to_all(send.reshape(device_count, peer_slots, padded), 'dom', spl...  7.36 us
    pallas_call x1, Pallas kernels, shards(): pl.pallas_call(own_kernel, out_shape=(jax.ShapeDtypeStruct((own, width),...  5.2 us
    ppermute x1, waiting for transfers between devices, shards(): other = lax.ppermute(spread, 'dom', swap)  2.47 us
    ppermute x1, waiting for transfers between devices, shards(): got = lax.ppermute(sent, 'dom', swap)  2.31 us
    dynamic_slice x1, local copies, waits for them, and re-layouts, shards(): sent = lax.dynamic_slice_in_dim(grads, (1 - core) * half, half, 0)  2.29 us
  transfers between devices with their start and end apart: 3, of which 2 were waited for; matrix products, arithmetic and copies ran while one was open for 1% of the time, Pallas kernels for 5%

profile of v1, /device:TPU:0, one launch (start us, length us, event | category | flops | bytes accessed | tf_op | source)
XLA Modules:
  0.0 107.9 jit_solution(15117548680562581859)
XLA Ops:
  0.6 0.0 copy-start.5
  0.6 0.0 copy-start.3
  0.7 0.0 copy-start.2
  0.7 0.1 pad.6.clone
  0.7 0.1 pad.7.clone
  0.8 1.2 %copy.19 = bf16[1024,227]{1,0:T(8,128)(2,1)S(1)} copy(bf16[1024,227]{0,1:T(8,128)(2,1)} %param.13) | data formatting | bytes 929792 | tf_op args[0]
  2.1 0.1 maximum_maximum_fusion.feat.feat_own
  2.2 0.0 copy-start
  2.2 0.2 convolution_convert_fusion
  2.5 0.6 reshape.26
  3.1 7.4 %all-to-all-start = ((bf16[16,4,256]{2,1,0:T(4,128)(2,1)}), bf16[16,4,256]{2,1,0:T(4,128)(2,1)S(1)}, u32[]{:S(2)}, u32[]{:S(2)}) async-start(bf16[16,4,256]{2,1,0:T(4,128)(2,1)} %reshape.26), calls=%async_computation | async-start | bytes 65536 | tf_op jit(solution)/shard_map/all_to_all | solution.py:197
  10.5 0.8 maximum_maximum_fusion.1.w_embed
  11.3 5.2 %own_rows.1 = (bf16[1024,512]{1,0:T(8,128)(2,1)}, bf16[1024,512]{1,0:T(8,128)(2,1)}, bf16[512,512]{1,0:T(8,128)(2,1)}, bf16[512,512]{1,0:T(8,128)(2,1)}) custom-call(bf16[1024,256]{1,0:T(8,128)(2,1)} %copy-done, bf16[256,512]{1,0:T(8,128)(2,1)} %maximum_maximum_fusion.1.w_embed, bf16[512,512]{1,0:T(8,128)(2,1)} %w_src.3, bf16[512,512]{1,0:T(8,128)(2,1)} %mesh.3, ...), custom_call_target="tpu_custom_call" | custom-call | flops 1342177280 | bytes 4194304 | tf_op jit(solution)/shard_map/own_rows/pallas_call | solution.py:205
  16.5 0.6 broadcast_in_dim.26.b_hidden
  17.1 0.0 all-to-all-done
  17.1 0.6 reshape.27.feat_in
  17.7 22.9 %edge_rows.1 = (bf16[512,512]{1,0:T(8,128)(2,1)}, bf16[1792,512]{1,0:T(8,128)(2,1)}) custom-call(s32[4]{0:T(128)} %count.1, s32[4,1024]{1,0:T(4,128)} %src.1, s32[4,1024]{1,0:T(4,128)} %dst.1, bf16[64,256]{1,0:T(8,128)(2,1)} %reshape.27.feat_in, bf16[1024,256]{1,0:T(8,128)(2,1)} %copy-done, bf16[256,512]{1,0:T(8,128)(2,1)} %maximum_maximum_fusion.1.w_embed, ...), custom_call_target="tpu_custom_call" | custom-call | flops 11811160064 | bytes 4194304 | tf_op jit(solution)/shard_map/edge_rows/pallas_call | solution.py:223
  40.6 2.3 %constant_dynamic-slice_fusion = bf16[896,512]{1,0:T(8,128)(2,1)} fusion(bf16[1792,512]{1,0:T(8,128)(2,1)} %get-tuple-element.17, s32[]{:T(128)S(6)} %select_n.28), kind=kLoop, calls=%fused_computation.11 | loop fusion | bytes 1835012 | tf_op jit(solution)/shard_map/dynamic_slice | solution.py:273
  42.9 0.4 collective-permute-start
  43.3 2.3 %collective-permute-done = bf16[896,512]{1,0:T(8,128)(2,1)S(1)} collective-permute-done((bf16[896,512]{1,0:T(8,128)(2,1)}, bf16[896,512]{1,0:T(8,128)(2,1)S(1)}, u32[]{:S(2)}, u32[]{:S(2)}) %collective-permute-start) | collective-permute-done | bytes 917536 | tf_op jit(solution)/shard_map/ppermute | solution.py:274
  45.6 0.2 add_convert_fusion
  45.9 29.3 %all_to_all.15 = bf16[8,112,512]{2,1,0:T(8,128)(2,1)S(1)} all-to-all(bf16[8,112,512]{2,1,0:T(8,128)(2,1)S(1)} %bitcast.6), channel_id=1, replica_groups={{0,2,4,6,8,10,12,14},{1,3,5,7,9,11,13,15},{16,18,20,22,24,26,28,30},{17..., dimensions={0} | all-to-all | bytes 1835008 | tf_op jit(solution)/shard_map/all_to_all | solution.py:276
  75.1 0.1 reduce_sum.12
  75.3 0.1 broadcast_in_dim.27
  75.4 26.2 %all_to_all.16 = bf16[8,112,512]{2,1,0:T(8,128)(2,1)S(1)} all-to-all(bf16[8,112,512]{2,1,0:T(8,128)(2,1)S(1)} %broadcast_in_dim.27), channel_id=1, replica_groups={{0,2,4,6,8,10,12,14},{1,3,5,7,9,11,13,15},{16,18,20,22,24,26,28,30},{17..., dimensions={0} | all-to-all | bytes 1835008 | tf_op jit(solution)/shard_map/all_to_all | solution.py:285
  101.6 0.0 collective-permute-start.1
  101.6 2.5 %collective-permute-done.1 = bf16[896,512]{1,0:T(8,128)(2,1)S(1)} collective-permute-done((bf16[896,512]{1,0:T(8,128)(2,1)S(1)}, bf16[896,512]{1,0:T(8,128)(2,1)S(1)}, u32[]{:S(2)}, u32[]{:S(2)}) %collective-permute-start.1) | collective-permute-done | bytes 917536 | tf_op jit(solution)/shard_map/ppermute | solution.py:293
  104.0 0.2 broadcast_select_fusion.1
  104.2 0.6 maximum_convert_fusion.2
  104.8 0.8 maximum_convert_fusion.1
  105.7 0.5 maximum_convert_fusion
  106.2 1.7 %fusion.1 = (f32[512,512]{1,0:T(8,128)}, f32[512,512]{1,0:T(8,128)}, f32[512,512]{1,0:T(8,128)}) fusion(f32[1792,512]{1,0:T(8,128)S(1)} %maximum_convert_fusion), kind=kLoop, calls=%fused_computation.12 | loop fusion | bytes 6291456 | tf_op jit(solution)/shard_map/slice | solution.py:303
  (10 shorter events, 0.0 us)
Async XLA Ops:
  0.6 1.6 %copy-start.5 = (s32[64]{0:T(128)S(1)}, s32[64]{0:T(128)}, u32[]{:S(2)}) copy-start(s32[64]{0:T(128)} %param.16) | copy-start | bytes 772
  0.6 9.8 %copy-start.3 = (bf16[512]{0:T(512)(128)(2,1)S(1)}, bf16[512]{0:T(512)(128)(2,1)}, u32[]{:S(2)}) copy-start(bf16[512]{0:T(512)(128)(2,1)} %param.21) | copy-start | bytes 3076
  0.7 9.8 %copy-start.2 = (bf16[227,512]{1,0:T(8,128)(2,1)S(1)}, bf16[227,512]{1,0:T(8,128)(2,1)}, u32[]{:S(2)}) copy-start(bf16[227,512]{1,0:T(8,128)(2,1)} %param.20) | copy-start | bytes 697348
  2.2 9.1 %copy-start = (bf16[1024,256]{1,0:T(8,128)(2,1)}, bf16[1024,256]{1,0:T(8,128)(2,1)S(1)}, u32[]{:S(2)}) copy-start(bf16[1024,256]{1,0:T(8,128)(2,1)S(1)} %maximum_maximum_fusion.feat.feat_own) | copy-start | bytes 1572868
  3.1 14.0 %all-to-all-start = ((bf16[16,4,256]{2,1,0:T(4,128)(2,1)}), bf16[16,4,256]{2,1,0:T(4,128)(2,1)S(1)}, u32[]{:S(2)}, u32[]{:S(2)}) async-start(bf16[16,4,256]{2,1,0:T(4,128)(2,1)} %reshape.26), calls=%async_computation | async-start | bytes 65536 | tf_op jit(solution)/shard_map/all_to_all | solution.py:197
  11.3 5.2 %copy-start.4 = (bf16[512]{0:T(512)(128)(2,1)S(1)}, bf16[512]{0:T(512)(128)(2,1)}, u32[]{:S(2)}) copy-start(bf16[512]{0:T(512)(128)(2,1)} %param.24) | copy-start | bytes 3076
  40.6 5.0 %copy-start.1 = (bf16[1792,512]{1,0:T(8,128)(2,1)S(1)}, bf16[1792,512]{1,0:T(8,128)(2,1)}, u32[]{:S(2)}) copy-start(bf16[1792,512]{1,0:T(8,128)(2,1)} %get-tuple-element.17) | copy-start | bytes 5505028
  42.9 2.7 %collective-permute-start = (bf16[896,512]{1,0:T(8,128)(2,1)}, bf16[896,512]{1,0:T(8,128)(2,1)S(1)}, u32[]{:S(2)}, u32[]{:S(2)}) collective-permute-start(bf16[896,512]{1,0:T(8,128)(2,1)} %constant_dynamic-slice_fusion), channel_id=1, source_target_pairs={{0,1},{1,0},{2,3},{3,2},{4,5},{5,4},{6,7},{7,6},{8,9},{9,8},{10,11... | collective-permute-start | bytes 2752520 | tf_op jit(solution)/shard_map/ppermute | solution.py:274
  101.6 2.5 %collective-permute-start.1 = (bf16[896,512]{1,0:T(8,128)(2,1)S(1)}, bf16[896,512]{1,0:T(8,128)(2,1)S(1)}, u32[]{:S(2)}, u32[]{:S(2)}) collective-permute-start(bf16[896,512]{1,0:T(8,128)(2,1)S(1)} %bitcast.7), channel_id=1, source_target_pairs={{0,1},{1,0},{2,3},{3,2},{4,5},{5,4},{6,7},{7,6},{8,9},{9,8},{10,11... | collective-permute-start | bytes 2752520 | tf_op jit(solution)/shard_map/ppermute | solution.py:293

commit v2 on v1

v2 whole, which is shorter than its diff:
```python
import functools

import jax
import jax.numpy as jnp
from jax import lax
from jax.experimental import pallas as pl
from jax.experimental.pallas import tpu as pltpu
from jax.sharding import PartitionSpec as P

BF16 = jnp.bfloat16
F32 = jnp.float32
VMEM_BYTES = 60 * 1024 * 1024


def mm(left, right, left_dim=1, right_dim=0):
    return lax.dot_general(
        left, right, (((left_dim,), (right_dim,)), ((), ())), preferred_element_type=F32
    )


def sigmoid(values):
    return 0.5 * jnp.tanh(0.5 * values) + 0.5


def round_up(value, step):
    return -(-value // step) * step


def pick_kernel(row_pack, grid_feat, feat, send):
    own, channels = grid_feat.shape
    padded = feat.shape[1]
    peers, peer_slots = send.shape[0], send.shape[1]
    last = padded - 128
    lane = lax.broadcasted_iota(jnp.int32, (own, 128), 1) + last
    feat[:, last:padded] = jnp.where(lane == channels, 1.0, 0.0).astype(BF16)
    feat[:, 0:channels] = grid_feat[...]
    row = lax.broadcasted_iota(jnp.int32, (own, peers * peer_slots), 0)
    pick = jnp.where(row == row_pack[...], 1.0, 0.0).astype(BF16)
    rows = mm(pick, feat[...], 0, 0)
    for j in range(peers):
        send[j] = rows[j * peer_slots : (j + 1) * peer_slots, :].astype(BF16)


def own_kernel(
    feat, w_embed, b_embed, w_src, mesh, w_dst, cot, w_out, latent, proj, near, back, w_pad, wide
):
    rows = feat.shape[0]
    channels = w_embed.shape[0]
    step = 256
    wide[...] = jnp.zeros_like(wide)
    wide[0:channels, :] = w_embed[...].astype(F32)
    wide[channels : channels + 1, :] = b_embed[...].astype(F32)
    w_pad[...] = wide[...].astype(BF16)

    def body(i, carry):
        part = pl.ds(pl.multiple_of(i * step, step), step)
        pre = mm(feat[part, :], w_pad[...])
        lat = (pre * sigmoid(pre)).astype(BF16)
        latent[part, :] = lat
        proj[part, :] = mm(lat, w_src[...]).astype(BF16)
        return carry

    lax.fori_loop(0, rows // step, body, 0)
    near[...] = mm(mesh[...], w_dst[...]).astype(BF16)
    full = mm(cot[...], w_out[...], 1, 1)
    high = full.astype(BF16)
    back[0] = high
    back[1] = (full - high.astype(F32)).astype(BF16)


def stage_bits(device_count):
    bits = device_count.bit_length() - 1
    first = list(range(1, bits - 1))
    second = first[1::-1] + first[2:]
    return first, second, bits - 1


def position_mask(me, order):
    mask = 0
    for i, bit in enumerate(order):
        mask = mask + (lax.rem(me // (1 << bit), 2) << (len(order) - 1 - i))
    return mask


def edge_kernel(
    channels,
    device_count,
    count,
    src,
    dst,
    feat_in,
    feat_own,
    w_embed,
    w_src,
    w_out,
    b_hidden,
    latent_own,
    proj_own,
    near,
    back,
    mesh,
    cot,
    mesh_out,
    kept,
    sent,
    table,
    pair,
    latent,
    feat,
    incoming,
    one_hot,
    one_hot_t,
    hid,
    pgrad,
    slot_sum,
    node_sum,
    hid_sum,
    bias_sum,
    grads,
):
    own = feat_own.shape[0]
    peers, peer_slots, padded = feat_in.shape
    more = peers * peer_slots
    slots = own + more
    blocks, edges = src.shape
    width = w_src.shape[0]
    block = mesh.shape[0] // blocks
    depth = table.shape[0]
    step = 256

    feat[0:own, :] = feat_own[...]
    for j in range(peers):
        incoming[j * peer_slots : (j + 1) * peer_slots, :] = feat_in[j].astype(F32)
    feat[own:slots, :] = incoming[...].astype(BF16)
    latent[0:own, :] = latent_own[...]
    pre_in = mm(feat[own:slots, :], w_embed[...])
    lat_in = (pre_in * sigmoid(pre_in)).astype(BF16)
    latent[own:slots, :] = lat_in
    table[block : block + own, :] = proj_own[...]
    table[block + own : block + slots, :] = mm(lat_in, w_src[...]).astype(BF16)
    tail = depth - slots - block
    tail_row = lax.broadcasted_iota(jnp.int32, (tail, width), 0)
    table[slots + block : depth, :] = jnp.where(
        tail_row == 0, jnp.broadcast_to(b_hidden[...], (tail, width)).astype(F32), 0.0
    ).astype(BF16)
    slot_sum[...] = jnp.zeros_like(slot_sum)
    bias_sum[...] = jnp.zeros_like(bias_sum)

    edge_lane = lax.broadcasted_iota(jnp.int32, (blocks, edges), 1)
    block_row = lax.broadcasted_iota(jnp.int32, (blocks, 1), 0)
    counts = jnp.zeros((blocks, 1), jnp.int32)
    for b in range(blocks):
        counts = jnp.where(block_row == b, count[b], counts)
    src_all = src[...]
    dst_all = jnp.where(edge_lane < counts, dst[...], -1)
    columns = jnp.transpose(jnp.concatenate([src_all, dst_all], axis=0))

    for b in range(blocks):
        rows = slice(b * block, (b + 1) * block)
        table[0:block, :] = near[rows, :]
        pair[0:block, :] = back[0, rows, :]
        pair[block : 2 * block, :] = back[1, rows, :]
        src_row = src_all[b : b + 1, :]
        dst_row = dst_all[b : b + 1, :]
        for e in range(0, edges, step):
            src_col = columns[e : e + step, b : b + 1]
            dst_col = columns[e : e + step, blocks + b : blocks + b + 1]
            lane = lax.broadcasted_iota(jnp.int32, (step, block), 1)
            near_hot = jnp.where(lane == dst_col, 1.0, 0.0).astype(BF16)
            one_hot[e : e + step, 0:block] = near_hot
            one_hot[e : e + step, block : 2 * block] = near_hot
            for k in range(0, depth - block, 128):
                lane = lax.broadcasted_iota(jnp.int32, (step, 128), 1) + k
                hot = lane == src_col
                if k <= slots < k + 128:
                    hot = hot | (lane == slots)
                hot = jnp.where(hot, 1.0, 0.0).astype(BF16)
                one_hot[e : e + step, 2 * block + k : 2 * block + k + 128] = hot
            pre = mm(one_hot[e : e + step, block : block + depth], table[...])
            grad = mm(one_hot[e : e + step, 0 : 2 * block], pair[...])
            sig = sigmoid(pre)
            act = pre * sig
            hid[e : e + step, :] = act.astype(BF16)
            pgrad[e : e + step, :] = (grad * (sig + act * (1.0 - sig))).astype(BF16)
        sub = lax.broadcasted_iota(jnp.int32, (block, edges), 0)
        one_hot_t[0:block, :] = jnp.where(sub == dst_row, 1.0, 0.0).astype(BF16)
        for r in range(0, depth - block, 128):
            sub = lax.broadcasted_iota(jnp.int32, (128, edges), 0) + r
            hot = sub == src_row
            if r <= slots < r + 128:
                hot = hot | (sub == slots)
            one_hot_t[block + r : block + r + 128, :] = jnp.where(hot, 1.0, 0.0).astype(BF16)
        slot_sum[...] += mm(one_hot_t[block : block + slots, :], pgrad[...])
        bias_sum[...] += mm(one_hot_t[block + slots : block + slots + 16, :], pgrad[...])
        node_sum[rows, :] = mm(one_hot_t[0:block, :], pgrad[...]).astype(BF16)
        hid_sum[rows, :] = mm(one_hot_t[0:block, :], hid[...]).astype(BF16)

    total = hid_sum[...]
    mesh_out[...] = (mesh[...].astype(F32) + mm(total, w_out[...])).astype(BF16)
    grads[0:width, :] = mm(total, cot[...], 0, 0)
    grads[width : 2 * width, :] = mm(mesh[...], node_sum[...], 0, 0)
    slot_grad = slot_sum[...].astype(BF16)
    grads[2 * width : 3 * width, :] = mm(latent[...], slot_grad, 0, 0)
    buffer_grad = mm(slot_grad, w_src[...], 1, 1)
    pre = mm(feat[...], w_embed[...])
    sig = sigmoid(pre)
    embed = (buffer_grad * (sig * (1.0 + pre * (1.0 - sig)))).astype(BF16)
    base = 3 * width
    grads[base : base + padded, :] = mm(feat[...], embed, 0, 0)
    grads[base + channels + 1 : base + channels + 2, :] = bias_sum[0:1, :]
    if grads.shape[0] > base + padded:
        rest = grads.shape[0] - base - padded
        grads[base + padded :, :] = jnp.zeros((rest, width), F32)

    me = lax.axis_index("dom")
    core = lax.rem(me, 2)
    first, second, _ = stage_bits(device_count)
    masks = position_mask(me, first), position_mask(me, second)
    mine = jnp.where(core == 0, masks[0], masks[1])
    theirs = jnp.where(core == 0, masks[1], masks[0])
    pieces = 1 << len(first)
    piece = kept.shape[0] // pieces
    for p in range(pieces):
        at = pl.ds(pl.multiple_of((core * pieces + (mine ^ p)) * piece, 16), piece)
        kept[p * piece : (p + 1) * piece, :] = grads[at, :]
        at = pl.ds(pl.multiple_of(((1 - core) * pieces + (theirs ^ p)) * piece, 16), piece)
        sent[p * piece : (p + 1) * piece, :] = grads[at, :].astype(BF16)


def unpack_kernel(channels, device_count, total, grad_embed, grad_src, grad_dst, grad_out, biases):
    width = total.shape[1]
    me = lax.axis_index("dom")
    core = lax.rem(me, 2)
    first, second, _ = stage_bits(device_count)
    masks = position_mask(me, first), position_mask(me, second)
    pieces = 1 << len(first)
    piece = total.shape[0] // (2 * pieces)
    base = 3 * width
    bounds = (
        (0, width, grad_out),
        (width, 2 * width, grad_dst),
        (2 * width, base, grad_src),
        (base, base + channels, grad_embed),
        (base + channels, base + channels + 2, biases),
    )
    for c in range(2 * pieces):
        half = c // pieces
        slot = (half ^ core) * pieces + ((c % pieces) ^ masks[half])
        begin, end = c * piece, (c + 1) * piece
        if begin >= base + channels + 2:
            continue
        values = total[pl.ds(pl.multiple_of(slot * piece, 16), piece), :].astype(F32)
        for low, high, target in bounds:
            lo, hi = max(low, begin), min(high, end)
            if lo < hi:
                target[lo - low : hi - low, :] = values[lo - begin : hi - begin, :]


def shards(
    grid_feat,
    mesh_latent,
    cotangent,
    row_pack,
    edge_src,
    edge_dst,
    edge_count,
    w_embed,
    b_embed,
    w_src,
    w_dst,
    b_hidden,
    w_out,
):
    device_count = lax.axis_size("dom")
    own, channels = grid_feat.shape
    width = w_src.shape[0]
    peer_slots = row_pack.shape[0] // device_count
    more = device_count * peer_slots
    slots = own + more
    blocks, edges = edge_src.shape
    nodes = mesh_latent.shape[0]
    block = nodes // blocks
    padded = round_up(channels + 2, 128)
    depth = block + round_up(slots + 16, 128)
    first, second, last_bit = stage_bits(device_count)
    pieces = 1 << len(first)
    grad_rows = round_up(3 * width + padded, 32 * pieces)
    half = grad_rows // 2

    vmem = pl.BlockSpec(memory_space=pltpu.VMEM)
    smem = pl.BlockSpec(memory_space=pltpu.SMEM)
    params = pltpu.CompilerParams(vmem_limit_bytes=VMEM_BYTES)
    shape = jax.ShapeDtypeStruct
    feat, send = pl.pallas_call(
        pick_kernel,
        out_shape=(shape((own, padded), BF16), shape((device_count, peer_slots, padded), BF16)),
        in_specs=[vmem] * 2,
        out_specs=(vmem,) * 2,
        compiler_params=params,
        name="pick_rows",
    )(row_pack[None, :], grid_feat)
    feat_in = lax.all_to_all(send, "dom", split_axis=0, concat_axis=0, tiled=True)

    own_macs = own * width * (padded + width) + 2 * nodes * width * width
    latent, proj, near, back, w_pad = pl.pallas_call(
        own_kernel,
        out_shape=(
            shape((own, width), BF16),
            shape((own, width), BF16),
            shape((nodes, width), BF16),
            shape((2, nodes, width), BF16),
            shape((padded, width), BF16),
        ),
        in_specs=[vmem] * 8,
        out_specs=(vmem,) * 5,
        scratch_shapes=[pltpu.VMEM((padded, width), F32)],
        compiler_params=params,
        cost_estimate=pl.CostEstimate(
            flops=2 * own_macs, bytes_accessed=8 * own * width, transcendentals=own * width
        ),
        name="own_rows",
    )(feat, w_embed, b_embed[None, :], w_src, mesh_latent, w_dst, cotangent, w_out)

    edge_macs = blocks * edges * width * (2 * depth + 3 * block)
    mesh_out, kept, sent = pl.pallas_call(
        functools.partial(edge_kernel, channels, device_count),
        out_shape=(
            shape((nodes, width), BF16),
            shape((half, width), F32),
            shape((half, width), BF16),
        ),
        in_specs=[smem] + [vmem] * 14,
        out_specs=(vmem,) * 3,
        scratch_shapes=[
            pltpu.VMEM((depth, width), BF16),
            pltpu.VMEM((2 * block, width), BF16),
            pltpu.VMEM((slots, width), BF16),
            pltpu.VMEM((slots, padded), BF16),
            pltpu.VMEM((more, padded), F32),
            pltpu.VMEM((edges, depth + block), BF16),
            pltpu.VMEM((depth, edges), BF16),
            pltpu.VMEM((edges, width), BF16),
            pltpu.VMEM((edges, width), BF16),
            pltpu.VMEM((slots, width), F32),
            pltpu.VMEM((nodes, width), BF16),
            pltpu.VMEM((nodes, width), BF16),
            pltpu.VMEM((16, width), F32),
            pltpu.VMEM((grad_rows, width), F32),
        ],
        compiler_params=params,
        cost_estimate=pl.CostEstimate(
            flops=2 * edge_macs, bytes_accessed=8 * own * width, transcendentals=blocks * edges * width
        ),
        name="edge_rows",
    )(
        edge_count,
        edge_src,
        edge_dst,
        feat_in,
        feat,
        w_pad,
        w_src,
        w_out,
        b_hidden[None, :],
        latent,
        proj,
        near,
        back,
        mesh_latent,
        cotangent,
    )

    def swap(values, bits):
        return lax.ppermute(
            values, "dom", [(d, d ^ (1 << bits[d % 2])) for d in range(device_count)]
        )

    held = kept + swap(sent, (0, 0)).astype(F32)
    for bits in zip(first, second):
        cut = held.shape[0] // 2
        got = swap(held[cut:].astype(BF16), bits)
        held = held[:cut] + got.astype(F32)
    held = held.astype(BF16)
    got = swap(held, (last_bit, last_bit))
    held = (held.astype(F32) + got.astype(F32)).astype(BF16)
    for bits in zip(reversed(first), reversed(second)):
        held = jnp.concatenate([held, swap(held, bits)], axis=0)
    held = jnp.concatenate([held, swap(held, (0, 0))], axis=0)

    grad_embed, grad_src, grad_dst, grad_out, biases = pl.pallas_call(
        functools.partial(unpack_kernel, channels, device_count),
        out_shape=(
            shape((channels, width), F32),
            shape((width, width), F32),
            shape((width, width), F32),
            shape((width, width), F32),
            shape((2, width), F32),
        ),
        in_specs=[vmem],
        out_specs=(vmem,) * 5,
        compiler_params=params,
        name="unpack_grads",
    )(held)
    return mesh_out, grad_embed, grad_src, grad_dst, grad_out, biases


def solution(mesh):
    return jax.shard_map(
        shards,
        mesh=mesh,
        in_specs=(
            P(("ens", "dom"), None),
            P(("ens", "dom"), None),
            P(("ens", "dom"), None),
            P("dom"),
            P("dom", None),
            P("dom", None),
            P("dom"),
            P(),
            P(),
            P(),
            P(),
            P(),
            P(),
        ),
        out_specs=(
            P(("ens", "dom"), None),
            P("ens", None),
            P("ens", None),
            P("ens", None),
            P("ens", None),
            P("ens", None),
        ),
        check_vma=False,
    )
```

time: 108 us -> 97.7 us (0.905)
  blocking collectives: 55.5 us -> 0 us
  waiting for transfers between devices: 4.78 us -> 36.9 us
  starting transfers between devices: 7.76 us -> 17 us
  Pallas kernels: 28.1 us -> 34.6 us
  local copies, waits for them, and re-layouts: 7.34 us -> 4.57 us
    all_to_all x2 -> x0, blocking collectives: 55.5 us -> none  [the longest x1 29.3 us: shards(): lax.all_to_all(pair.reshape(chips, half // chips, width), 'dom', split_ax...]
    ppermute x2 -> x7, waiting for transfers between devices: 4.78 us -> 36.9 us  [swap(): lax.ppermute(values, 'dom', [(d, d ^ 1 << bits[d % 2]) for d in range(dev...]
    ppermute x2 -> x7, starting transfers between devices: 0.4 us -> 9.64 us  [swap(): lax.ppermute(values, 'dom', [(d, d ^ 1 << bits[d % 2]) for d in range(dev...]
    pallas_call x2 -> x4, Pallas kernels: 28.1 us -> 34.6 us  [the longest x1 23.6 us: shards(): pl.pallas_call(functools.partial(edge_kernel, channels, device_count), ou...]
    dynamic_slice x1 -> x0, local copies, waits for them, and re-layouts: 2.29 us -> none  [shards(): sent = lax.dynamic_slice_in_dim(grads, (1 - core) * half, half, 0)]
    add x0 -> x2, other arithmetic: none -> 1.98 us  [the longest x1 1.82 us: shards(): held = kept + swap(sent, (0, 0)).astype(F32)]
    slice x1 -> x2, local copies, waits for them, and re-layouts: 1.74 us -> 0.09 us  [shards(): got = swap(held[cut:].astype(BF16), bits)]
    slice x2 -> x0, other arithmetic: 1.42 us -> none  [the longest x1 0.83 us: shards(): total[base:base + channels]]
  transfers between devices with their start and end apart: 3 -> 8, of which waited for: 2 -> 7; matrix products, arithmetic and copies ran while one was open for 1% -> 2% of each run, Pallas kernels for 5% -> 6%
where the time goes in v2:
time: 97.7 us; the launch traced here: 97.3 us
  waiting for transfers between devices  36.9 us (38%)
  Pallas kernels  34.6 us (35%)
  starting transfers between devices  17 us (17%)
  local copies, waits for them, and re-layouts  4.57 us (5%)
  other arithmetic  3.59 us (4%)
    ppermute x7, waiting for transfers between devices, swap(): lax.ppermute(values, 'dom', [(d, d ^ 1 << bits[d % 2]) for d in range(dev...  36.9 us
    pallas_call x1, Pallas kernels, shards(): pl.pallas_call(functools.partial(edge_kernel, channels, device_count), ou...  23.6 us
    ppermute x7, starting transfers between devices, swap(): lax.ppermute(values, 'dom', [(d, d ^ 1 << bits[d % 2]) for d in range(dev...  9.64 us
    all_to_all x1, starting transfers between devices, shards(): lax.all_to_all(send, 'dom', split_axis=0, concat_axis=0, tiled=True)  7.36 us
    pallas_call x1, Pallas kernels, shards(): pl.pallas_call(own_kernel, out_shape=(shape((own, width), BF16), shape((o...  5.59 us
    pallas_call x1, Pallas kernels, shards(): pl.pallas_call(functools.partial(unpack_kernel, channels, device_count),...  3.38 us
    unnamed x5, local copies, waits for them, and re-layouts  2.64 us
    pallas_call x1, Pallas kernels, shards(): pl.pallas_call(pick_kernel, out_shape=(shape((own, padded), BF16), shape(...  2 us
  transfers between devices with their start and end apart: 8, of which 7 were waited for; matrix products, arithmetic and copies ran while one was open for 2% of the time, Pallas kernels for 6%

profile of v2, /device:TPU:0, one launch (start us, length us, event | category | flops | bytes accessed | tf_op | source)
XLA Modules:
  0.0 97.3 jit_solution(17340482550483029473)
XLA Ops:
  0.6 2.0 %copy.19.grid_feat = bf16[1024,227]{1,0:T(8,128)(2,1)} copy(bf16[1024,227]{0,1:T(8,128)(2,1)} %param.13) | data formatting | bytes 929792 | tf_op args[0]
  2.7 2.0 %pick_rows.1 = (bf16[1024,256]{1,0:T(8,128)(2,1)}, bf16[16,4,256]{2,1,0:T(4,128)(2,1)}) custom-call(s32[1,64]{1,0:T(1,128)} %bitcast.1, bf16[1024,227]{1,0:T(8,128)(2,1)} %copy.19.grid_feat), custom_call_target="tpu_custom_call" | custom-call | tf_op jit(solution)/shard_map/pick_rows/pallas_call | solution.py:294
  4.7 7.4 %all-to-all-start = ((bf16[16,4,256]{2,1,0:T(4,128)(2,1)}), bf16[16,4,256]{2,1,0:T(4,128)(2,1)S(1)}, u32[]{:S(2)}, u32[]{:S(2)}) async-start(bf16[16,4,256]{2,1,0:T(4,128)(2,1)} %get-tuple-element.21), calls=%async_computation | async-start | bytes 65536 | tf_op jit(solution)/shard_map/all_to_all | solution.py:302
  12.0 1.3 %broadcast_in_dim.10.b_embed = bf16[1,512]{1,0:T(2,128)(2,1)} reshape(bf16[512]{0:T(512)(128)(2,1)} %param.21) | data formatting | bytes 2048 | tf_op jit(solution)/shard_map/broadcast_in_dim | solution.py:322
  13.3 5.6 %own_rows.1 = (bf16[1024,512]{1,0:T(8,128)(2,1)}, bf16[1024,512]{1,0:T(8,128)(2,1)}, bf16[512,512]{1,0:T(8,128)(2,1)}, bf16[2,512,512]{2,1,0:T(8,128)(2,1)}, bf16[256,512]{1,0:T(8,128)(2,1)}) custom-call(bf16[1024,256]{1,0:T(8,128)(2,1)} %get-tuple-element.22.feat.feat_own, bf16[227,512]{1,0:T(8,128)(2,1)} %w_embed.1, ...), custom_call_target="tpu_custom_call" | custom-call | flops 1342177280 | bytes 4194304 | tf_op jit(solution)/shard_map/own_rows/pallas_call | solution.py:305
  18.9 0.0 copy-done.1
  18.9 0.6 broadcast_in_dim.11.b_hidden
  19.5 0.0 all-to-all-done.feat_in
  19.5 0.6 copy-done
  20.1 23.6 %edge_rows.1 = (bf16[512,512]{1,0:T(8,128)(2,1)}, f32[896,512]{1,0:T(8,128)}, bf16[896,512]{1,0:T(8,128)(2,1)}) custom-call(s32[4]{0:T(128)} %count.1, s32[4,1024]{1,0:T(4,128)} %src.1, s32[4,1024]{1,0:T(4,128)} %dst.1, bf16[16,4,256]{2,1,0:T(4,128)(2,1)} %copy-done, bf16[1024,256]{1,0:T(8,128)(2,1)} %get-tuple-element.22.feat.feat_own, ...), custom_call_target="tpu_custom_call" | custom-call | flops 12348030976 | bytes 4194304 | tf_op jit(solution)/shard_map/edge_rows/pallas_call | solution.py:325
  43.7 0.4 collective-permute-start
  44.1 2.3 %collective-permute-done = bf16[896,512]{1,0:T(8,128)(2,1)S(1)} collective-permute-done((bf16[896,512]{1,0:T(8,128)(2,1)}, bf16[896,512]{1,0:T(8,128)(2,1)S(1)}, u32[]{:S(2)}, u32[]{:S(2)}) %collective-permute-start) | collective-permute-done | bytes 917536 | tf_op jit(solution)/shard_map/ppermute | solution.py:374
  46.4 1.8 %convert_add_fusion = f32[896,512]{1,0:T(8,128)S(1)} fusion(f32[896,512]{1,0:T(8,128)} %get-tuple-element.29, bf16[896,512]{1,0:T(8,128)(2,1)S(1)} %collective-permute-done), kind=kLoop, calls=%fused_computation.1 | loop fusion | flops 917504 | bytes 4587520 | tf_op jit(solution)/shard_map/add | solution.py:378
  48.2 0.1 slice.28
  48.3 1.9 %collective-permute-start.1 = (bf16[448,512]{1,0:T(8,128)(2,1)S(1)}, bf16[448,512]{1,0:T(8,128)(2,1)S(1)}, u32[]{:S(2)}, u32[]{:S(2)}) collective-permute-start(bf16[448,512]{1,0:T(8,128)(2,1)S(1)} %slice.28), channel_id=1, source_target_pairs={{0,2},{1,5},{2,0},{3,7},{4,6},{5,1},{6,4},{7,3},{8,10},{9,13},{10,... | collective-permute-start | bytes 1376264 | tf_op jit(solution)/shard_map/ppermute | solution.py:374
  50.2 6.6 %collective-permute-done.1 = bf16[448,512]{1,0:T(8,128)(2,1)S(1)} collective-permute-done((bf16[448,512]{1,0:T(8,128)(2,1)S(1)}, bf16[448,512]{1,0:T(8,128)(2,1)S(1)}, u32[]{:S(2)}, u32[]{:S(2)}) %collective-permute-start.1) | collective-permute-done | bytes 458784 | tf_op jit(solution)/shard_map/ppermute | solution.py:374
  56.8 0.2 slice_add_fusion
  57.0 2.0 %collective-permute-start.2 = (bf16[224,512]{1,0:T(8,128)(2,1)S(1)}, bf16[224,512]{1,0:T(8,128)(2,1)S(1)}, u32[]{:S(2)}, u32[]{:S(2)}) collective-permute-start(bf16[224,512]{1,0:T(8,128)(2,1)S(1)} %slice.29), channel_id=1, source_target_pairs={{0,4},{1,3},{2,6},{3,1},{4,0},{5,7},{6,2},{7,5},{8,12},{9,11},{10,... | collective-permute-start | bytes 688136 | tf_op jit(solution)/shard_map/ppermute | solution.py:374
  59.0 4.1 %collective-permute-done.2 = bf16[224,512]{1,0:T(8,128)(2,1)S(1)} collective-permute-done((bf16[224,512]{1,0:T(8,128)(2,1)S(1)}, bf16[224,512]{1,0:T(8,128)(2,1)S(1)}, u32[]{:S(2)}, u32[]{:S(2)}) %collective-permute-start.2) | collective-permute-done | bytes 229408 | tf_op jit(solution)/shard_map/ppermute | solution.py:374
  63.1 0.1 fusion
  63.2 2.9 %collective-permute-start.3 = (bf16[224,512]{1,0:T(8,128)(2,1)S(1)}, bf16[224,512]{1,0:T(8,128)(2,1)S(1)}, u32[]{:S(2)}, u32[]{:S(2)}) collective-permute-start(bf16[224,512]{1,0:T(8,128)(2,1)S(1)} %fusion), channel_id=1, source_target_pairs={{0,8},{1,9},{2,10},{3,11},{4,12},{5,13},{6,14},{7,15},{8,0},{9,1},... | collective-permute-start | bytes 688136 | tf_op jit(solution)/shard_map/ppermute | solution.py:374
  66.0 9.2 %collective-permute-done.3 = bf16[224,512]{1,0:T(8,128)(2,1)S(1)} collective-permute-done((bf16[224,512]{1,0:T(8,128)(2,1)S(1)}, bf16[224,512]{1,0:T(8,128)(2,1)S(1)}, u32[]{:S(2)}, u32[]{:S(2)}) %collective-permute-start.3) | collective-permute-done | bytes 229408 | tf_op jit(solution)/shard_map/ppermute | solution.py:374
  75.2 0.1 add_convert_fusion
  75.3 0.7 collective-permute-start.4
  76.0 5.4 %collective-permute-done.4 = bf16[224,512]{1,0:T(8,128)(2,1)S(1)} collective-permute-done((bf16[224,512]{1,0:T(8,128)(2,1)S(1)}, bf16[224,512]{1,0:T(8,128)(2,1)S(1)}, u32[]{:S(2)}, u32[]{:S(2)}) %collective-permute-start.4) | collective-permute-done | bytes 229408 | tf_op jit(solution)/shard_map/ppermute | solution.py:374
  81.4 1.7 %collective-permute-start.5 = (bf16[448,512]{1,0:T(8,128)(2,1)S(1)}, bf16[448,512]{1,0:T(8,128)(2,1)S(1)}, u32[]{:S(2)}, u32[]{:S(2)}) collective-permute-start(bf16[448,512]{1,0:T(8,128)(2,1)S(1)} %pad_maximum_fusion.2), channel_id=1, source_target_pairs={{0,2},{1,5},{2,0},{3,7},{4,6},{5,1},{6,4},{7,3},{8,10},{9,13},{10,... | collective-permute-start | bytes 1376264 | tf_op jit(solution)/shard_map/ppermute | solution.py:374
  83.1 6.8 %collective-permute-done.5 = bf16[448,512]{1,0:T(8,128)(2,1)S(1)} collective-permute-done((bf16[448,512]{1,0:T(8,128)(2,1)S(1)}, bf16[448,512]{1,0:T(8,128)(2,1)S(1)}, u32[]{:S(2)}, u32[]{:S(2)}) %collective-permute-start.5) | collective-permute-done | bytes 458784 | tf_op jit(solution)/shard_map/ppermute | solution.py:374
  89.9 0.1 pad_maximum_fusion.1
  90.0 0.1 collective-permute-start.6
  90.1 2.5 %collective-permute-done.6 = bf16[896,512]{1,0:T(8,128)(2,1)S(1)} collective-permute-done((bf16[896,512]{1,0:T(8,128)(2,1)S(1)}, bf16[896,512]{1,0:T(8,128)(2,1)S(1)}, u32[]{:S(2)}, u32[]{:S(2)}) %collective-permute-start.6) | collective-permute-done | bytes 917536 | tf_op jit(solution)/shard_map/ppermute | solution.py:374
  92.5 1.4 %pad_maximum_fusion.total = bf16[1792,512]{1,0:T(8,128)(2,1)} fusion(bf16[896,512]{1,0:T(8,128)(2,1)S(1)} %collective-permute-done.6, bf16[448,512]{1,0:T(8,128)(2,1)S(1)} %collective-permute-done.5, bf16[224,512]{1,0:T(8,128)(2,1)S(1)} %collective-permute-done.4, bf16[224,512]{1,0:T(8,128)(2,1)S(1)} %add_convert_fusion), kind=kLoop, calls=%fused_computation | loop fusion | flops 7340032 | bytes 3670016 | tf_op jit(solution)/shard_map/concatenate | solution.py:388
  93.9 3.4 %unpack_grads.1 = (f32[227,512]{1,0:T(8,128)}, f32[512,512]{1,0:T(8,128)}, f32[512,512]{1,0:T(8,128)}, f32[512,512]{1,0:T(8,128)}, f32[2,512]{1,0:T(2,128)}) custom-call(bf16[1792,512]{1,0:T(8,128)(2,1)} %pad_maximum_fusion.total), custom_call_target="tpu_custom_call" | custom-call | tf_op jit(solution)/shard_map/unpack_grads/pallas_call | solution.py:390
  (4 shorter events, 0.1 us)
Async XLA Ops:
  4.7 14.8 %all-to-all-start = ((bf16[16,4,256]{2,1,0:T(4,128)(2,1)}), bf16[16,4,256]{2,1,0:T(4,128)(2,1)S(1)}, u32[]{:S(2)}, u32[]{:S(2)}) async-start(bf16[16,4,256]{2,1,0:T(4,128)(2,1)} %get-tuple-element.21), calls=%async_computation | async-start | bytes 65536 | tf_op jit(solution)/shard_map/all_to_all | solution.py:302
  13.3 5.6 %copy-start.1 = (bf16[512]{0:T(512)(128)(2,1)S(1)}, bf16[512]{0:T(512)(128)(2,1)}, u32[]{:S(2)}) copy-start(bf16[512]{0:T(512)(128)(2,1)} %param.24) | copy-start | bytes 3076
  19.5 0.6 copy-start
  43.7 2.7 %collective-permute-start = (bf16[896,512]{1,0:T(8,128)(2,1)}, bf16[896,512]{1,0:T(8,128)(2,1)S(1)}, u32[]{:S(2)}, u32[]{:S(2)}) collective-permute-start(bf16[896,512]{1,0:T(8,128)(2,1)} %get-tuple-element.30), channel_id=1, source_target_pairs={{0,1},{1,0},{2,3},{3,2},{4,5},{5,4},{6,7},{7,6},{8,9},{9,8},{10,11... | collective-permute-start | bytes 2752520 | tf_op jit(solution)/shard_map/ppermute | solution.py:374
  48.3 8.5 %collective-permute-start.1 = (bf16[448,512]{1,0:T(8,128)(2,1)S(1)}, bf16[448,512]{1,0:T(8,128)(2,1)S(1)}, u32[]{:S(2)}, u32[]{:S(2)}) collective-permute-start(bf16[448,512]{1,0:T(8,128)(2,1)S(1)} %slice.28), channel_id=1, source_target_pairs={{0,2},{1,5},{2,0},{3,7},{4,6},{5,1},{6,4},{7,3},{8,10},{9,13},{10,... | collective-permute-start | bytes 1376264 | tf_op jit(solution)/shard_map/ppermute | solution.py:374
  57.0 6.1 %collective-permute-start.2 = (bf16[224,512]{1,0:T(8,128)(2,1)S(1)}, bf16[224,512]{1,0:T(8,128)(2,1)S(1)}, u32[]{:S(2)}, u32[]{:S(2)}) collective-permute-start(bf16[224,512]{1,0:T(8,128)(2,1)S(1)} %slice.29), channel_id=1, source_target_pairs={{0,4},{1,3},{2,6},{3,1},{4,0},{5,7},{6,2},{7,5},{8,12},{9,11},{10,... | collective-permute-start | bytes 688136 | tf_op jit(solution)/shard_map/ppermute | solution.py:374
  63.2 12.1 %collective-permute-start.3 = (bf16[224,512]{1,0:T(8,128)(2,1)S(1)}, bf16[224,512]{1,0:T(8,128)(2,1)S(1)}, u32[]{:S(2)}, u32[]{:S(2)}) collective-permute-start(bf16[224,512]{1,0:T(8,128)(2,1)S(1)} %fusion), channel_id=1, source_target_pairs={{0,8},{1,9},{2,10},{3,11},{4,12},{5,13},{6,14},{7,15},{8,0},{9,1},... | collective-permute-start | bytes 688136 | tf_op jit(solution)/shard_map/ppermute | solution.py:374
  75.3 6.1 %collective-permute-start.4 = (bf16[224,512]{1,0:T(8,128)(2,1)S(1)}, bf16[224,512]{1,0:T(8,128)(2,1)S(1)}, u32[]{:S(2)}, u32[]{:S(2)}) collective-permute-start(bf16[224,512]{1,0:T(8,128)(2,1)S(1)} %add_convert_fusion), channel_id=1, source_target_pairs={{0,4},{1,3},{2,6},{3,1},{4,0},{5,7},{6,2},{7,5},{8,12},{9,11},{10,... | collective-permute-start | bytes 688136 | tf_op jit(solution)/shard_map/ppermute | solution.py:374
  81.4 8.5 %collective-permute-start.5 = (bf16[448,512]{1,0:T(8,128)(2,1)S(1)}, bf16[448,512]{1,0:T(8,128)(2,1)S(1)}, u32[]{:S(2)}, u32[]{:S(2)}) collective-permute-start(bf16[448,512]{1,0:T(8,128)(2,1)S(1)} %pad_maximum_fusion.2), channel_id=1, source_target_pairs={{0,2},{1,5},{2,0},{3,7},{4,6},{5,1},{6,4},{7,3},{8,10},{9,13},{10,... | collective-permute-start | bytes 1376264 | tf_op jit(solution)/shard_map/ppermute | solution.py:374
  90.0 2.5 %collective-permute-start.6 = (bf16[896,512]{1,0:T(8,128)(2,1)S(1)}, bf16[896,512]{1,0:T(8,128)(2,1)S(1)}, u32[]{:S(2)}, u32[]{:S(2)}) collective-permute-start(bf16[896,512]{1,0:T(8,128)(2,1)S(1)} %pad_maximum_fusion.1), channel_id=1, source_target_pairs={{0,1},{1,0},{2,3},{3,2},{4,5},{5,4},{6,7},{7,6},{8,9},{9,8},{10,11... | collective-permute-start | bytes 2752520 | tf_op jit(solution)/shard_map/ppermute | solution.py:374

commit v3 on v2

v3 whole, which is shorter than its diff:
```python
import functools

import jax
import jax.numpy as jnp
from jax import lax
from jax.experimental import pallas as pl
from jax.experimental.pallas import tpu as pltpu
from jax.sharding import PartitionSpec as P

BF16 = jnp.bfloat16
F32 = jnp.float32


def mm(left, right, left_dim=1, right_dim=0):
    return lax.dot_general(
        left, right, (((left_dim,), (right_dim,)), ((), ())), preferred_element_type=F32
    )


def sigmoid(values):
    return 0.5 * jnp.tanh(0.5 * values) + 0.5


def round_up(value, step):
    return -(-value // step) * step


def pick_kernel(row_pack, feat_t, send):
    channels, own = feat_t.shape
    peers, peer_slots, padded = send.shape
    row = lax.broadcasted_iota(jnp.int32, (own, peers * peer_slots), 0)
    pick = jnp.where(row == row_pack[...], 1.0, 0.0).astype(BF16)
    rows = mm(pick, feat_t[...], 0, 1)
    last = padded - 128
    lane = lax.broadcasted_iota(jnp.int32, (peers * peer_slots, 128), 1) + last
    ones = jnp.where(lane == channels, 1.0, 0.0).astype(BF16)
    for j in range(peers):
        part = slice(j * peer_slots, (j + 1) * peer_slots)
        send[j, :, last:padded] = ones[part, :]
        send[j, :, 0:channels] = rows[part, :].astype(BF16)


def stage_bits(device_count):
    bits = device_count.bit_length() - 1
    first = list(range(1, bits - 1))
    second = first[1::-1] + first[2:]
    return first, second, bits - 1


def position_mask(me, order):
    mask = 0
    for i, bit in enumerate(order):
        mask = mask + (lax.rem(me // (1 << bit), 2) << (len(order) - 1 - i))
    return mask


def place(device_count):
    me = lax.axis_index("dom")
    first, second, _ = stage_bits(device_count)
    masks = position_mask(me, first), position_mask(me, second)
    return lax.rem(me, 2), masks, 1 << len(first)


def split_pieces(device_count, grads, kept, sent):
    core, masks, pieces = place(device_count)
    mine = jnp.where(core == 0, masks[0], masks[1])
    theirs = jnp.where(core == 0, masks[1], masks[0])
    piece = kept.shape[0] // pieces
    for p in range(pieces):
        at = pl.ds(pl.multiple_of((core * pieces + (mine ^ p)) * piece, 16), piece)
        kept[p * piece : (p + 1) * piece, :] = grads[at, :]
        at = pl.ds(pl.multiple_of(((1 - core) * pieces + (theirs ^ p)) * piece, 16), piece)
        sent[p * piece : (p + 1) * piece, :] = grads[at, :].astype(BF16)


def forward_kernel(
    device_count,
    count,
    src,
    dst,
    feat_in,
    feat_t,
    w_embed,
    biases,
    w_src,
    w_dst,
    w_out,
    mesh,
    cot,
    mesh_out,
    pgrad,
    latent,
    feat,
    w_pad,
    bias_sum,
    kept,
    sent,
    table,
    pair,
    wide,
    wide_t,
    incoming,
    one_hot,
    one_hot_t,
    hid,
    near,
    back,
    node_sum,
    hid_sum,
    grads,
):
    channels, own = feat_t.shape
    peers, peer_slots, padded = feat_in.shape
    more = peers * peer_slots
    slots = own + more
    blocks, edges = src.shape
    width = w_src.shape[0]
    nodes = mesh.shape[0]
    block = nodes // blocks
    depth = table.shape[0]
    step = 256

    last = padded - 32
    wide[last:padded, :] = jnp.zeros((32, width), F32)
    wide[0:channels, :] = w_embed[...].astype(F32)
    wide[channels : channels + 1, :] = biases[0:1, :].astype(F32)
    w_pad[...] = wide[...].astype(BF16)
    wide_t[last:padded, :] = jnp.zeros((32, own), F32)
    wide_t[0:channels, :] = feat_t[...].astype(F32)
    wide_t[channels : channels + 1, :] = jnp.ones((1, own), F32)
    feat[0:own, :] = jnp.transpose(wide_t[...]).astype(BF16)
    for j in range(peers):
        incoming[j * peer_slots : (j + 1) * peer_slots, :] = feat_in[j].astype(F32)
    feat[own:slots, :] = incoming[...].astype(BF16)
    for r in range(0, slots, step):
        end = min(r + step, slots)
        pre = mm(feat[r:end, :], w_pad[...])
        lat = (pre * sigmoid(pre)).astype(BF16)
        latent[r:end, :] = lat
        table[block + r : block + end, :] = mm(lat, w_src[...]).astype(BF16)
    near[...] = mm(mesh[...], w_dst[...]).astype(BF16)
    full = mm(cot[...], w_out[...], 1, 1)
    high = full.astype(BF16)
    back[0] = high
    back[1] = (full - high.astype(F32)).astype(BF16)
    tail = depth - slots - block
    tail_row = lax.broadcasted_iota(jnp.int32, (tail, width), 0)
    table[slots + block : depth, :] = jnp.where(
        tail_row == 0, jnp.broadcast_to(biases[1:2, :].astype(F32), (tail, width)), 0.0
    ).astype(BF16)

    edge_lane = lax.broadcasted_iota(jnp.int32, (blocks, edges), 1)
    block_row = lax.broadcasted_iota(jnp.int32, (blocks, 1), 0)
    counts = jnp.zeros((blocks, 1), jnp.int32)
    for b in range(blocks):
        counts = jnp.where(block_row == b, count[b], counts)
    src_all = src[...]
    dst_all = jnp.where(edge_lane < counts, dst[...], -1)
    columns = jnp.transpose(jnp.concatenate([src_all, dst_all], axis=0))
    bias_total = jnp.zeros((1, width), F32)

    for b in range(blocks):
        rows = slice(b * block, (b + 1) * block)
        table[0:block, :] = near[rows, :]
        pair[0:block, :] = back[0, rows, :]
        pair[block : 2 * block, :] = back[1, rows, :]
        dst_row = dst_all[b : b + 1, :]
        for e in range(0, edges, step):
            src_col = columns[e : e + step, b : b + 1]
            dst_col = columns[e : e + step, blocks + b : blocks + b + 1]
            lane = lax.broadcasted_iota(jnp.int32, (step, block), 1)
            near_hot = jnp.where(lane == dst_col, 1.0, 0.0).astype(BF16)
            one_hot[e : e + step, 0:block] = near_hot
            one_hot[e : e + step, block : 2 * block] = near_hot
            for k in range(0, depth - block, 128):
                lane = lax.broadcasted_iota(jnp.int32, (step, 128), 1) + k
                hot = lane == src_col
                if k <= slots < k + 128:
                    hot = hot | (lane == slots)
                hot = jnp.where(hot, 1.0, 0.0).astype(BF16)
                one_hot[e : e + step, 2 * block + k : 2 * block + k + 128] = hot
            pre = mm(one_hot[e : e + step, block : block + depth], table[...])
            grad = mm(one_hot[e : e + step, 0 : 2 * block], pair[...])
            sig = sigmoid(pre)
            act = pre * sig
            hid[e : e + step, :] = act.astype(BF16)
            at = slice(b * edges + e, b * edges + e + step)
            pgrad[at, :] = (grad * (sig + act * (1.0 - sig))).astype(BF16)
        sub = lax.broadcasted_iota(jnp.int32, (block, edges), 0)
        one_hot_t[...] = jnp.where(sub == dst_row, 1.0, 0.0).astype(BF16)
        node = mm(one_hot_t[...], pgrad[b * edges : (b + 1) * edges, :])
        bias_total = bias_total + jnp.sum(node, axis=0, keepdims=True)
        node_sum[rows, :] = node.astype(BF16)
        hid_sum[rows, :] = mm(one_hot_t[...], hid[...]).astype(BF16)

    bias_sum[...] = jnp.broadcast_to(bias_total, bias_sum.shape)
    total = hid_sum[...]
    mesh_out[...] = (mesh[...].astype(F32) + mm(total, w_out[...])).astype(BF16)
    grads[0:width, :] = mm(total, cot[...], 0, 0)
    grads[width : 2 * width, :] = mm(mesh[...], node_sum[...], 0, 0)
    split_pieces(device_count, grads, kept, sent)


def scatter_rows(src, pgrad, one_hot_t, first_block, block_count):
    edges = src.shape[1]
    slots = one_hot_t.shape[0]
    parts = []
    for b in range(first_block, first_block + block_count):
        at = slice((b - first_block) * edges, (b - first_block + 1) * edges)
        for r in range(0, slots, 128):
            size = min(128, slots - r)
            sub = lax.broadcasted_iota(jnp.int32, (size, edges), 0) + r
            hot = jnp.where(sub == src[b : b + 1, :], 1.0, 0.0).astype(BF16)
            one_hot_t[r : r + size, at] = hot
    rows = slice(first_block * edges, (first_block + block_count) * edges)
    return mm(one_hot_t[...], pgrad[rows, :])


def scatter_kernel(src, pgrad, slot_sum, one_hot_t):
    slot_sum[...] = scatter_rows(src, pgrad, one_hot_t, 0, src.shape[0] // 2)


def backward_kernel(
    channels,
    device_count,
    src,
    pgrad,
    slot_half,
    latent,
    feat,
    w_pad,
    w_src,
    bias_sum,
    kept,
    sent,
    one_hot_t,
    grads,
):
    width = w_src.shape[0]
    padded = feat.shape[1]
    half = src.shape[0] // 2
    rest = src.shape[0] - half
    slot_sum = slot_half[...] + scatter_rows(src, pgrad, one_hot_t, half, rest)
    slot_grad = slot_sum.astype(BF16)
    grads[0:width, :] = mm(latent[...], slot_grad, 0, 0)
    buffer_grad = mm(slot_grad, w_src[...], 1, 1)
    pre = mm(feat[...], w_pad[...])
    sig = sigmoid(pre)
    embed = (buffer_grad * (sig * (1.0 + pre * (1.0 - sig)))).astype(BF16)
    grads[width : width + padded, :] = mm(feat[...], embed, 0, 0)
    grads[width + channels + 1 : width + channels + 2, :] = bias_sum[0:1, :]
    if grads.shape[0] > width + padded:
        spare = grads.shape[0] - width - padded
        grads[width + padded :, :] = jnp.zeros((spare, width), F32)
    split_pieces(device_count, grads, kept, sent)


def unpack_kernel(device_count, bounds, held, got, *targets):
    core, masks, pieces = place(device_count)
    piece = held.shape[0] // pieces
    used = bounds[-1][1]
    for c in range(2 * pieces):
        half = c // pieces
        begin, end = c * piece, (c + 1) * piece
        if begin >= used:
            continue
        slot = (c % pieces) ^ masks[half]
        at = pl.ds(pl.multiple_of(slot * piece, 16), piece)
        values = jnp.where(core == half, held[at, :].astype(F32), got[at, :].astype(F32))
        for (low, high), target in zip(bounds, targets):
            lo, hi = max(low, begin), min(high, end)
            if lo < hi:
                target[lo - low : hi - low, :] = values[lo - begin : hi - begin, :]


def shards(
    grid_feat,
    mesh_latent,
    cotangent,
    row_pack,
    edge_src,
    edge_dst,
    edge_count,
    w_embed,
    b_embed,
    w_src,
    w_dst,
    b_hidden,
    w_out,
):
    device_count = lax.axis_size("dom")
    own, channels = grid_feat.shape
    width = w_src.shape[0]
    peer_slots = row_pack.shape[0] // device_count
    more = device_count * peer_slots
    slots = own + more
    blocks, edges = edge_src.shape
    nodes = mesh_latent.shape[0]
    block = nodes // blocks
    padded = round_up(channels + 2, 128)
    depth = block + round_up(slots + 16, 128)
    first, second, last_bit = stage_bits(device_count)
    pieces = 1 << len(first)
    mesh_rows = round_up(2 * width, 32 * pieces)
    grid_rows = round_up(width + padded, 32 * pieces)
    half_blocks = blocks // 2

    vmem = pl.BlockSpec(memory_space=pltpu.VMEM)
    smem = pl.BlockSpec(memory_space=pltpu.SMEM)
    shape = jax.ShapeDtypeStruct

    def limit(mib):
        return pltpu.CompilerParams(vmem_limit_bytes=mib * 1024 * 1024)

    feat_t = grid_feat.T
    send = pl.pallas_call(
        pick_kernel,
        out_shape=shape((device_count, peer_slots, padded), BF16),
        in_specs=[vmem] * 2,
        out_specs=vmem,
        compiler_params=limit(16),
        name="pick_rows",
    )(row_pack[None, :], feat_t)
    feat_in = lax.all_to_all(send, "dom", split_axis=0, concat_axis=0, tiled=True)
    bias_rows = jnp.stack([b_embed, b_hidden])

    forward_macs = (
        slots * width * (padded + width)
        + blocks * edges * width * (depth + 4 * block)
        + 5 * nodes * width * width
    )
    mesh_out, pgrad, latent, feat, w_pad, bias_sum, kept_mesh, sent_mesh = pl.pallas_call(
        functools.partial(forward_kernel, device_count),
        out_shape=(
            shape((nodes, width), BF16),
            shape((blocks * edges, width), BF16),
            shape((slots, width), BF16),
            shape((slots, padded), BF16),
            shape((padded, width), BF16),
            shape((8, width), F32),
            shape((mesh_rows // 2, width), F32),
            shape((mesh_rows // 2, width), BF16),
        ),
        in_specs=[smem] + [vmem] * 11,
        out_specs=(vmem,) * 8,
        scratch_shapes=[
            pltpu.VMEM((depth, width), BF16),
            pltpu.VMEM((2 * block, width), BF16),
            pltpu.VMEM((padded, width), F32),
            pltpu.VMEM((padded, own), F32),
            pltpu.VMEM((more, padded), F32),
            pltpu.VMEM((edges, depth + block), BF16),
            pltpu.VMEM((block, edges), BF16),
            pltpu.VMEM((edges, width), BF16),
            pltpu.VMEM((nodes, width), BF16),
            pltpu.VMEM((2, nodes, width), BF16),
            pltpu.VMEM((nodes, width), BF16),
            pltpu.VMEM((nodes, width), BF16),
            pltpu.VMEM((mesh_rows, width), F32),
        ],
        compiler_params=limit(40),
        cost_estimate=pl.CostEstimate(
            flops=2 * forward_macs,
            bytes_accessed=16 * own * width,
            transcendentals=blocks * edges * width,
        ),
        name="forward_rows",
    )(
        edge_count,
        edge_src,
        edge_dst,
        feat_in,
        feat_t,
        w_embed,
        bias_rows,
        w_src,
        w_dst,
        w_out,
        mesh_latent,
        cotangent,
    )

    def swap(values, bits):
        return lax.ppermute(
            values, "dom", [(d, d ^ (1 << bits[d % 2])) for d in range(device_count)]
        )

    def cut(held):
        middle = held.shape[0] // 2
        return held[:middle], held[middle:].astype(BF16)

    def pair_sum(kept, sent):
        return cut(kept + swap(sent, (0, 0)).astype(F32))

    def reduce_pieces(held, sent):
        stages = list(zip(first, second))
        for bits in stages[:-1]:
            held, sent = cut(held + swap(sent, bits).astype(F32))
        held = (held + swap(sent, stages[-1]).astype(F32)).astype(BF16)
        got = swap(held, (last_bit, last_bit))
        held = (held.astype(F32) + got.astype(F32)).astype(BF16)
        for bits in reversed(stages):
            held = jnp.concatenate([held, swap(held, bits)], axis=0)
        return held, swap(held, (0, 0))

    held_mesh, next_mesh = pair_sum(kept_mesh, sent_mesh)
    slot_half = pl.pallas_call(
        scatter_kernel,
        out_shape=shape((slots, width), F32),
        in_specs=[vmem] * 2,
        out_specs=vmem,
        scratch_shapes=[pltpu.VMEM((slots, half_blocks * edges), BF16)],
        compiler_params=limit(24),
        cost_estimate=pl.CostEstimate(
            flops=2 * half_blocks * edges * slots * width,
            bytes_accessed=half_blocks * edges * width * 2,
            transcendentals=0,
        ),
        name="scatter_rows",
    )(edge_src, pgrad)

    slot_half, held_mesh, next_mesh = lax.optimization_barrier((slot_half, held_mesh, next_mesh))
    kept_grid, sent_grid = pl.pallas_call(
        functools.partial(backward_kernel, channels, device_count),
        out_shape=(
            shape((grid_rows // 2, width), F32),
            shape((grid_rows // 2, width), BF16),
        ),
        in_specs=[vmem] * 8,
        out_specs=(vmem,) * 2,
        scratch_shapes=[
            pltpu.VMEM((slots, (blocks - half_blocks) * edges), BF16),
            pltpu.VMEM((grid_rows, width), F32),
        ],
        compiler_params=limit(40),
        cost_estimate=pl.CostEstimate(
            flops=2 * slots * width * (half_blocks * edges + 2 * width + 2 * padded),
            bytes_accessed=half_blocks * edges * width * 2,
            transcendentals=slots * width,
        ),
        name="backward_rows",
    )(edge_src, pgrad, slot_half, latent, feat, w_pad, w_src, bias_sum)

    def unpack(pair, bounds):
        return pl.pallas_call(
            functools.partial(unpack_kernel, device_count, bounds),
            out_shape=tuple(shape((high - low, width), F32) for low, high in bounds),
            in_specs=[vmem] * 2,
            out_specs=(vmem,) * len(bounds),
            compiler_params=limit(16),
            name="unpack_rows",
        )(*pair)

    mesh_pair = reduce_pieces(held_mesh, next_mesh)
    grid_pair = reduce_pieces(*pair_sum(kept_grid, sent_grid))
    grad_out, grad_dst = unpack(mesh_pair, ((0, width), (width, 2 * width)))
    end = width + channels
    grad_src, grad_embed, biases = unpack(grid_pair, ((0, width), (width, end), (end, end + 2)))
    return mesh_out, grad_embed, grad_src, grad_dst, grad_out, biases


def solution(mesh):
    return jax.shard_map(
        shards,
        mesh=mesh,
        in_specs=(
            P(("ens", "dom"), None),
            P(("ens", "dom"), None),
            P(("ens", "dom"), None),
            P("dom"),
            P("dom", None),
            P("dom", None),
            P("dom"),
            P(),
            P(),
            P(),
            P(),
            P(),
            P(),
        ),
        out_specs=(
            P(("ens", "dom"), None),
            P("ens", None),
            P("ens", None),
            P("ens", None),
            P("ens", None),
            P("ens", None),
        ),
        check_vma=False,
    )
```

time: 97.7 us -> 89.7 us (0.918)
  local copies, waits for them, and re-layouts: 4.57 us -> 13.2 us
  Pallas kernels: 34.6 us -> 26.4 us
  starting transfers between devices: 17 us -> 13.7 us
  other arithmetic: 3.59 us -> 0.59 us
  waiting for transfers between devices: 36.9 us -> 34.3 us
    unnamed x5 -> x30, local copies, waits for them, and re-layouts: 2.64 us -> 11.7 us
    pallas_call x4 -> x6, Pallas kernels: 34.6 us -> 26.4 us  [the longest x1 15.5 us: shards(): pl.pallas_call(functools.partial(forward_kernel, device_count), out_shape...]
    ppermute x7 -> x14, waiting for transfers between devices: 36.9 us -> 29 us  [swap(): lax.ppermute(values, 'dom', [(d, d ^ 1 << bits[d % 2]) for d in range(dev...]
    all_to_all x1, waiting for transfers between devices: 0.01 us -> 5.25 us  [shards(): lax.all_to_all(send, 'dom', split_axis=0, concat_axis=0, tiled=True)]
    ppermute x7 -> x14, starting transfers between devices: 9.64 us -> 6.35 us  [swap(): lax.ppermute(values, 'dom', [(d, d ^ 1 << bits[d % 2]) for d in range(dev...]
    broadcast_in_dim x2 -> x0, local copies, waits for them, and re-layouts: 1.84 us -> none  [the longest x1 1.26 us: shards(): b_embed[None, :]]
    add x2 -> x4, other arithmetic: 1.98 us -> 0.38 us  [the longest x2 0.26 us: pair_sum(): return cut(kept + swap(sent, (0, 0)).astype(F32))]
    concatenate x3 -> x4, other arithmetic: 1.49 us -> 0.09 us  [reduce_pieces(): held = jnp.concatenate([held, swap(held, bits)], axis=0)]
  transfers between devices with their start and end apart: 8 -> 15, of which waited for: 7 -> 13; matrix products, arithmetic and copies ran while one was open for 2% -> 2% of each run, Pallas kernels for 6% -> 4%
where the time goes in v3:
time: 89.7 us; the launch traced here: 89 us
  waiting for transfers between devices  34.3 us (38%)
  Pallas kernels  26.4 us (29%)
  starting transfers between devices  13.7 us (15%)
  local copies, waits for them, and re-layouts  13.2 us (15%)
    ppermute x14, waiting for transfers between devices, swap(): lax.ppermute(values, 'dom', [(d, d ^ 1 << bits[d % 2]) for d in range(dev...  29 us
    pallas_call x1, Pallas kernels, shards(): pl.pallas_call(functools.partial(forward_kernel, device_count), out_shape...  15.5 us
    unnamed x30, local copies, waits for them, and re-layouts  11.7 us
    all_to_all x1, starting transfers between devices, shards(): lax.all_to_all(send, 'dom', split_axis=0, concat_axis=0, tiled=True)  7.36 us
    ppermute x14, starting transfers between devices, swap(): lax.ppermute(values, 'dom', [(d, d ^ 1 << bits[d % 2]) for d in range(dev...  6.35 us
    all_to_all x1, waiting for transfers between devices, shards(): lax.all_to_all(send, 'dom', split_axis=0, concat_axis=0, tiled=True)  5.25 us
    pallas_call x1, Pallas kernels, shards(): pl.pallas_call(functools.partial(backward_kernel, channels, device_count)...  4.87 us
    pallas_call x2, Pallas kernels, unpack(): pl.pallas_call(functools.partial(unpack_kernel, device_count, bounds), ou...  2.68 us
  transfers between devices with their start and end apart: 15, of which 13 were waited for; matrix products, arithmetic and copies ran while one was open for 2% of the time, Pallas kernels for 4%

profile of v3, /device:TPU:0, one launch (start us, length us, event | category | flops | bytes accessed | tf_op | source)
XLA Modules:
  0.0 89.0 jit_solution(6025960157294421658)
XLA Ops:
  0.6 1.0 %copy-done = bf16[1024,227]{0,1:T(8,128)(2,1)S(1)} copy-done((bf16[1024,227]{0,1:T(8,128)(2,1)S(1)}, bf16[1024,227]{0,1:T(8,128)(2,1)}, u32[]{:S(2)}) %copy-start) | copy-done | bytes 464920
  2.3 0.9 %pick_rows.1 = bf16[16,4,256]{2,1,0:T(4,128)(2,1)} custom-call(s32[1,64]{1,0:T(1,128)S(1)} %bitcast.4, bf16[227,1024]{1,0:T(8,128)(2,1)S(1)} %bitcast.2), custom_call_target="tpu_custom_call" | custom-call | tf_op jit(solution)/shard_map/pick_rows/pallas_call | solution.py:316
  3.2 7.4 %all-to-all-start = ((bf16[16,4,256]{2,1,0:T(4,128)(2,1)}), bf16[16,4,256]{2,1,0:T(4,128)(2,1)S(1)}, u32[]{:S(2)}, u32[]{:S(2)}) async-start(bf16[16,4,256]{2,1,0:T(4,128)(2,1)} %pick_rows.1), calls=%async_computation | async-start | bytes 65536 | tf_op jit(solution)/shard_map/all_to_all | solution.py:324
  12.0 5.3 %all-to-all-done.feat_in = bf16[16,4,256]{2,1,0:T(4,128)(2,1)S(1)} async-done(((bf16[16,4,256]{2,1,0:T(4,128)(2,1)}), bf16[16,4,256]{2,1,0:T(4,128)(2,1)S(1)}, u32[]{:S(2)}, u32[]{:S(2)}) %all-to-all-start) | async-done | bytes 32800 | tf_op jit(solution)/shard_map/all_to_all | solution.py:324
  17.2 1.0 %copy-done.1 = bf16[1024,227]{0,1:T(8,128)(2,1)S(1)} copy-done((bf16[1024,227]{0,1:T(8,128)(2,1)S(1)}, bf16[1024,227]{0,1:T(8,128)(2,1)}, u32[]{:S(2)}) %copy-start.1) | copy-done | bytes 464920
  18.2 1.0 %copy-done.3 = bf16[512,512]{1,0:T(8,128)(2,1)S(1)} copy-done((bf16[512,512]{1,0:T(8,128)(2,1)S(1)}, bf16[512,512]{1,0:T(8,128)(2,1)}, u32[]{:S(2)}) %copy-start.3) | copy-done | bytes 524312
  19.3 1.0 %copy-done.4 = bf16[512,512]{1,0:T(8,128)(2,1)S(1)} copy-done((bf16[512,512]{1,0:T(8,128)(2,1)S(1)}, bf16[512,512]{1,0:T(8,128)(2,1)}, u32[]{:S(2)}) %copy-start.4) | copy-done | bytes 524312
  20.3 1.0 %copy-done.5 = bf16[512,512]{1,0:T(8,128)(2,1)S(1)} copy-done((bf16[512,512]{1,0:T(8,128)(2,1)S(1)}, bf16[512,512]{1,0:T(8,128)(2,1)}, u32[]{:S(2)}) %copy-start.5) | copy-done | bytes 524312
  21.4 1.0 %copy-done.6 = bf16[512,512]{1,0:T(8,128)(2,1)S(1)} copy-done((bf16[512,512]{1,0:T(8,128)(2,1)S(1)}, bf16[512,512]{1,0:T(8,128)(2,1)}, u32[]{:S(2)}) %copy-start.6) | copy-done | bytes 524312
  22.4 1.0 %copy-done.7 = bf16[512,512]{1,0:T(8,128)(2,1)S(1)} copy-done((bf16[512,512]{1,0:T(8,128)(2,1)S(1)}, bf16[512,512]{1,0:T(8,128)(2,1)}, u32[]{:S(2)}) %copy-start.7) | copy-done | bytes 524312
  23.5 0.9 %copy-done.9 = bf16[227,512]{1,0:T(8,128)(2,1)S(1)} copy-done((bf16[227,512]{1,0:T(8,128)(2,1)S(1)}, bf16[227,512]{1,0:T(8,128)(2,1)}, u32[]{:S(2)}) %copy-start.9) | copy-done | bytes 232472
  24.4 0.7 copy-done.10
  25.1 0.7 copy-done.11
  26.5 15.5 %forward_rows.1 = (bf16[512,512]{1,0:T(8,128)(2,1)}, bf16[4096,512]{1,0:T(8,128)(2,1)S(1)}, bf16[1088,512]{1,0:T(8,128)(2,1)S(1)}, bf16[1088,256]{1,0:T(8,128)(2...) custom-call(s32[4]{0:T(128)S(1)} %copy-done.13, ...), custom_call_target="tpu_custom_call" | custom-call | flops 9714008064 | bytes 8388608 | tf_op jit(solution)/shard_map/forward_rows/pallas_call | solution.py:332
  41.9 2.5 %scatter_rows.1.slot_half = f32[1088,512]{1,0:T(8,128)S(1)} custom-call(s32[4,1024]{1,0:T(4,128)S(1)} %copy-done.11, bf16[4096,512]{1,0:T(8,128)(2,1)S(1)} %get-tuple-element.25.pgrad), custom_call_target="tpu_custom_call" | custom-call | flops 2281701376 | bytes 2097152 | tf_op jit(solution)/shard_map/scatter_rows/pallas_call | solution.py:407
  44.7 0.8 copy-done.8
  45.5 4.9 %backward_rows.1 = (f32[384,512]{1,0:T(8,128)S(1)}, bf16[384,512]{1,0:T(8,128)(2,1)S(1)}) custom-call(s32[4,1024]{1,0:T(4,128)S(1)} %copy-done.12, bf16[4096,512]{1,0:T(8,128)(2,1)S(1)} %get-tuple-element.25.pgrad, f32[1088,512]{1,0:T(8,128)S(1)} %scatter_rows.1.slot_half, bf16[1088,512]{1,0:T(8,128)(2,1)S(1)} %get-tuple-element.29.latent, ...), custom_call_target="tpu_custom_call" | custom-call | flops 3992977408 | bytes 2097152 | tf_op jit(solution)/shard_map/backward_rows/pallas_call | solution.py:423
  51.3 1.0 %collective-permute-done.1 = bf16[384,512]{1,0:T(8,128)(2,1)S(1)} collective-permute-done((bf16[384,512]{1,0:T(8,128)(2,1)S(1)}, bf16[384,512]{1,0:T(8,128)(2,1)S(1)}, u32[]{:S(2)}, u32[]{:S(2)}) %collective-permute-start.1) | collective-permute-done | bytes 393248 | tf_op jit(solution)/shard_map/ppermute | solution.py:384
  52.5 0.7 collective-permute-start.2
  53.2 4.1 %collective-permute-done.8 = bf16[256,512]{1,0:T(8,128)(2,1)S(1)} collective-permute-done((bf16[256,512]{1,0:T(8,128)(2,1)S(1)}, bf16[256,512]{1,0:T(8,128)(2,1)S(1)}, u32[]{:S(2)}, u32[]{:S(2)}) %collective-permute-start.8) | collective-permute-done | bytes 262176 | tf_op jit(solution)/shard_map/ppermute | solution.py:384
  57.8 1.6 %collective-permute-done.2 = bf16[192,512]{1,0:T(8,128)(2,1)S(1)} collective-permute-done((bf16[192,512]{1,0:T(8,128)(2,1)S(1)}, bf16[192,512]{1,0:T(8,128)(2,1)S(1)}, u32[]{:S(2)}, u32[]{:S(2)}) %collective-permute-start.2) | collective-permute-done | bytes 196640 | tf_op jit(solution)/shard_map/ppermute | solution.py:384
  59.9 2.5 %collective-permute-done.9 = bf16[128,512]{1,0:T(8,128)(2,1)S(1)} collective-permute-done((bf16[128,512]{1,0:T(8,128)(2,1)S(1)}, bf16[128,512]{1,0:T(8,128)(2,1)S(1)}, u32[]{:S(2)}, u32[]{:S(2)}) %collective-permute-start.9) | collective-permute-done | bytes 131104 | tf_op jit(solution)/shard_map/ppermute | solution.py:384
  62.9 1.3 %collective-permute-done.3 = bf16[96,512]{1,0:T(8,128)(2,1)S(1)} collective-permute-done((bf16[96,512]{1,0:T(8,128)(2,1)S(1)}, bf16[96,512]{1,0:T(8,128)(2,1)S(1)}, u32[]{:S(2)}, u32[]{:S(2)}) %collective-permute-start.3) | collective-permute-done | bytes 98336 | tf_op jit(solution)/shard_map/ppermute | solution.py:384
  64.3 1.3 %collective-permute-start.4 = (bf16[96,512]{1,0:T(8,128)(2,1)S(1)}, bf16[96,512]{1,0:T(8,128)(2,1)S(1)}, u32[]{:S(2)}, u32[]{:S(2)}) collective-permute-start(bf16[96,512]{1,0:T(8,128)(2,1)S(1)} %fusion.1), channel_id=1, source_target_pairs={{0,8},{1,9},{2,10},{3,11},{4,12},{5,13},{6,14},{7,15},{8,0},{9,1},... | collective-permute-start | bytes 294920 | tf_op jit(solution)/shard_map/ppermute | solution.py:384
  65.6 6.7 %collective-permute-done.10 = bf16[128,512]{1,0:T(8,128)(2,1)S(1)} collective-permute-done((bf16[128,512]{1,0:T(8,128)(2,1)S(1)}, bf16[128,512]{1,0:T(8,128)(2,1)S(1)}, u32[]{:S(2)}, u32[]{:S(2)}) %collective-permute-start.10) | collective-permute-done | bytes 131104 | tf_op jit(solution)/shard_map/ppermute | solution.py:384
  72.4 1.4 %collective-permute-done.4 = bf16[96,512]{1,0:T(8,128)(2,1)S(1)} collective-permute-done((bf16[96,512]{1,0:T(8,128)(2,1)S(1)}, bf16[96,512]{1,0:T(8,128)(2,1)S(1)}, u32[]{:S(2)}, u32[]{:S(2)}) %collective-permute-start.4) | collective-permute-done | bytes 98336 | tf_op jit(solution)/shard_map/ppermute | solution.py:384
  74.6 2.8 %collective-permute-done.11 = bf16[128,512]{1,0:T(8,128)(2,1)S(1)} collective-permute-done((bf16[128,512]{1,0:T(8,128)(2,1)S(1)}, bf16[128,512]{1,0:T(8,128)(2,1)S(1)}, u32[]{:S(2)}, u32[]{:S(2)}) %collective-permute-start.11) | collective-permute-done | bytes 131104 | tf_op jit(solution)/shard_map/ppermute | solution.py:384
  78.1 1.2 %collective-permute-done.5 = bf16[96,512]{1,0:T(8,128)(2,1)S(1)} collective-permute-done((bf16[96,512]{1,0:T(8,128)(2,1)S(1)}, bf16[96,512]{1,0:T(8,128)(2,1)S(1)}, u32[]{:S(2)}, u32[]{:S(2)}) %collective-permute-start.5) | collective-permute-done | bytes 98336 | tf_op jit(solution)/shard_map/ppermute | solution.py:384
  79.9 3.9 %collective-permute-done.12 = bf16[256,512]{1,0:T(8,128)(2,1)S(1)} collective-permute-done((bf16[256,512]{1,0:T(8,128)(2,1)S(1)}, bf16[256,512]{1,0:T(8,128)(2,1)S(1)}, u32[]{:S(2)}, u32[]{:S(2)}) %collective-permute-start.12) | collective-permute-done | bytes 262176 | tf_op jit(solution)/shard_map/ppermute | solution.py:384
  84.0 2.0 %collective-permute-done.6 = bf16[192,512]{1,0:T(8,128)(2,1)S(1)} collective-permute-done((bf16[192,512]{1,0:T(8,128)(2,1)S(1)}, bf16[192,512]{1,0:T(8,128)(2,1)S(1)}, u32[]{:S(2)}, u32[]{:S(2)}) %collective-permute-start.6) | collective-permute-done | bytes 196640 | tf_op jit(solution)/shard_map/ppermute | solution.py:384
  86.1 1.5 %unpack_rows.3 = (f32[512,512]{1,0:T(8,128)}, f32[512,512]{1,0:T(8,128)}) custom-call(bf16[512,512]{1,0:T(8,128)(2,1)S(1)} %pad_maximum_fusion.held, bf16[512,512]{1,0:T(8,128)(2,1)S(1)} %collective-permute-done.13.got), custom_call_target="tpu_custom_call" | custom-call | tf_op jit(solution)/shard_map/unpack_rows/pallas_call | solution.py:445
  87.8 1.2 %unpack_rows.2 = (f32[512,512]{1,0:T(8,128)}, f32[227,512]{1,0:T(8,128)}, f32[2,512]{1,0:T(2,128)}) custom-call(bf16[384,512]{1,0:T(8,128)(2,1)S(1)} %pad_maximum_fusion.1.held, bf16[384,512]{1,0:T(8,128)(2,1)S(1)} %collective-permute-done.7.got), custom_call_target="tpu_custom_call" | custom-call | tf_op jit(solution)/shard_map/unpack_rows/pallas_call | solution.py:445
  (55 shorter events, 7.9 us)
Async XLA Ops:
  0.6 1.0 %copy-start = (bf16[1024,227]{0,1:T(8,128)(2,1)S(1)}, bf16[1024,227]{0,1:T(8,128)(2,1)}, u32[]{:S(2)}) copy-start(bf16[1024,227]{0,1:T(8,128)(2,1)} %param.13) | copy-start | bytes 1394692
  1.7 0.7 copy-start.2
  3.2 14.0 %all-to-all-start = ((bf16[16,4,256]{2,1,0:T(4,128)(2,1)}), bf16[16,4,256]{2,1,0:T(4,128)(2,1)S(1)}, u32[]{:S(2)}, u32[]{:S(2)}) async-start(bf16[16,4,256]{2,1,0:T(4,128)(2,1)} %pick_rows.1), calls=%async_computation | async-start | bytes 65536 | tf_op jit(solution)/shard_map/all_to_all | solution.py:324
  17.2 1.0 %copy-start.1 = (bf16[1024,227]{0,1:T(8,128)(2,1)S(1)}, bf16[1024,227]{0,1:T(8,128)(2,1)}, u32[]{:S(2)}) copy-start(bf16[1024,227]{0,1:T(8,128)(2,1)} %param.13) | copy-start | bytes 1394692
  18.2 1.0 %copy-start.3 = (bf16[512,512]{1,0:T(8,128)(2,1)S(1)}, bf16[512,512]{1,0:T(8,128)(2,1)}, u32[]{:S(2)}) copy-start(bf16[512,512]{1,0:T(8,128)(2,1)} %w_dst.1) | copy-start | bytes 1572868
  19.3 1.0 %copy-start.4 = (bf16[512,512]{1,0:T(8,128)(2,1)S(1)}, bf16[512,512]{1,0:T(8,128)(2,1)}, u32[]{:S(2)}) copy-start(bf16[512,512]{1,0:T(8,128)(2,1)} %w_out.1) | copy-start | bytes 1572868
  20.3 1.0 %copy-start.5 = (bf16[512,512]{1,0:T(8,128)(2,1)S(1)}, bf16[512,512]{1,0:T(8,128)(2,1)}, u32[]{:S(2)}) copy-start(bf16[512,512]{1,0:T(8,128)(2,1)} %mesh.1) | copy-start | bytes 1572868
  21.4 1.0 %copy-start.6 = (bf16[512,512]{1,0:T(8,128)(2,1)S(1)}, bf16[512,512]{1,0:T(8,128)(2,1)}, u32[]{:S(2)}) copy-start(bf16[512,512]{1,0:T(8,128)(2,1)} %cot.1) | copy-start | bytes 1572868
  22.4 1.0 %copy-start.7 = (bf16[512,512]{1,0:T(8,128)(2,1)S(1)}, bf16[512,512]{1,0:T(8,128)(2,1)}, u32[]{:S(2)}) copy-start(bf16[512,512]{1,0:T(8,128)(2,1)} %w_src.3) | copy-start | bytes 1572868
  23.5 0.9 %copy-start.9 = (bf16[227,512]{1,0:T(8,128)(2,1)S(1)}, bf16[227,512]{1,0:T(8,128)(2,1)}, u32[]{:S(2)}) copy-start(bf16[227,512]{1,0:T(8,128)(2,1)} %w_embed.1) | copy-start | bytes 697348
  24.4 0.7 copy-start.10
  25.1 0.7 copy-start.11
  25.8 0.7 copy-start.13
  41.9 2.5 %collective-permute-start = (bf16[512,512]{1,0:T(8,128)(2,1)S(1)}, bf16[512,512]{1,0:T(8,128)(2,1)S(1)}, u32[]{:S(2)}, u32[]{:S(2)}) collective-permute-start(bf16[512,512]{1,0:T(8,128)(2,1)S(1)} %get-tuple-element.27), channel_id=1, source_target_pairs={{0,1},{1,0},{2,3},{3,2},{4,5},{5,4},{6,7},{7,6},{8,9},{9,8},{10,11... | collective-permute-start | bytes 1572872 | tf_op jit(solution)/shard_map/ppermute | solution.py:384
  44.4 1.0 %copy-start.8 = (bf16[512,512]{1,0:T(8,128)(2,1)S(1)}, bf16[512,512]{1,0:T(8,128)(2,1)}, u32[]{:S(2)}) copy-start(bf16[512,512]{1,0:T(8,128)(2,1)} %w_src.3) | copy-start | bytes 1572868
  44.4 1.0 %copy-start.12 = (s32[4,1024]{1,0:T(4,128)S(1)}, s32[4,1024]{1,0:T(4,128)}, u32[]{:S(2)}) copy-start(s32[4,1024]{1,0:T(4,128)} %src.5) | copy-start | bytes 49156
  44.6 5.7 %copy-start.14 = (f32[512,512]{1,0:T(8,128)}, f32[512,512]{1,0:T(8,128)S(1)}, u32[]{:S(2)}) copy-start(f32[512,512]{1,0:T(8,128)S(1)} %convert_add_fusion) | copy-start | bytes 3145732
  50.4 7.0 %slice-start = ((f32[512,512]{1,0:T(8,128)}), f32[256,512]{1,0:T(8,128)S(1)}, s32[]{:S(2)}) async-start(f32[512,512]{1,0:T(8,128)} %copy-done.14), calls=%async_computation.1 | async-start | bytes 1048576 | tf_op jit(solution)/shard_map/slice | solution.py:390
  50.4 1.9 %collective-permute-start.1 = (bf16[384,512]{1,0:T(8,128)(2,1)S(1)}, bf16[384,512]{1,0:T(8,128)(2,1)S(1)}, u32[]{:S(2)}, u32[]{:S(2)}) collective-permute-start(bf16[384,512]{1,0:T(8,128)(2,1)S(1)} %get-tuple-element.34), channel_id=1, source_target_pairs={{0,1},{1,0},{2,3},{3,2},{4,5},{5,4},{6,7},{7,6},{8,9},{9,8},{10,11... | collective-permute-start | bytes 1179656 | tf_op jit(solution)/shard_map/ppermute | solution.py:384
  51.0 6.4 %collective-permute-start.8 = (bf16[256,512]{1,0:T(8,128)(2,1)S(1)}, bf16[256,512]{1,0:T(8,128)(2,1)S(1)}, u32[]{:S(2)}, u32[]{:S(2)}) collective-permute-start(bf16[256,512]{1,0:T(8,128)(2,1)S(1)} %slice.55), channel_id=1, source_target_pairs={{0,2},{1,5},{2,0},{3,7},{4,6},{5,1},{6,4},{7,3},{8,10},{9,13},{10,... | collective-permute-start | bytes 786440 | tf_op jit(solution)/shard_map/ppermute | solution.py:384
  52.5 7.0 %collective-permute-start.2 = (bf16[192,512]{1,0:T(8,128)(2,1)S(1)}, bf16[192,512]{1,0:T(8,128)(2,1)S(1)}, u32[]{:S(2)}, u32[]{:S(2)}) collective-permute-start(bf16[192,512]{1,0:T(8,128)(2,1)S(1)} %slice.56), channel_id=1, source_target_pairs={{0,2},{1,5},{2,0},{3,7},{4,6},{5,1},{6,4},{7,3},{8,10},{9,13},{10,... | collective-permute-start | bytes 589832 | tf_op jit(solution)/shard_map/ppermute | solution.py:384
  57.4 5.0 %collective-permute-start.9 = (bf16[128,512]{1,0:T(8,128)(2,1)S(1)}, bf16[128,512]{1,0:T(8,128)(2,1)S(1)}, u32[]{:S(2)}, u32[]{:S(2)}) collective-permute-start(bf16[128,512]{1,0:T(8,128)(2,1)S(1)} %slice.57), channel_id=1, source_target_pairs={{0,4},{1,3},{2,6},{3,1},{4,0},{5,7},{6,2},{7,5},{8,12},{9,11},{10,... | collective-permute-start | bytes 393224 | tf_op jit(solution)/shard_map/ppermute | solution.py:384
  59.6 4.7 %collective-permute-start.3 = (bf16[96,512]{1,0:T(8,128)(2,1)S(1)}, bf16[96,512]{1,0:T(8,128)(2,1)S(1)}, u32[]{:S(2)}, u32[]{:S(2)}) collective-permute-start(bf16[96,512]{1,0:T(8,128)(2,1)S(1)} %slice.58), channel_id=1, source_target_pairs={{0,4},{1,3},{2,6},{3,1},{4,0},{5,7},{6,2},{7,5},{8,12},{9,11},{10,... | collective-permute-start | bytes 294920 | tf_op jit(solution)/shard_map/ppermute | solution.py:384
  62.5 9.8 %collective-permute-start.10 = (bf16[128,512]{1,0:T(8,128)(2,1)S(1)}, bf16[128,512]{1,0:T(8,128)(2,1)S(1)}, u32[]{:S(2)}, u32[]{:S(2)}) collective-permute-start(bf16[128,512]{1,0:T(8,128)(2,1)S(1)} %fusion), channel_id=1, source_target_pairs={{0,8},{1,9},{2,10},{3,11},{4,12},{5,13},{6,14},{7,15},{8,0},{9,1},... | collective-permute-start | bytes 393224 | tf_op jit(solution)/shard_map/ppermute | solution.py:384
  64.3 9.6 %collective-permute-start.4 = (bf16[96,512]{1,0:T(8,128)(2,1)S(1)}, bf16[96,512]{1,0:T(8,128)(2,1)S(1)}, u32[]{:S(2)}, u32[]{:S(2)}) collective-permute-start(bf16[96,512]{1,0:T(8,128)(2,1)S(1)} %fusion.1), channel_id=1, source_target_pairs={{0,8},{1,9},{2,10},{3,11},{4,12},{5,13},{6,14},{7,15},{8,0},{9,1},... | collective-permute-start | bytes 294920 | tf_op jit(solution)/shard_map/ppermute | solution.py:384
  72.4 5.0 %collective-permute-start.11 = (bf16[128,512]{1,0:T(8,128)(2,1)S(1)}, bf16[128,512]{1,0:T(8,128)(2,1)S(1)}, u32[]{:S(2)}, u32[]{:S(2)}) collective-permute-start(bf16[128,512]{1,0:T(8,128)(2,1)S(1)} %add_convert_fusion), channel_id=1, source_target_pairs={{0,4},{1,3},{2,6},{3,1},{4,0},{5,7},{6,2},{7,5},{8,12},{9,11},{10,... | collective-permute-start | bytes 393224 | tf_op jit(solution)/shard_map/ppermute | solution.py:384
  73.9 5.5 %collective-permute-start.5 = (bf16[96,512]{1,0:T(8,128)(2,1)S(1)}, bf16[96,512]{1,0:T(8,128)(2,1)S(1)}, u32[]{:S(2)}, u32[]{:S(2)}) collective-permute-start(bf16[96,512]{1,0:T(8,128)(2,1)S(1)} %add_convert_fusion.1), channel_id=1, source_target_pairs={{0,4},{1,3},{2,6},{3,1},{4,0},{5,7},{6,2},{7,5},{8,12},{9,11},{10,... | collective-permute-start | bytes 294920 | tf_op jit(solution)/shard_map/ppermute | solution.py:384
  77.4 6.4 %collective-permute-start.12 = (bf16[256,512]{1,0:T(8,128)(2,1)S(1)}, bf16[256,512]{1,0:T(8,128)(2,1)S(1)}, u32[]{:S(2)}, u32[]{:S(2)}) collective-permute-start(bf16[256,512]{1,0:T(8,128)(2,1)S(1)} %pad_maximum_fusion.2), channel_id=1, source_target_pairs={{0,2},{1,5},{2,0},{3,7},{4,6},{5,1},{6,4},{7,3},{8,10},{9,13},{10,... | collective-permute-start | bytes 786440 | tf_op jit(solution)/shard_map/ppermute | solution.py:384
  79.4 6.6 %collective-permute-start.6 = (bf16[192,512]{1,0:T(8,128)(2,1)S(1)}, bf16[192,512]{1,0:T(8,128)(2,1)S(1)}, u32[]{:S(2)}, u32[]{:S(2)}) collective-permute-start(bf16[192,512]{1,0:T(8,128)(2,1)S(1)} %pad_maximum_fusion.3), channel_id=1, source_target_pairs={{0,2},{1,5},{2,0},{3,7},{4,6},{5,1},{6,4},{7,3},{8,10},{9,13},{10,... | collective-permute-start | bytes 589832 | tf_op jit(solution)/shard_map/ppermute | solution.py:384
  83.9 2.2 %collective-permute-start.13 = (bf16[512,512]{1,0:T(8,128)(2,1)S(1)}, bf16[512,512]{1,0:T(8,128)(2,1)S(1)}, u32[]{:S(2)}, u32[]{:S(2)}) collective-permute-start(bf16[512,512]{1,0:T(8,128)(2,1)S(1)} %pad_maximum_fusion.held), channel_id=1, source_target_pairs={{0,1},{1,0},{2,3},{3,2},{4,5},{5,4},{6,7},{7,6},{8,9},{9,8},{10,11... | collective-permute-start | bytes 1572872 | tf_op jit(solution)/shard_map/ppermute | solution.py:384
  86.0 1.8 %collective-permute-start.7 = (bf16[384,512]{1,0:T(8,128)(2,1)S(1)}, bf16[384,512]{1,0:T(8,128)(2,1)S(1)}, u32[]{:S(2)}, u32[]{:S(2)}) collective-permute-start(bf16[384,512]{1,0:T(8,128)(2,1)S(1)} %pad_maximum_fusion.1.held), channel_id=1, source_target_pairs={{0,1},{1,0},{2,3},{3,2},{4,5},{5,4},{6,7},{7,6},{8,9},{9,8},{10,11... | collective-permute-start | bytes 1179656 | tf_op jit(solution)/shard_map/ppermute | solution.py:384

commit v4 on v3

--- a/solution.py
+++ b/solution.py
@@ -25,15 +25,23 @@
     return -(-value // step) * step
 
 
-def pick_kernel(row_pack, feat_t, send):
+def fetch(source, target, sems, index):
+    copy = pltpu.make_async_copy(source, target, sems.at[index])
+    copy.start()
+    return copy
+
+
+def pick_kernel(row_pack, feat_hbm, send, feat_t, sems):
+    rows_copy = fetch(feat_hbm, feat_t, sems, 0)
     channels, own = feat_t.shape
     peers, peer_slots, padded = send.shape
     row = lax.broadcasted_iota(jnp.int32, (own, peers * peer_slots), 0)
     pick = jnp.where(row == row_pack[...], 1.0, 0.0).astype(BF16)
-    rows = mm(pick, feat_t[...], 0, 1)
     last = padded - 128
     lane = lax.broadcasted_iota(jnp.int32, (peers * peer_slots, 128), 1) + last
     ones = jnp.where(lane == channels, 1.0, 0.0).astype(BF16)
+    rows_copy.wait()
+    rows = mm(pick, feat_t[...], 0, 1)
     for j in range(peers):
         part = slice(j * peer_slots, (j + 1) * peer_slots)
         send[j, :, last:padded] = ones[part, :]
@@ -73,43 +81,114 @@
         sent[p * piece : (p + 1) * piece, :] = grads[at, :].astype(BF16)
 
 
+def own_kernel(
+    feat_hbm,
+    w_embed_hbm,
+    w_src_hbm,
+    w_dst_hbm,
+    w_out_hbm,
+    mesh_hbm,
+    cot_hbm,
+    b_embed,
+    latent,
+    feat,
+    w_pad,
+    proj,
+    near,
+    back,
+    feat_t,
+    w_embed,
+    w_src,
+    w_dst,
+    w_out,
+    mesh,
+    cot,
+    wide,
+    wide_t,
+    sems,
+):
+    feat_copy = fetch(feat_hbm, feat_t, sems, 0)
+    embed_copy = fetch(w_embed_hbm, w_embed, sems, 1)
+    src_copy = fetch(w_src_hbm, w_src, sems, 2)
+    mesh_copy = fetch(mesh_hbm, mesh, sems, 3)
+    dst_copy = fetch(w_dst_hbm, w_dst, sems, 4)
+    cot_copy = fetch(cot_hbm, cot, sems, 5)
+    out_copy = fetch(w_out_hbm, w_out, sems, 6)
+    channels, own = feat_t.shape
+    padded, width = w_pad.shape
+    last = padded - 32
+    step = 256
+    wide[last:padded, :] = jnp.zeros((32, width), F32)
+    wide_t[last:padded, :] = jnp.zeros((32, own), F32)
+    embed_copy.wait()
+    wide[0:channels, :] = w_embed[...].astype(F32)
+    wide[channels : channels + 1, :] = b_embed[...].astype(F32).reshape(1, width)
+    w_pad[...] = wide[...].astype(BF16)
+    feat_copy.wait()
+    wide_t[0:channels, :] = feat_t[...].astype(F32)
+    wide_t[channels : channels + 1, :] = jnp.ones((1, own), F32)
+    feat[...] = jnp.transpose(wide_t[...]).astype(BF16)
+    src_copy.wait()
+    for r in range(0, own, step):
+        pre = mm(feat[r : r + step, :], w_pad[...])
+        lat = (pre * sigmoid(pre)).astype(BF16)
+        latent[r : r + step, :] = lat
+        proj[r : r + step, :] = mm(lat, w_src[...]).astype(BF16)
+    mesh_copy.wait()
+    dst_copy.wait()
+    near[...] = mm(mesh[...], w_dst[...]).astype(BF16)
+    cot_copy.wait()
+    out_copy.wait()
+    full = mm(cot[...], w_out[...], 1, 1)
+    high = full.astype(BF16)
+    back[0] = high
+    back[1] = (full - high.astype(F32)).astype(BF16)
+
+
 def forward_kernel(
     device_count,
     count,
     src,
     dst,
     feat_in,
-    feat_t,
-    w_embed,
-    biases,
-    w_src,
-    w_dst,
-    w_out,
-    mesh,
-    cot,
+    b_hidden,
+    latent_own,
+    feat_own,
+    w_pad,
+    proj,
+    near,
+    back,
+    w_src_hbm,
+    w_out_hbm,
+    mesh_hbm,
+    cot_hbm,
     mesh_out,
     pgrad,
-    latent,
-    feat,
-    w_pad,
+    latent_in,
+    feat_rows,
     bias_sum,
     kept,
     sent,
     table,
     pair,
-    wide,
-    wide_t,
     incoming,
     one_hot,
     one_hot_t,
     hid,
-    near,
-    back,
     node_sum,
     hid_sum,
     grads,
+    w_src,
+    w_out,
+    mesh,
+    cot,
+    sems,
 ):
-    channels, own = feat_t.shape
+    src_copy = fetch(w_src_hbm, w_src, sems, 0)
+    mesh_copy = fetch(mesh_hbm, mesh, sems, 1)
+    out_copy = fetch(w_out_hbm, w_out, sems, 2)
+    cot_copy = fetch(cot_hbm, cot, sems, 3)
+    own = latent_own.shape[0]
     peers, peer_slots, padded = feat_in.shape
     more = peers * peer_slots
     slots = own + more
@@ -120,34 +199,21 @@
     depth = table.shape[0]
     step = 256
 
-    last = padded - 32
-    wide[last:padded, :] = jnp.zeros((32, width), F32)
-    wide[0:channels, :] = w_embed[...].astype(F32)
-    wide[channels : channels + 1, :] = biases[0:1, :].astype(F32)
-    w_pad[...] = wide[...].astype(BF16)
-    wide_t[last:padded, :] = jnp.zeros((32, own), F32)
-    wide_t[0:channels, :] = feat_t[...].astype(F32)
-    wide_t[channels : channels + 1, :] = jnp.ones((1, own), F32)
-    feat[0:own, :] = jnp.transpose(wide_t[...]).astype(BF16)
     for j in range(peers):
         incoming[j * peer_slots : (j + 1) * peer_slots, :] = feat_in[j].astype(F32)
-    feat[own:slots, :] = incoming[...].astype(BF16)
-    for r in range(0, slots, step):
-        end = min(r + step, slots)
-        pre = mm(feat[r:end, :], w_pad[...])
-        lat = (pre * sigmoid(pre)).astype(BF16)
-        latent[r:end, :] = lat
-        table[block + r : block + end, :] = mm(lat, w_src[...]).astype(BF16)
-    near[...] = mm(mesh[...], w_dst[...]).astype(BF16)
-    full = mm(cot[...], w_out[...], 1, 1)
-    high = full.astype(BF16)
-    back[0] = high
-    back[1] = (full - high.astype(F32)).astype(BF16)
+    feat_rows[...] = incoming[...].astype(BF16)
+    pre_in = mm(feat_rows[...], w_pad[...])
+    lat_in = (pre_in * sigmoid(pre_in)).astype(BF16)
+    latent_in[...] = lat_in
+    table[block : block + own, :] = proj[...]
     tail = depth - slots - block
     tail_row = lax.broadcasted_iota(jnp.int32, (tail, width), 0)
+    bias_row = b_hidden[...].astype(F32).reshape(1, width)
     table[slots + block : depth, :] = jnp.where(
-        tail_row == 0, jnp.broadcast_to(biases[1:2, :].astype(F32), (tail, width)), 0.0
+        tail_row == 0, jnp.broadcast_to(bias_row, (tail, width)), 0.0
     ).astype(BF16)
+    src_copy.wait()
+    table[block + own : block + slots, :] = mm(lat_in, w_src[...]).astype(BF16)
 
     edge_lane = lax.broadcasted_iota(jnp.int32, (blocks, edges), 1)
     block_row = lax.broadcasted_iota(jnp.int32, (blocks, 1), 0)
@@ -195,6 +261,9 @@
 
     bias_sum[...] = jnp.broadcast_to(bias_total, bias_sum.shape)
     total = hid_sum[...]
+    mesh_copy.wait()
+    out_copy.wait()
+    cot_copy.wait()
     mesh_out[...] = (mesh[...].astype(F32) + mm(total, w_out[...])).astype(BF16)
     grads[0:width, :] = mm(total, cot[...], 0, 0)
     grads[width : 2 * width, :] = mm(mesh[...], node_sum[...], 0, 0)
@@ -220,32 +289,45 @@
     slot_sum[...] = scatter_rows(src, pgrad, one_hot_t, 0, src.shape[0] // 2)
 
 
+def scatter_rest_kernel(src, pgrad, slot_half, slot_grad, one_hot_t):
+    half = src.shape[0] // 2
+    rest = scatter_rows(src, pgrad, one_hot_t, half, src.shape[0] - half)
+    slot_grad[...] = (slot_half[...] + rest).astype(BF16)
+
+
 def backward_kernel(
     channels,
     device_count,
-    src,
-    pgrad,
-    slot_half,
+    slot_grad,
+    latent_own,
+    latent_in,
+    feat_own,
+    feat_in,
+    w_pad,
+    bias_sum,
+    w_src_hbm,
+    kept,
+    sent,
     latent,
     feat,
-    w_pad,
+    grads,
     w_src,
-    bias_sum,
-    kept,
-    sent,
-    one_hot_t,
-    grads,
+    sems,
 ):
+    src_copy = fetch(w_src_hbm, w_src, sems, 0)
+    own = latent_own.shape[0]
+    slots = latent.shape[0]
     width = w_src.shape[0]
     padded = feat.shape[1]
-    half = src.shape[0] // 2
-    rest = src.shape[0] - half
-    slot_sum = slot_half[...] + scatter_rows(src, pgrad, one_hot_t, half, rest)
-    slot_grad = slot_sum.astype(BF16)
-    grads[0:width, :] = mm(latent[...], slot_grad, 0, 0)
-    buffer_grad = mm(slot_grad, w_src[...], 1, 1)
+    latent[0:own, :] = latent_own[...]
+    latent[own:slots, :] = latent_in[...]
+    feat[0:own, :] = feat_own[...]
+    feat[own:slots, :] = feat_in[...]
     pre = mm(feat[...], w_pad[...])
     sig = sigmoid(pre)
+    grads[0:width, :] = mm(latent[...], slot_grad[...], 0, 0)
+    src_copy.wait()
+    buffer_grad = mm(slot_grad[...], w_src[...], 1, 1)
     embed = (buffer_grad * (sig * (1.0 + pre * (1.0 - sig)))).astype(BF16)
     grads[width : width + padded, :] = mm(feat[...], embed, 0, 0)
     grads[width + channels + 1 : width + channels + 2, :] = bias_sum[0:1, :]
@@ -304,61 +386,95 @@
     mesh_rows = round_up(2 * width, 32 * pieces)
     grid_rows = round_up(width + padded, 32 * pieces)
     half_blocks = blocks // 2
+    stages = list(zip(first, second))
 
     vmem = pl.BlockSpec(memory_space=pltpu.VMEM)
     smem = pl.BlockSpec(memory_space=pltpu.SMEM)
+    hbm = pl.BlockSpec(memory_space=pltpu.HBM)
     shape = jax.ShapeDtypeStruct
 
     def limit(mib):
         return pltpu.CompilerParams(vmem_limit_bytes=mib * 1024 * 1024)
 
     feat_t = grid_feat.T
+    dma = pltpu.SemaphoreType.DMA
     send = pl.pallas_call(
         pick_kernel,
         out_shape=shape((device_count, peer_slots, padded), BF16),
-        in_specs=[vmem] * 2,
+        in_specs=[vmem, hbm],
         out_specs=vmem,
+        scratch_shapes=[pltpu.VMEM((channels, own), BF16), dma((1,))],
         compiler_params=limit(16),
+        cost_estimate=pl.CostEstimate(
+            flops=20_000_000_000, bytes_accessed=own * padded * 2, transcendentals=0
+        ),
         name="pick_rows",
     )(row_pack[None, :], feat_t)
     feat_in = lax.all_to_all(send, "dom", split_axis=0, concat_axis=0, tiled=True)
-    bias_rows = jnp.stack([b_embed, b_hidden])
-
-    forward_macs = (
-        slots * width * (padded + width)
-        + blocks * edges * width * (depth + 4 * block)
-        + 5 * nodes * width * width
-    )
-    mesh_out, pgrad, latent, feat, w_pad, bias_sum, kept_mesh, sent_mesh = pl.pallas_call(
+
+    own_macs = own * width * (padded + width) + 2 * nodes * width * width
+    latent_own, feat_own, w_pad, proj, near, back = pl.pallas_call(
+        own_kernel,
+        out_shape=(
+            shape((own, width), BF16),
+            shape((own, padded), BF16),
+            shape((padded, width), BF16),
+            shape((own, width), BF16),
+            shape((nodes, width), BF16),
+            shape((2, nodes, width), BF16),
+        ),
+        in_specs=[hbm] * 7 + [vmem],
+        out_specs=(vmem,) * 6,
+        scratch_shapes=[
+            pltpu.VMEM((channels, own), BF16),
+            pltpu.VMEM((channels, width), BF16),
+            pltpu.VMEM((width, width), BF16),
+            pltpu.VMEM((width, width), BF16),
+            pltpu.VMEM((width, width), BF16),
+            pltpu.VMEM((nodes, width), BF16),
+            pltpu.VMEM((nodes, width), BF16),
+            pltpu.VMEM((padded, width), F32),
+            pltpu.VMEM((padded, own), F32),
+            dma((7,)),
+        ],
+        compiler_params=limit(24),
+        cost_estimate=pl.CostEstimate(
+            flops=4 * own_macs, bytes_accessed=8 * own * width, transcendentals=own * width
+        ),
+        name="own_rows",
+    )(feat_t, w_embed, w_src, w_dst, w_out, mesh_latent, cotangent, b_embed)
+
+    forward_macs = blocks * edges * width * (depth + 4 * block) + 3 * nodes * width * width
+    mesh_out, pgrad, latent_in, feat_rows, bias_sum, kept_mesh, sent_mesh = pl.pallas_call(
         functools.partial(forward_kernel, device_count),
         out_shape=(
             shape((nodes, width), BF16),
             shape((blocks * edges, width), BF16),
-            shape((slots, width), BF16),
-            shape((slots, padded), BF16),
-            shape((padded, width), BF16),
+            shape((more, width), BF16),
+            shape((more, padded), BF16),
             shape((8, width), F32),
             shape((mesh_rows // 2, width), F32),
             shape((mesh_rows // 2, width), BF16),
         ),
-        in_specs=[smem] + [vmem] * 11,
-        out_specs=(vmem,) * 8,
+        in_specs=[smem] + [vmem] * 10 + [hbm] * 4,
+        out_specs=(vmem,) * 7,
         scratch_shapes=[
             pltpu.VMEM((depth, width), BF16),
             pltpu.VMEM((2 * block, width), BF16),
-            pltpu.VMEM((padded, width), F32),
-            pltpu.VMEM((padded, own), F32),
             pltpu.VMEM((more, padded), F32),
             pltpu.VMEM((edges, depth + block), BF16),
             pltpu.VMEM((block, edges), BF16),
             pltpu.VMEM((edges, width), BF16),
             pltpu.VMEM((nodes, width), BF16),
-            pltpu.VMEM((2, nodes, width), BF16),
+            pltpu.VMEM((nodes, width), BF16),
+            pltpu.VMEM((mesh_rows, width), F32),
+            pltpu.VMEM((width, width), BF16),
+            pltpu.VMEM((width, width), BF16),
             pltpu.VMEM((nodes, width), BF16),
             pltpu.VMEM((nodes, width), BF16),
-            pltpu.VMEM((mesh_rows, width), F32),
+            dma((4,)),
         ],
-        compiler_params=limit(40),
+        compiler_params=limit(36),
         cost_estimate=pl.CostEstimate(
             flops=2 * forward_macs,
             bytes_accessed=16 * own * width,
@@ -370,11 +486,14 @@
         edge_src,
         edge_dst,
         feat_in,
-        feat_t,
-        w_embed,
-        bias_rows,
+        b_hidden,
+        latent_own,
+        feat_own,
+        w_pad,
+        proj,
+        near,
+        back,
         w_src,
-        w_dst,
         w_out,
         mesh_latent,
         cotangent,
@@ -392,11 +511,11 @@
     def pair_sum(kept, sent):
         return cut(kept + swap(sent, (0, 0)).astype(F32))
 
-    def reduce_pieces(held, sent):
-        stages = list(zip(first, second))
-        for bits in stages[:-1]:
-            held, sent = cut(held + swap(sent, bits).astype(F32))
-        held = (held + swap(sent, stages[-1]).astype(F32)).astype(BF16)
+    def reduce_pieces(held, got):
+        for bits in stages[1:]:
+            held, sent = cut(held + got.astype(F32))
+            got = swap(sent, bits)
+        held = (held + got.astype(F32)).astype(BF16)
         got = swap(held, (last_bit, last_bit))
         held = (held.astype(F32) + got.astype(F32)).astype(BF16)
         for bits in reversed(stages):
@@ -418,28 +537,47 @@
         ),
         name="scatter_rows",
     )(edge_src, pgrad)
-
     slot_half, held_mesh, next_mesh = lax.optimization_barrier((slot_half, held_mesh, next_mesh))
+    got_mesh = swap(next_mesh, stages[0])
+    slot_grad = pl.pallas_call(
+        scatter_rest_kernel,
+        out_shape=shape((slots, width), BF16),
+        in_specs=[vmem] * 3,
+        out_specs=vmem,
+        scratch_shapes=[pltpu.VMEM((slots, (blocks - half_blocks) * edges), BF16)],
+        compiler_params=limit(24),
+        cost_estimate=pl.CostEstimate(
+            flops=4 * half_blocks * edges * slots * width,
+            bytes_accessed=half_blocks * edges * width * 2,
+            transcendentals=0,
+        ),
+        name="scatter_rest",
+    )(edge_src, pgrad, slot_half)
+    slot_grad, got_mesh = lax.optimization_barrier((slot_grad, got_mesh))
+
     kept_grid, sent_grid = pl.pallas_call(
         functools.partial(backward_kernel, channels, device_count),
         out_shape=(
             shape((grid_rows // 2, width), F32),
             shape((grid_rows // 2, width), BF16),
         ),
-        in_specs=[vmem] * 8,
+        in_specs=[vmem] * 7 + [hbm],
         out_specs=(vmem,) * 2,
         scratch_shapes=[
-            pltpu.VMEM((slots, (blocks - half_blocks) * edges), BF16),
+            pltpu.VMEM((slots, width), BF16),
+            pltpu.VMEM((slots, padded), BF16),
             pltpu.VMEM((grid_rows, width), F32),
+            pltpu.VMEM((width, width), BF16),
+            dma((1,)),
         ],
-        compiler_params=limit(40),
+        compiler_params=limit(24),
         cost_estimate=pl.CostEstimate(
-            flops=2 * slots * width * (half_blocks * edges + 2 * width + 2 * padded),
-            bytes_accessed=half_blocks * edges * width * 2,
+            flops=4 * slots * width * (2 * width + 2 * padded),
+            bytes_accessed=slots * width * 2,
             transcendentals=slots * width,
         ),
         name="backward_rows",
-    )(edge_src, pgrad, slot_half, latent, feat, w_pad, w_src, bias_sum)
+    )(slot_grad, latent_own, latent_in, feat_own, feat_rows, w_pad, bias_sum, w_src)
 
     def unpack(pair, bounds):
         return pl.pallas_call(
@@ -451,8 +589,9 @@
             name="unpack_rows",
         )(*pair)
 
-    mesh_pair = reduce_pieces(held_mesh, next_mesh)
-    grid_pair = reduce_pieces(*pair_sum(kept_grid, sent_grid))
+    mesh_pair = reduce_pieces(held_mesh, got_mesh)
+    held_grid, next_grid = pair_sum(kept_grid, sent_grid)
+    grid_pair = reduce_pieces(held_grid, swap(next_grid, stages[0]))
     grad_out, grad_dst = unpack(mesh_pair, ((0, width), (width, 2 * width)))
     end = width + channels
     grad_src, grad_embed, biases = unpack(grid_pair, ((0, width), (width, end), (end, end + 2)))

time: 89.7 us -> 92.8 us (1.035)
  waiting for transfers between devices: 34.3 us -> 23.2 us
  starting transfers between devices: 13.7 us -> 24.3 us
  Pallas kernels: 26.4 us -> 29.4 us
    ppermute x14, starting transfers between devices: 6.35 us -> 17 us  [swap(): lax.ppermute(values, 'dom', [(d, d ^ 1 << bits[d % 2]) for d in range(dev...]
    pallas_call x0 -> x2, Pallas kernels: none -> 5.83 us  [the longest x1 3.35 us: shards(): pl.pallas_call(own_kernel, out_shape=(shape((own, width), BF16), shape((o...]
    ppermute x14, waiting for transfers between devices: 29 us -> 23.2 us  [swap(): lax.ppermute(values, 'dom', [(d, d ^ 1 << bits[d % 2]) for d in range(dev...]
    all_to_all x1, waiting for transfers between devices: 5.25 us -> 0.01 us  [shards(): lax.all_to_all(send, 'dom', split_axis=0, concat_axis=0, tiled=True)]
    pallas_call x1, Pallas kernels: 4.87 us -> 2.49 us  [shards(): pl.pallas_call(functools.partial(backward_kernel, channels, device_count)...]
    unnamed x30 -> x54, local copies, waits for them, and re-layouts: 11.7 us -> 13.6 us
    another operation x2 -> x0, local copies, waits for them, and re-layouts: 1.37 us -> none  [shards(): bias_rows = jnp.stack([b_embed, b_hidden])]
    pallas_call x1, Pallas kernels: 15.5 us -> 14.5 us  [shards(): pl.pallas_call(functools.partial(forward_kernel, device_count), out_shape...]
  transfers between devices with their start and end apart: 15 -> 15, of which waited for: 13 -> 11; matrix products, arithmetic and copies ran while one was open for 2% -> 0% of each run, Pallas kernels for 4% -> 11%
where the time goes in v4:
time: 92.8 us; the launch traced here: 92.3 us
  Pallas kernels  29.4 us (32%)
  starting transfers between devices  24.3 us (26%)
  waiting for transfers between devices  23.2 us (25%)
  local copies, waits for them, and re-layouts  13.7 us (15%)
  between operations  1.04 us (1%)
    ppermute x14, waiting for transfers between devices, swap(): lax.ppermute(values, 'dom', [(d, d ^ 1 << bits[d % 2]) for d in range(dev...  23.2 us
    ppermute x14, starting transfers between devices, swap(): lax.ppermute(values, 'dom', [(d, d ^ 1 << bits[d % 2]) for d in range(dev...  17 us
    pallas_call x1, Pallas kernels, shards(): pl.pallas_call(functools.partial(forward_kernel, device_count), out_shape...  14.5 us
    unnamed x54, local copies, waits for them, and re-layouts  13.6 us
    all_to_all x1, starting transfers between devices, shards(): lax.all_to_all(send, 'dom', split_axis=0, concat_axis=0, tiled=True)  7.37 us
    pallas_call x1, Pallas kernels, shards(): pl.pallas_call(own_kernel, out_shape=(shape((own, width), BF16), shape((o...  3.35 us
    pallas_call x1, Pallas kernels, shards(): pl.pallas_call(scatter_kernel, out_shape=shape((slots, width), F32), in_s...  2.69 us
    pallas_call x2, Pallas kernels, unpack(): pl.pallas_call(functools.partial(unpack_kernel, device_count, bounds), ou...  2.68 us
  transfers between devices with their start and end apart: 15, of which 11 were waited for; matrix products, arithmetic and copies ran while one was open for 0% of the time, Pallas kernels for 11%

profile of v4, /device:TPU:0, one launch (start us, length us, event | category | flops | bytes accessed | tf_op | source)
XLA Modules:
  0.0 92.3 jit_solution(3722253964419777502)
XLA Ops:
  0.6 1.0 %copy-done.5 = bf16[1024,227]{0,1:T(8,128)(2,1)S(1)} copy-done((bf16[1024,227]{0,1:T(8,128)(2,1)S(1)}, bf16[1024,227]{0,1:T(8,128)(2,1)}, u32[]{:S(2)}) %copy-start.5) | copy-done | bytes 464920
  2.4 1.3 %pick_rows.1 = bf16[16,4,256]{2,1,0:T(4,128)(2,1)} custom-call(s32[1,64]{1,0:T(1,128)S(1)} %bitcast.4, bf16[227,1024]{1,0:T(8,128)(2,1)S(1)} %bitcast.2), custom_call_target="tpu_custom_call" | custom-call | flops 20000000000 | bytes 524288 | tf_op jit(solution)/shard_map/pick_rows/pallas_call | solution.py:401
  3.7 7.4 %all-to-all-start = ((bf16[16,4,256]{2,1,0:T(4,128)(2,1)}), bf16[16,4,256]{2,1,0:T(4,128)(2,1)S(1)}, u32[]{:S(2)}, u32[]{:S(2)}) async-start(bf16[16,4,256]{2,1,0:T(4,128)(2,1)} %pick_rows.1), calls=%async_computation | async-start | bytes 65536 | tf_op jit(solution)/shard_map/all_to_all | solution.py:413
  11.2 3.4 %own_rows.1 = (bf16[1024,512]{1,0:T(8,128)(2,1)S(1)}, bf16[1024,256]{1,0:T(8,128)(2,1)S(1)}, bf16[256,512]{1,0:T(8,128)(2,1)S(1)}, bf16[1024,512]{1,0:T(8,128)(2...) custom-call(bf16[227,1024]{1,0:T(8,128)(2,1)S(1)} %bitcast.3, bf16[227,512]{1,0:T(8,128)(2,1)S(1)} %copy-done.7, ...), custom_call_target="tpu_custom_call" | custom-call | flops 2684354560 | bytes 4194304 | tf_op jit(solution)/shard_map/own_rows/pallas_call | solution.py:416
  15.5 1.0 %copy-done.16 = bf16[1024,512]{1,0:T(8,128)(2,1)} copy-done((bf16[1024,512]{1,0:T(8,128)(2,1)}, bf16[1024,512]{1,0:T(8,128)(2,1)S(1)}, u32[]{:S(2)}) %copy-start.16) | copy-done | bytes 1048600
  19.8 1.2 %copy-done.15 = bf16[1024,512]{1,0:T(8,128)(2,1)S(1)} copy-done((bf16[1024,512]{1,0:T(8,128)(2,1)S(1)}, bf16[1024,512]{1,0:T(8,128)(2,1)}, u32[]{:S(2)}) %copy-start.15) | copy-done | bytes 1048600
  21.0 1.2 %copy-done.17 = bf16[1024,512]{1,0:T(8,128)(2,1)S(1)} copy-done((bf16[1024,512]{1,0:T(8,128)(2,1)S(1)}, bf16[1024,512]{1,0:T(8,128)(2,1)}, u32[]{:S(2)}) %copy-start.17) | copy-done | bytes 1048600
  22.2 1.2 %copy-done.19 = bf16[2,512,512]{2,1,0:T(8,128)(2,1)S(1)} copy-done((bf16[2,512,512]{2,1,0:T(8,128)(2,1)S(1)}, bf16[2,512,512]{2,1,0:T(8,128)(2,1)}, u32[]{:S(2)}) %copy-start.19) | copy-done | bytes 1048600
  23.5 1.0 %copy-done.21 = bf16[1024,256]{1,0:T(8,128)(2,1)S(1)} copy-done((bf16[1024,256]{1,0:T(8,128)(2,1)S(1)}, bf16[1024,256]{1,0:T(8,128)(2,1)}, u32[]{:S(2)}) %copy-start.21) | copy-done | bytes 524312
  24.5 1.0 %copy-done.23 = bf16[512,512]{1,0:T(8,128)(2,1)S(1)} copy-done((bf16[512,512]{1,0:T(8,128)(2,1)S(1)}, bf16[512,512]{1,0:T(8,128)(2,1)}, u32[]{:S(2)}) %copy-start.23) | copy-done | bytes 524312
  26.5 14.5 %forward_rows.1 = (bf16[512,512]{1,0:T(8,128)(2,1)}, bf16[4096,512]{1,0:T(8,128)(2,1)S(1)}, bf16[64,512]{1,0:T(8,128)(2,1)S(1)}, bf16[64,256]{1,0:T(8,128)(2,1)S...) custom-call(s32[4]{0:T(128)S(1)} %copy-done.13, s32[4,1024]{1,0:T(4,128)S(1)} %copy-done.9, ...), custom_call_target="tpu_custom_call" | custom-call | flops 8321499136 | bytes 8388608 | tf_op jit(solution)/shard_map/forward_rows/pallas_call | solution.py:448
  41.4 2.7 %scatter_rows.1.slot_half = f32[1088,512]{1,0:T(8,128)S(1)} custom-call(s32[4,1024]{1,0:T(4,128)S(1)} %copy-done.9, bf16[4096,512]{1,0:T(8,128)(2,1)S(1)} %get-tuple-element.38.pgrad), custom_call_target="tpu_custom_call" | custom-call | flops 2281701376 | bytes 2097152 | tf_op jit(solution)/shard_map/scatter_rows/pallas_call | solution.py:526
  44.3 1.7 %collective-permute-start.1 = (bf16[256,512]{1,0:T(8,128)(2,1)S(1)}, bf16[256,512]{1,0:T(8,128)(2,1)S(1)}, u32[]{:S(2)}, u32[]{:S(2)}) collective-permute-start(bf16[256,512]{1,0:T(8,128)(2,1)S(1)} %slice.55), channel_id=1, source_target_pairs={{0,2},{1,5},{2,0},{3,7},{4,6},{5,1},{6,4},{7,3},{8,10},{9,13},{10,... | collective-permute-start | bytes 786440 | tf_op jit(solution)/shard_map/ppermute | solution.py:503
  46.1 2.5 %scatter_rest.1.slot_grad = bf16[1088,512]{1,0:T(8,128)(2,1)S(1)} custom-call(s32[4,1024]{1,0:T(4,128)S(1)} %copy-done.9, bf16[4096,512]{1,0:T(8,128)(2,1)S(1)} %get-tuple-element.38.pgrad, f32[1088,512]{1,0:T(8,128)S(1)} %scatter_rows.1.slot_half), custom_call_target="tpu_custom_call" | custom-call | flops 4563402752 | bytes 2097152 | tf_op jit(solution)/shard_map/scatter_rest/pallas_call | solution.py:542
  48.6 2.2 %collective-permute-done.1 = bf16[256,512]{1,0:T(8,128)(2,1)S(1)} collective-permute-done((bf16[256,512]{1,0:T(8,128)(2,1)S(1)}, bf16[256,512]{1,0:T(8,128)(2,1)S(1)}, u32[]{:S(2)}, u32[]{:S(2)}) %collective-permute-start.1) | collective-permute-done | bytes 262176 | tf_op jit(solution)/shard_map/ppermute | solution.py:503
  50.8 2.5 %backward_rows.1 = (f32[384,512]{1,0:T(8,128)S(1)}, bf16[384,512]{1,0:T(8,128)(2,1)S(1)}) custom-call(bf16[1088,512]{1,0:T(8,128)(2,1)S(1)} %scatter_rest.1.slot_grad, bf16[1024,512]{1,0:T(8,128)(2,1)S(1)} %copy-done.15, bf16[64,512]{1,0:T(8,128)(2,1)S(1)} %get-tuple-element.44.latent_in, bf16[1024,256]{1,0:T(8,128)(2,1)S(1)} %copy-done.21, ...), custom_call_target="tpu_custom_call" | custom-call | flops 3422552064 | bytes 1114112 | tf_op jit(solution)/shard_map/backward_rows/pallas_call | solution.py:558
  53.4 1.7 %collective-permute-done.2 = bf16[384,512]{1,0:T(8,128)(2,1)S(1)} collective-permute-done((bf16[384,512]{1,0:T(8,128)(2,1)S(1)}, bf16[384,512]{1,0:T(8,128)(2,1)S(1)}, u32[]{:S(2)}, u32[]{:S(2)}) %collective-permute-start.2) | collective-permute-done | bytes 393248 | tf_op jit(solution)/shard_map/ppermute | solution.py:503
  55.2 1.7 %collective-permute-start.3 = (bf16[192,512]{1,0:T(8,128)(2,1)S(1)}, bf16[192,512]{1,0:T(8,128)(2,1)S(1)}, u32[]{:S(2)}, u32[]{:S(2)}) collective-permute-start(bf16[192,512]{1,0:T(8,128)(2,1)S(1)} %slice.56), channel_id=1, source_target_pairs={{0,2},{1,5},{2,0},{3,7},{4,6},{5,1},{6,4},{7,3},{8,10},{9,13},{10,... | collective-permute-start | bytes 589832 | tf_op jit(solution)/shard_map/ppermute | solution.py:503
  57.1 1.5 %collective-permute-start.9 = (bf16[128,512]{1,0:T(8,128)(2,1)S(1)}, bf16[128,512]{1,0:T(8,128)(2,1)S(1)}, u32[]{:S(2)}, u32[]{:S(2)}) collective-permute-start(bf16[128,512]{1,0:T(8,128)(2,1)S(1)} %slice.57), channel_id=1, source_target_pairs={{0,4},{1,3},{2,6},{3,1},{4,0},{5,7},{6,2},{7,5},{8,12},{9,11},{10,... | collective-permute-start | bytes 393224 | tf_op jit(solution)/shard_map/ppermute | solution.py:503
  58.6 3.8 %collective-permute-done.3 = bf16[192,512]{1,0:T(8,128)(2,1)S(1)} collective-permute-done((bf16[192,512]{1,0:T(8,128)(2,1)S(1)}, bf16[192,512]{1,0:T(8,128)(2,1)S(1)}, u32[]{:S(2)}, u32[]{:S(2)}) %collective-permute-start.3) | collective-permute-done | bytes 196640 | tf_op jit(solution)/shard_map/ppermute | solution.py:503
  62.4 1.2 %collective-permute-start.4 = (bf16[96,512]{1,0:T(8,128)(2,1)S(1)}, bf16[96,512]{1,0:T(8,128)(2,1)S(1)}, u32[]{:S(2)}, u32[]{:S(2)}) collective-permute-start(bf16[96,512]{1,0:T(8,128)(2,1)S(1)} %slice.58), channel_id=1, source_target_pairs={{0,4},{1,3},{2,6},{3,1},{4,0},{5,7},{6,2},{7,5},{8,12},{9,11},{10,... | collective-permute-start | bytes 294920 | tf_op jit(solution)/shard_map/ppermute | solution.py:503
  63.6 2.6 %collective-permute-start.10 = (bf16[128,512]{1,0:T(8,128)(2,1)S(1)}, bf16[128,512]{1,0:T(8,128)(2,1)S(1)}, u32[]{:S(2)}, u32[]{:S(2)}) collective-permute-start(bf16[128,512]{1,0:T(8,128)(2,1)S(1)} %fusion), channel_id=1, source_target_pairs={{0,8},{1,9},{2,10},{3,11},{4,12},{5,13},{6,14},{7,15},{8,0},{9,1},... | collective-permute-start | bytes 393224 | tf_op jit(solution)/shard_map/ppermute | solution.py:503
  66.3 1.6 %collective-permute-done.4 = bf16[96,512]{1,0:T(8,128)(2,1)S(1)} collective-permute-done((bf16[96,512]{1,0:T(8,128)(2,1)S(1)}, bf16[96,512]{1,0:T(8,128)(2,1)S(1)}, u32[]{:S(2)}, u32[]{:S(2)}) %collective-permute-start.4) | collective-permute-done | bytes 98336 | tf_op jit(solution)/shard_map/ppermute | solution.py:503
  67.9 2.3 %collective-permute-start.5 = (bf16[96,512]{1,0:T(8,128)(2,1)S(1)}, bf16[96,512]{1,0:T(8,128)(2,1)S(1)}, u32[]{:S(2)}, u32[]{:S(2)}) collective-permute-start(bf16[96,512]{1,0:T(8,128)(2,1)S(1)} %fusion.1), channel_id=1, source_target_pairs={{0,8},{1,9},{2,10},{3,11},{4,12},{5,13},{6,14},{7,15},{8,0},{9,1},... | collective-permute-start | bytes 294920 | tf_op jit(solution)/shard_map/ppermute | solution.py:503
  70.2 4.4 %collective-permute-done.10 = bf16[128,512]{1,0:T(8,128)(2,1)S(1)} collective-permute-done((bf16[128,512]{1,0:T(8,128)(2,1)S(1)}, bf16[128,512]{1,0:T(8,128)(2,1)S(1)}, u32[]{:S(2)}, u32[]{:S(2)}) %collective-permute-start.10) | collective-permute-done | bytes 131104 | tf_op jit(solution)/shard_map/ppermute | solution.py:503
  76.8 3.9 %collective-permute-done.11 = bf16[128,512]{1,0:T(8,128)(2,1)S(1)} collective-permute-done((bf16[128,512]{1,0:T(8,128)(2,1)S(1)}, bf16[128,512]{1,0:T(8,128)(2,1)S(1)}, u32[]{:S(2)}, u32[]{:S(2)}) %collective-permute-start.11) | collective-permute-done | bytes 131104 | tf_op jit(solution)/shard_map/ppermute | solution.py:503
  80.8 1.9 %collective-permute-start.12 = (bf16[256,512]{1,0:T(8,128)(2,1)S(1)}, bf16[256,512]{1,0:T(8,128)(2,1)S(1)}, u32[]{:S(2)}, u32[]{:S(2)}) collective-permute-start(bf16[256,512]{1,0:T(8,128)(2,1)S(1)} %pad_maximum_fusion.2), channel_id=1, source_target_pairs={{0,2},{1,5},{2,0},{3,7},{4,6},{5,1},{6,4},{7,3},{8,10},{9,13},{10,... | collective-permute-start | bytes 786440 | tf_op jit(solution)/shard_map/ppermute | solution.py:503
  82.9 1.9 %collective-permute-start.7 = (bf16[192,512]{1,0:T(8,128)(2,1)S(1)}, bf16[192,512]{1,0:T(8,128)(2,1)S(1)}, u32[]{:S(2)}, u32[]{:S(2)}) collective-permute-start(bf16[192,512]{1,0:T(8,128)(2,1)S(1)} %pad_maximum_fusion.3), channel_id=1, source_target_pairs={{0,2},{1,5},{2,0},{3,7},{4,6},{5,1},{6,4},{7,3},{8,10},{9,13},{10,... | collective-permute-start | bytes 589832 | tf_op jit(solution)/shard_map/ppermute | solution.py:503
  84.7 2.5 %collective-permute-done.12 = bf16[256,512]{1,0:T(8,128)(2,1)S(1)} collective-permute-done((bf16[256,512]{1,0:T(8,128)(2,1)S(1)}, bf16[256,512]{1,0:T(8,128)(2,1)S(1)}, u32[]{:S(2)}, u32[]{:S(2)}) %collective-permute-start.12) | collective-permute-done | bytes 262176 | tf_op jit(solution)/shard_map/ppermute | solution.py:503
  87.3 2.0 %collective-permute-done.7 = bf16[192,512]{1,0:T(8,128)(2,1)S(1)} collective-permute-done((bf16[192,512]{1,0:T(8,128)(2,1)S(1)}, bf16[192,512]{1,0:T(8,128)(2,1)S(1)}, u32[]{:S(2)}, u32[]{:S(2)}) %collective-permute-start.7) | collective-permute-done | bytes 196640 | tf_op jit(solution)/shard_map/ppermute | solution.py:503
  89.4 1.5 %unpack_rows.3 = (f32[512,512]{1,0:T(8,128)}, f32[512,512]{1,0:T(8,128)}) custom-call(bf16[512,512]{1,0:T(8,128)(2,1)S(1)} %pad_maximum_fusion.held, bf16[512,512]{1,0:T(8,128)(2,1)S(1)} %collective-permute-done.13.got), custom_call_target="tpu_custom_call" | custom-call | tf_op jit(solution)/shard_map/unpack_rows/pallas_call | solution.py:583
  91.1 1.2 %unpack_rows.2 = (f32[512,512]{1,0:T(8,128)}, f32[227,512]{1,0:T(8,128)}, f32[2,512]{1,0:T(2,128)}) custom-call(bf16[384,512]{1,0:T(8,128)(2,1)S(1)} %pad_maximum_fusion.1.held, bf16[384,512]{1,0:T(8,128)(2,1)S(1)} %collective-permute-done.8.got), custom_call_target="tpu_custom_call" | custom-call | tf_op jit(solution)/shard_map/unpack_rows/pallas_call | solution.py:583
  (78 shorter events, 9.9 us)
Async XLA Ops:
  2.3 8.7 %copy-start = (bf16[512,512]{1,0:T(8,128)(2,1)S(1)}, bf16[512,512]{1,0:T(8,128)(2,1)}, u32[]{:S(2)}) copy-start(bf16[512,512]{1,0:T(8,128)(2,1)} %w_dst_hbm.1) | copy-start | bytes 1572868
  2.3 8.7 %copy-start.1 = (bf16[512,512]{1,0:T(8,128)(2,1)S(1)}, bf16[512,512]{1,0:T(8,128)(2,1)}, u32[]{:S(2)}) copy-start(bf16[512,512]{1,0:T(8,128)(2,1)} %w_out_hbm.3) | copy-start | bytes 1572868
  2.3 8.7 %copy-start.2 = (bf16[512,512]{1,0:T(8,128)(2,1)S(1)}, bf16[512,512]{1,0:T(8,128)(2,1)}, u32[]{:S(2)}) copy-start(bf16[512,512]{1,0:T(8,128)(2,1)} %mesh_hbm.3) | copy-start | bytes 1572868
  2.3 8.8 %copy-start.3 = (bf16[512,512]{1,0:T(8,128)(2,1)S(1)}, bf16[512,512]{1,0:T(8,128)(2,1)}, u32[]{:S(2)}) copy-start(bf16[512,512]{1,0:T(8,128)(2,1)} %cot_hbm.3) | copy-start | bytes 1572868
  2.3 8.8 %copy-start.4 = (bf16[512,512]{1,0:T(8,128)(2,1)S(1)}, bf16[512,512]{1,0:T(8,128)(2,1)}, u32[]{:S(2)}) copy-start(bf16[512,512]{1,0:T(8,128)(2,1)} %w_src_hbm.5) | copy-start | bytes 1572868
  2.3 8.8 %copy-start.6 = (bf16[1024,227]{0,1:T(8,128)(2,1)S(1)}, bf16[1024,227]{0,1:T(8,128)(2,1)}, u32[]{:S(2)}) copy-start(bf16[1024,227]{0,1:T(8,128)(2,1)} %param.13) | copy-start | bytes 1394692
  2.3 8.8 %copy-start.7 = (bf16[227,512]{1,0:T(8,128)(2,1)S(1)}, bf16[227,512]{1,0:T(8,128)(2,1)}, u32[]{:S(2)}) copy-start(bf16[227,512]{1,0:T(8,128)(2,1)} %w_embed_hbm.1) | copy-start | bytes 697348
  2.4 8.8 %copy-start.10 = (bf16[512]{0:T(512)(128)(2,1)S(1)}, bf16[512]{0:T(512)(128)(2,1)}, u32[]{:S(2)}) copy-start(bf16[512]{0:T(512)(128)(2,1)} %b_embed.1) | copy-start | bytes 3076
  3.7 16.1 %all-to-all-start = ((bf16[16,4,256]{2,1,0:T(4,128)(2,1)}), bf16[16,4,256]{2,1,0:T(4,128)(2,1)S(1)}, u32[]{:S(2)}, u32[]{:S(2)}) async-start(bf16[16,4,256]{2,1,0:T(4,128)(2,1)} %pick_rows.1), calls=%async_computation | async-start | bytes 65536 | tf_op jit(solution)/shard_map/all_to_all | solution.py:413
  11.1 8.6 %copy-start.8 = (s32[4,1024]{1,0:T(4,128)S(1)}, s32[4,1024]{1,0:T(4,128)}, u32[]{:S(2)}) copy-start(s32[4,1024]{1,0:T(4,128)} %dst.1) | copy-start | bytes 49156
  11.1 8.6 %copy-start.9 = (s32[4,1024]{1,0:T(4,128)S(1)}, s32[4,1024]{1,0:T(4,128)}, u32[]{:S(2)}) copy-start(s32[4,1024]{1,0:T(4,128)} %src.5) | copy-start | bytes 49156
  11.1 8.6 %copy-start.11 = (bf16[512]{0:T(512)(128)(2,1)S(1)}, bf16[512]{0:T(512)(128)(2,1)}, u32[]{:S(2)}) copy-start(bf16[512]{0:T(512)(128)(2,1)} %b_hidden.1) | copy-start | bytes 3076
  11.2 8.6 %copy-start.13 = (s32[4]{0:T(128)S(1)}, s32[4]{0:T(128)}, u32[]{:S(2)}) copy-start(s32[4]{0:T(128)} %count.1) | copy-start | bytes 52
  19.8 1.2 %copy-start.15 = (bf16[1024,512]{1,0:T(8,128)(2,1)S(1)}, bf16[1024,512]{1,0:T(8,128)(2,1)}, u32[]{:S(2)}) copy-start(bf16[1024,512]{1,0:T(8,128)(2,1)} %copy-done.14) | copy-start | bytes 3145732
  21.0 1.2 %copy-start.17 = (bf16[1024,512]{1,0:T(8,128)(2,1)S(1)}, bf16[1024,512]{1,0:T(8,128)(2,1)}, u32[]{:S(2)}) copy-start(bf16[1024,512]{1,0:T(8,128)(2,1)} %copy-done.16) | copy-start | bytes 3145732
  22.2 1.2 %copy-start.19 = (bf16[2,512,512]{2,1,0:T(8,128)(2,1)S(1)}, bf16[2,512,512]{2,1,0:T(8,128)(2,1)}, u32[]{:S(2)}) copy-start(bf16[2,512,512]{2,1,0:T(8,128)(2,1)} %copy-done.18) | copy-start | bytes 3145732
  41.0 3.2 %collective-permute-start = (bf16[512,512]{1,0:T(8,128)(2,1)S(1)}, bf16[512,512]{1,0:T(8,128)(2,1)S(1)}, u32[]{:S(2)}, u32[]{:S(2)}) collective-permute-start(bf16[512,512]{1,0:T(8,128)(2,1)S(1)} %get-tuple-element.40), channel_id=1, source_target_pairs={{0,1},{1,0},{2,3},{3,2},{4,5},{5,4},{6,7},{7,6},{8,9},{9,8},{10,11... | collective-permute-start | bytes 1572872 | tf_op jit(solution)/shard_map/ppermute | solution.py:503
  44.3 4.3 %copy-start.26 = (f32[512,512]{1,0:T(8,128)}, f32[512,512]{1,0:T(8,128)S(1)}, u32[]{:S(2)}) copy-start(f32[512,512]{1,0:T(8,128)S(1)} %convert_add_fusion) | copy-start | bytes 3145732
  44.3 6.4 %collective-permute-start.1 = (bf16[256,512]{1,0:T(8,128)(2,1)S(1)}, bf16[256,512]{1,0:T(8,128)(2,1)S(1)}, u32[]{:S(2)}, u32[]{:S(2)}) collective-permute-start(bf16[256,512]{1,0:T(8,128)(2,1)S(1)} %slice.55), channel_id=1, source_target_pairs={{0,2},{1,5},{2,0},{3,7},{4,6},{5,1},{6,4},{7,3},{8,10},{9,13},{10,... | collective-permute-start | bytes 786440 | tf_op jit(solution)/shard_map/ppermute | solution.py:503
  53.3 3.7 %slice-start = ((f32[512,512]{1,0:T(8,128)}), f32[256,512]{1,0:T(8,128)S(1)}, s32[]{:S(2)}) async-start(f32[512,512]{1,0:T(8,128)} %copy-done.26), calls=%async_computation.1 | async-start | bytes 1048576 | tf_op jit(solution)/shard_map/slice | solution.py:509
  53.3 1.8 %collective-permute-start.2 = (bf16[384,512]{1,0:T(8,128)(2,1)S(1)}, bf16[384,512]{1,0:T(8,128)(2,1)S(1)}, u32[]{:S(2)}, u32[]{:S(2)}) collective-permute-start(bf16[384,512]{1,0:T(8,128)(2,1)S(1)} %get-tuple-element.48), channel_id=1, source_target_pairs={{0,1},{1,0},{2,3},{3,2},{4,5},{5,4},{6,7},{7,6},{8,9},{9,8},{10,11... | collective-permute-start | bytes 1179656 | tf_op jit(solution)/shard_map/ppermute | solution.py:503
  55.2 7.1 %collective-permute-start.3 = (bf16[192,512]{1,0:T(8,128)(2,1)S(1)}, bf16[192,512]{1,0:T(8,128)(2,1)S(1)}, u32[]{:S(2)}, u32[]{:S(2)}) collective-permute-start(bf16[192,512]{1,0:T(8,128)(2,1)S(1)} %slice.56), channel_id=1, source_target_pairs={{0,2},{1,5},{2,0},{3,7},{4,6},{5,1},{6,4},{7,3},{8,10},{9,13},{10,... | collective-permute-start | bytes 589832 | tf_op jit(solution)/shard_map/ppermute | solution.py:503
  57.1 6.5 %collective-permute-start.9 = (bf16[128,512]{1,0:T(8,128)(2,1)S(1)}, bf16[128,512]{1,0:T(8,128)(2,1)S(1)}, u32[]{:S(2)}, u32[]{:S(2)}) collective-permute-start(bf16[128,512]{1,0:T(8,128)(2,1)S(1)} %slice.57), channel_id=1, source_target_pairs={{0,4},{1,3},{2,6},{3,1},{4,0},{5,7},{6,2},{7,5},{8,12},{9,11},{10,... | collective-permute-start | bytes 393224 | tf_op jit(solution)/shard_map/ppermute | solution.py:503
  62.4 5.4 %collective-permute-start.4 = (bf16[96,512]{1,0:T(8,128)(2,1)S(1)}, bf16[96,512]{1,0:T(8,128)(2,1)S(1)}, u32[]{:S(2)}, u32[]{:S(2)}) collective-permute-start(bf16[96,512]{1,0:T(8,128)(2,1)S(1)} %slice.58), channel_id=1, source_target_pairs={{0,4},{1,3},{2,6},{3,1},{4,0},{5,7},{6,2},{7,5},{8,12},{9,11},{10,... | collective-permute-start | bytes 294920 | tf_op jit(solution)/shard_map/ppermute | solution.py:503
  63.6 11.0 %collective-permute-start.10 = (bf16[128,512]{1,0:T(8,128)(2,1)S(1)}, bf16[128,512]{1,0:T(8,128)(2,1)S(1)}, u32[]{:S(2)}, u32[]{:S(2)}) collective-permute-start(bf16[128,512]{1,0:T(8,128)(2,1)S(1)} %fusion), channel_id=1, source_target_pairs={{0,8},{1,9},{2,10},{3,11},{4,12},{5,13},{6,14},{7,15},{8,0},{9,1},... | collective-permute-start | bytes 393224 | tf_op jit(solution)/shard_map/ppermute | solution.py:503
  67.9 8.0 %collective-permute-start.5 = (bf16[96,512]{1,0:T(8,128)(2,1)S(1)}, bf16[96,512]{1,0:T(8,128)(2,1)S(1)}, u32[]{:S(2)}, u32[]{:S(2)}) collective-permute-start(bf16[96,512]{1,0:T(8,128)(2,1)S(1)} %fusion.1), channel_id=1, source_target_pairs={{0,8},{1,9},{2,10},{3,11},{4,12},{5,13},{6,14},{7,15},{8,0},{9,1},... | collective-permute-start | bytes 294920 | tf_op jit(solution)/shard_map/ppermute | solution.py:503
  74.6 6.1 %collective-permute-start.11 = (bf16[128,512]{1,0:T(8,128)(2,1)S(1)}, bf16[128,512]{1,0:T(8,128)(2,1)S(1)}, u32[]{:S(2)}, u32[]{:S(2)}) collective-permute-start(bf16[128,512]{1,0:T(8,128)(2,1)S(1)} %add_convert_fusion), channel_id=1, source_target_pairs={{0,4},{1,3},{2,6},{3,1},{4,0},{5,7},{6,2},{7,5},{8,12},{9,11},{10,... | collective-permute-start | bytes 393224 | tf_op jit(solution)/shard_map/ppermute | solution.py:503
  75.9 6.9 %collective-permute-start.6 = (bf16[96,512]{1,0:T(8,128)(2,1)S(1)}, bf16[96,512]{1,0:T(8,128)(2,1)S(1)}, u32[]{:S(2)}, u32[]{:S(2)}) collective-permute-start(bf16[96,512]{1,0:T(8,128)(2,1)S(1)} %add_convert_fusion.1), channel_id=1, source_target_pairs={{0,4},{1,3},{2,6},{3,1},{4,0},{5,7},{6,2},{7,5},{8,12},{9,11},{10,... | collective-permute-start | bytes 294920 | tf_op jit(solution)/shard_map/ppermute | solution.py:503
  80.8 6.4 %collective-permute-start.12 = (bf16[256,512]{1,0:T(8,128)(2,1)S(1)}, bf16[256,512]{1,0:T(8,128)(2,1)S(1)}, u32[]{:S(2)}, u32[]{:S(2)}) collective-permute-start(bf16[256,512]{1,0:T(8,128)(2,1)S(1)} %pad_maximum_fusion.2), channel_id=1, source_target_pairs={{0,2},{1,5},{2,0},{3,7},{4,6},{5,1},{6,4},{7,3},{8,10},{9,13},{10,... | collective-permute-start | bytes 786440 | tf_op jit(solution)/shard_map/ppermute | solution.py:503
  82.9 6.4 %collective-permute-start.7 = (bf16[192,512]{1,0:T(8,128)(2,1)S(1)}, bf16[192,512]{1,0:T(8,128)(2,1)S(1)}, u32[]{:S(2)}, u32[]{:S(2)}) collective-permute-start(bf16[192,512]{1,0:T(8,128)(2,1)S(1)} %pad_maximum_fusion.3), channel_id=1, source_target_pairs={{0,2},{1,5},{2,0},{3,7},{4,6},{5,1},{6,4},{7,3},{8,10},{9,13},{10,... | collective-permute-start | bytes 589832 | tf_op jit(solution)/shard_map/ppermute | solution.py:503
  87.2 2.2 %collective-permute-start.13 = (bf16[512,512]{1,0:T(8,128)(2,1)S(1)}, bf16[512,512]{1,0:T(8,128)(2,1)S(1)}, u32[]{:S(2)}, u32[]{:S(2)}) collective-permute-start(bf16[512,512]{1,0:T(8,128)(2,1)S(1)} %pad_maximum_fusion.held), channel_id=1, source_target_pairs={{0,1},{1,0},{2,3},{3,2},{4,5},{5,4},{6,7},{7,6},{8,9},{9,8},{10,11... | collective-permute-start | bytes 1572872 | tf_op jit(solution)/shard_map/ppermute | solution.py:503
  89.3 1.8 %collective-permute-start.8 = (bf16[384,512]{1,0:T(8,128)(2,1)S(1)}, bf16[384,512]{1,0:T(8,128)(2,1)S(1)}, u32[]{:S(2)}, u32[]{:S(2)}) collective-permute-start(bf16[384,512]{1,0:T(8,128)(2,1)S(1)} %pad_maximum_fusion.1.held), channel_id=1, source_target_pairs={{0,1},{1,0},{2,3},{3,2},{4,5},{5,4},{6,7},{7,6},{8,9},{9,8},{10,11... | collective-permute-start | bytes 1179656 | tf_op jit(solution)/shard_map/ppermute | solution.py:503
  (11 other events, 9.9 us)

commit v5 on v3

--- a/solution.py
+++ b/solution.py
@@ -25,15 +25,23 @@
     return -(-value // step) * step
 
 
-def pick_kernel(row_pack, feat_t, send):
+def fetch(source, target, sems, index):
+    copy = pltpu.make_async_copy(source, target, sems.at[index])
+    copy.start()
+    return copy
+
+
+def pick_kernel(row_pack, feat_hbm, send, feat_t, sems):
+    rows_copy = fetch(feat_hbm, feat_t, sems, 0)
     channels, own = feat_t.shape
     peers, peer_slots, padded = send.shape
     row = lax.broadcasted_iota(jnp.int32, (own, peers * peer_slots), 0)
     pick = jnp.where(row == row_pack[...], 1.0, 0.0).astype(BF16)
-    rows = mm(pick, feat_t[...], 0, 1)
     last = padded - 128
     lane = lax.broadcasted_iota(jnp.int32, (peers * peer_slots, 128), 1) + last
     ones = jnp.where(lane == channels, 1.0, 0.0).astype(BF16)
+    rows_copy.wait()
+    rows = mm(pick, feat_t[...], 0, 1)
     for j in range(peers):
         part = slice(j * peer_slots, (j + 1) * peer_slots)
         send[j, :, last:padded] = ones[part, :]
@@ -81,7 +89,8 @@
     feat_in,
     feat_t,
     w_embed,
-    biases,
+    b_embed,
+    b_hidden,
     w_src,
     w_dst,
     w_out,
@@ -123,7 +132,7 @@
     last = padded - 32
     wide[last:padded, :] = jnp.zeros((32, width), F32)
     wide[0:channels, :] = w_embed[...].astype(F32)
-    wide[channels : channels + 1, :] = biases[0:1, :].astype(F32)
+    wide[channels : channels + 1, :] = b_embed[...].astype(F32).reshape(1, width)
     w_pad[...] = wide[...].astype(BF16)
     wide_t[last:padded, :] = jnp.zeros((32, own), F32)
     wide_t[0:channels, :] = feat_t[...].astype(F32)
@@ -145,8 +154,9 @@
     back[1] = (full - high.astype(F32)).astype(BF16)
     tail = depth - slots - block
     tail_row = lax.broadcasted_iota(jnp.int32, (tail, width), 0)
+    bias_row = b_hidden[...].astype(F32).reshape(1, width)
     table[slots + block : depth, :] = jnp.where(
-        tail_row == 0, jnp.broadcast_to(biases[1:2, :].astype(F32), (tail, width)), 0.0
+        tail_row == 0, jnp.broadcast_to(bias_row, (tail, width)), 0.0
     ).astype(BF16)
 
     edge_lane = lax.broadcasted_iota(jnp.int32, (blocks, edges), 1)
@@ -304,25 +314,31 @@
     mesh_rows = round_up(2 * width, 32 * pieces)
     grid_rows = round_up(width + padded, 32 * pieces)
     half_blocks = blocks // 2
+    stages = list(zip(first, second))
 
     vmem = pl.BlockSpec(memory_space=pltpu.VMEM)
     smem = pl.BlockSpec(memory_space=pltpu.SMEM)
+    hbm = pl.BlockSpec(memory_space=pltpu.HBM)
     shape = jax.ShapeDtypeStruct
 
     def limit(mib):
         return pltpu.CompilerParams(vmem_limit_bytes=mib * 1024 * 1024)
 
     feat_t = grid_feat.T
+    dma = pltpu.SemaphoreType.DMA
     send = pl.pallas_call(
         pick_kernel,
         out_shape=shape((device_count, peer_slots, padded), BF16),
-        in_specs=[vmem] * 2,
+        in_specs=[vmem, hbm],
         out_specs=vmem,
+        scratch_shapes=[pltpu.VMEM((channels, own), BF16), dma((1,))],
         compiler_params=limit(16),
+        cost_estimate=pl.CostEstimate(
+            flops=20_000_000_000, bytes_accessed=own * padded * 2, transcendentals=0
+        ),
         name="pick_rows",
     )(row_pack[None, :], feat_t)
     feat_in = lax.all_to_all(send, "dom", split_axis=0, concat_axis=0, tiled=True)
-    bias_rows = jnp.stack([b_embed, b_hidden])
 
     forward_macs = (
         slots * width * (padded + width)
@@ -341,7 +357,7 @@
             shape((mesh_rows // 2, width), F32),
             shape((mesh_rows // 2, width), BF16),
         ),
-        in_specs=[smem] + [vmem] * 11,
+        in_specs=[smem] + [vmem] * 12,
         out_specs=(vmem,) * 8,
         scratch_shapes=[
             pltpu.VMEM((depth, width), BF16),
@@ -372,7 +388,8 @@
         feat_in,
         feat_t,
         w_embed,
-        bias_rows,
+        b_embed,
+        b_hidden,
         w_src,
         w_dst,
         w_out,
@@ -392,11 +409,11 @@
     def pair_sum(kept, sent):
         return cut(kept + swap(sent, (0, 0)).astype(F32))
 
-    def reduce_pieces(held, sent):
-        stages = list(zip(first, second))
-        for bits in stages[:-1]:
-            held, sent = cut(held + swap(sent, bits).astype(F32))
-        held = (held + swap(sent, stages[-1]).astype(F32)).astype(BF16)
+    def reduce_pieces(held, got):
+        for bits in stages[1:]:
+            held, sent = cut(held + got.astype(F32))
+            got = swap(sent, bits)
+        held = (held + got.astype(F32)).astype(BF16)
         got = swap(held, (last_bit, last_bit))
         held = (held.astype(F32) + got.astype(F32)).astype(BF16)
         for bits in reversed(stages):
@@ -420,6 +437,7 @@
     )(edge_src, pgrad)
 
     slot_half, held_mesh, next_mesh = lax.optimization_barrier((slot_half, held_mesh, next_mesh))
+    got_mesh = swap(next_mesh, stages[0])
     kept_grid, sent_grid = pl.pallas_call(
         functools.partial(backward_kernel, channels, device_count),
         out_shape=(
@@ -441,6 +459,8 @@
         name="backward_rows",
     )(edge_src, pgrad, slot_half, latent, feat, w_pad, w_src, bias_sum)
 
+    sent_grid, got_mesh = lax.optimization_barrier((sent_grid, got_mesh))
+
     def unpack(pair, bounds):
         return pl.pallas_call(
             functools.partial(unpack_kernel, device_count, bounds),
@@ -451,8 +471,9 @@
             name="unpack_rows",
         )(*pair)
 
-    mesh_pair = reduce_pieces(held_mesh, next_mesh)
-    grid_pair = reduce_pieces(*pair_sum(kept_grid, sent_grid))
+    mesh_pair = reduce_pieces(held_mesh, got_mesh)
+    held_grid, next_grid = pair_sum(kept_grid, sent_grid)
+    grid_pair = reduce_pieces(held_grid, swap(next_grid, stages[0]))
     grad_out, grad_dst = unpack(mesh_pair, ((0, width), (width, 2 * width)))
     end = width + channels
     grad_src, grad_embed, biases = unpack(grid_pair, ((0, width), (width, end), (end, end + 2)))

time: 89.7 us -> 80.9 us (0.902)
  blocking collectives: 0 us -> 13.9 us
  local copies, waits for them, and re-layouts: 13.2 us -> 1.83 us
  starting transfers between devices: 13.7 us -> 7.05 us
  waiting for transfers between devices: 34.3 us -> 29.9 us
    all_to_all x0 -> x1, blocking collectives: none -> 13.9 us  [shards(): lax.all_to_all(send, 'dom', split_axis=0, concat_axis=0, tiled=True)]
    unnamed x30, local copies, waits for them, and re-layouts: 11.7 us -> 1.73 us
    all_to_all x1 -> x0, starting transfers between devices: 7.36 us -> none  [shards(): lax.all_to_all(send, 'dom', split_axis=0, concat_axis=0, tiled=True)]
    all_to_all x1 -> x0, waiting for transfers between devices: 5.25 us -> none  [shards(): lax.all_to_all(send, 'dom', split_axis=0, concat_axis=0, tiled=True)]
    another operation x2 -> x0, local copies, waits for them, and re-layouts: 1.37 us -> none  [shards(): bias_rows = jnp.stack([b_embed, b_hidden])]
    ppermute x14, waiting for transfers between devices: 29 us -> 29.9 us  [swap(): lax.ppermute(values, 'dom', [(d, d ^ 1 << bits[d % 2]) for d in range(dev...]
  transfers between devices with their start and end apart: 15 -> 14, of which waited for: 13 -> 11; matrix products, arithmetic and copies ran while one was open for 2% -> 0% of each run, Pallas kernels for 4% -> 11%
where the time goes in v5:
time: 80.9 us; the launch traced here: 80.7 us
  waiting for transfers between devices  29.9 us (37%)
  Pallas kernels  26.4 us (33%)
  blocking collectives  13.9 us (17%)
  starting transfers between devices  7.05 us (9%)
  local copies, waits for them, and re-layouts  1.83 us (2%)
  between operations  0.97 us (1%)
    ppermute x14, waiting for transfers between devices, swap(): lax.ppermute(values, 'dom', [(d, d ^ 1 << bits[d % 2]) for d in range(dev...  29.9 us
    pallas_call x1, Pallas kernels, shards(): pl.pallas_call(functools.partial(forward_kernel, device_count), out_shape...  15.6 us
    all_to_all x1, blocking collectives, shards(): lax.all_to_all(send, 'dom', split_axis=0, concat_axis=0, tiled=True)  13.9 us
    ppermute x14, starting transfers between devices, swap(): lax.ppermute(values, 'dom', [(d, d ^ 1 << bits[d % 2]) for d in range(dev...  7.05 us
    pallas_call x1, Pallas kernels, shards(): pl.pallas_call(functools.partial(backward_kernel, channels, device_count)...  4.94 us
    pallas_call x2, Pallas kernels, unpack(): pl.pallas_call(functools.partial(unpack_kernel, device_count, bounds), ou...  2.68 us
    pallas_call x1, Pallas kernels, shards(): pl.pallas_call(scatter_kernel, out_shape=shape((slots, width), F32), in_s...  2.48 us
    unnamed x30, local copies, waits for them, and re-layouts  1.73 us
  transfers between devices with their start and end apart: 14, of which 11 were waited for; matrix products, arithmetic and copies ran while one was open for 0% of the time, Pallas kernels for 11%

profile of v5, /device:TPU:0, one launch (start us, length us, event | category | flops | bytes accessed | tf_op | source)
XLA Modules:
  0.0 80.7 jit_solution(8045036005084106197)
XLA Ops:
  0.6 1.0 %copy-done.5 = bf16[1024,227]{0,1:T(8,128)(2,1)S(1)} copy-done((bf16[1024,227]{0,1:T(8,128)(2,1)S(1)}, bf16[1024,227]{0,1:T(8,128)(2,1)}, u32[]{:S(2)}) %copy-start.5) | copy-done | bytes 464920
  1.7 0.7 copy-done.12
  2.4 0.7 pick_rows.1
  3.1 13.9 %all_to_all.5.feat_in = bf16[16,4,256]{2,1,0:T(4,128)(2,1)S(1)} all-to-all(bf16[16,4,256]{2,1,0:T(4,128)(2,1)S(1)} %pick_rows.1), channel_id=1, replica_groups=mesh['ens'=2,'dom'=16] {'dom'}, dimensions={0} | all-to-all | bytes 65536 | tf_op jit(solution)/shard_map/all_to_all | solution.py:341
  17.1 15.6 %forward_rows.1 = (bf16[512,512]{1,0:T(8,128)(2,1)}, bf16[4096,512]{1,0:T(8,128)(2,1)S(1)}, bf16[1088,512]{1,0:T(8,128)(2,1)S(1)}, bf16[1088,256]{1,0:T(8,128)(2...) custom-call(s32[4]{0:T(128)S(1)} %copy-done.13, ...), custom_call_target="tpu_custom_call" | custom-call | flops 9714008064 | bytes 8388608 | tf_op jit(solution)/shard_map/forward_rows/pallas_call | solution.py:348
  32.8 2.5 %scatter_rows.1.slot_half = f32[1088,512]{1,0:T(8,128)S(1)} custom-call(s32[4,1024]{1,0:T(4,128)S(1)} %copy-done.9, bf16[4096,512]{1,0:T(8,128)(2,1)S(1)} %get-tuple-element.27.pgrad), custom_call_target="tpu_custom_call" | custom-call | flops 2281701376 | bytes 2097152 | tf_op jit(solution)/shard_map/scatter_rows/pallas_call | solution.py:424
  35.3 0.2 convert_add_fusion
  35.5 0.5 collective-permute-start.1
  36.0 4.9 %backward_rows.1 = (f32[384,512]{1,0:T(8,128)S(1)}, bf16[384,512]{1,0:T(8,128)(2,1)S(1)}) custom-call(s32[4,1024]{1,0:T(4,128)S(1)} %copy-done.9, bf16[4096,512]{1,0:T(8,128)(2,1)S(1)} %get-tuple-element.27.pgrad, f32[1088,512]{1,0:T(8,128)S(1)} %scatter_rows.1.slot_half, bf16[1088,512]{1,0:T(8,128)(2,1)S(1)} %get-tuple-element.31.latent, ...), custom_call_target="tpu_custom_call" | custom-call | flops 3992977408 | bytes 2097152 | tf_op jit(solution)/shard_map/backward_rows/pallas_call | solution.py:441
  41.0 1.0 %collective-permute-done.1 = bf16[256,512]{1,0:T(8,128)(2,1)S(1)} collective-permute-done((bf16[256,512]{1,0:T(8,128)(2,1)S(1)}, bf16[256,512]{1,0:T(8,128)(2,1)S(1)}, u32[]{:S(2)}, u32[]{:S(2)}) %collective-permute-start.1) | collective-permute-done | bytes 262176 | tf_op jit(solution)/shard_map/ppermute | solution.py:401
  41.9 1.7 %collective-permute-done.2 = bf16[384,512]{1,0:T(8,128)(2,1)S(1)} collective-permute-done((bf16[384,512]{1,0:T(8,128)(2,1)S(1)}, bf16[384,512]{1,0:T(8,128)(2,1)S(1)}, u32[]{:S(2)}, u32[]{:S(2)}) %collective-permute-start.2) | collective-permute-done | bytes 393248 | tf_op jit(solution)/shard_map/ppermute | solution.py:401
  43.7 0.1 convert_add_fusion.1
  43.8 0.8 collective-permute-start.3
  44.6 0.1 convert_add_fusion.2
  44.7 0.5 collective-permute-start.9
  45.2 5.6 %collective-permute-done.3 = bf16[192,512]{1,0:T(8,128)(2,1)S(1)} collective-permute-done((bf16[192,512]{1,0:T(8,128)(2,1)S(1)}, bf16[192,512]{1,0:T(8,128)(2,1)S(1)}, u32[]{:S(2)}, u32[]{:S(2)}) %collective-permute-start.3) | collective-permute-done | bytes 196640 | tf_op jit(solution)/shard_map/ppermute | solution.py:401
  50.9 0.8 collective-permute-start.4
  51.7 0.6 collective-permute-start.10
  52.3 3.9 %collective-permute-done.4 = bf16[96,512]{1,0:T(8,128)(2,1)S(1)} collective-permute-done((bf16[96,512]{1,0:T(8,128)(2,1)S(1)}, bf16[96,512]{1,0:T(8,128)(2,1)S(1)}, u32[]{:S(2)}, u32[]{:S(2)}) %collective-permute-start.4) | collective-permute-done | bytes 98336 | tf_op jit(solution)/shard_map/ppermute | solution.py:401
  56.2 0.8 %collective-permute-start.5 = (bf16[96,512]{1,0:T(8,128)(2,1)S(1)}, bf16[96,512]{1,0:T(8,128)(2,1)S(1)}, u32[]{:S(2)}, u32[]{:S(2)}) collective-permute-start(bf16[96,512]{1,0:T(8,128)(2,1)S(1)} %fusion.1), channel_id=1, source_target_pairs={{0,8},{1,9},{2,10},{3,11},{4,12},{5,13},{6,14},{7,15},{8,0},{9,1},... | collective-permute-start | bytes 294920 | tf_op jit(solution)/shard_map/ppermute | solution.py:401
  57.0 5.7 %collective-permute-done.10 = bf16[128,512]{1,0:T(8,128)(2,1)S(1)} collective-permute-done((bf16[128,512]{1,0:T(8,128)(2,1)S(1)}, bf16[128,512]{1,0:T(8,128)(2,1)S(1)}, u32[]{:S(2)}, u32[]{:S(2)}) %collective-permute-start.10) | collective-permute-done | bytes 131104 | tf_op jit(solution)/shard_map/ppermute | solution.py:401
  62.8 0.9 %collective-permute-done.5 = bf16[96,512]{1,0:T(8,128)(2,1)S(1)} collective-permute-done((bf16[96,512]{1,0:T(8,128)(2,1)S(1)}, bf16[96,512]{1,0:T(8,128)(2,1)S(1)}, u32[]{:S(2)}, u32[]{:S(2)}) %collective-permute-start.5) | collective-permute-done | bytes 98336 | tf_op jit(solution)/shard_map/ppermute | solution.py:401
  63.8 1.1 %collective-permute-start.6 = (bf16[96,512]{1,0:T(8,128)(2,1)S(1)}, bf16[96,512]{1,0:T(8,128)(2,1)S(1)}, u32[]{:S(2)}, u32[]{:S(2)}) collective-permute-start(bf16[96,512]{1,0:T(8,128)(2,1)S(1)} %add_convert_fusion.1), channel_id=1, source_target_pairs={{0,4},{1,3},{2,6},{3,1},{4,0},{5,7},{6,2},{7,5},{8,12},{9,11},{10,... | collective-permute-start | bytes 294920 | tf_op jit(solution)/shard_map/ppermute | solution.py:401
  64.9 4.2 %collective-permute-done.11 = bf16[128,512]{1,0:T(8,128)(2,1)S(1)} collective-permute-done((bf16[128,512]{1,0:T(8,128)(2,1)S(1)}, bf16[128,512]{1,0:T(8,128)(2,1)S(1)}, u32[]{:S(2)}, u32[]{:S(2)}) %collective-permute-start.11) | collective-permute-done | bytes 131104 | tf_op jit(solution)/shard_map/ppermute | solution.py:401
  69.1 0.8 %collective-permute-start.12 = (bf16[256,512]{1,0:T(8,128)(2,1)S(1)}, bf16[256,512]{1,0:T(8,128)(2,1)S(1)}, u32[]{:S(2)}, u32[]{:S(2)}) collective-permute-start(bf16[256,512]{1,0:T(8,128)(2,1)S(1)} %pad_maximum_fusion.2), channel_id=1, source_target_pairs={{0,2},{1,5},{2,0},{3,7},{4,6},{5,1},{6,4},{7,3},{8,10},{9,13},{10,... | collective-permute-start | bytes 786440 | tf_op jit(solution)/shard_map/ppermute | solution.py:401
  70.0 1.2 %collective-permute-done.6 = bf16[96,512]{1,0:T(8,128)(2,1)S(1)} collective-permute-done((bf16[96,512]{1,0:T(8,128)(2,1)S(1)}, bf16[96,512]{1,0:T(8,128)(2,1)S(1)}, u32[]{:S(2)}, u32[]{:S(2)}) %collective-permute-start.6) | collective-permute-done | bytes 98336 | tf_op jit(solution)/shard_map/ppermute | solution.py:401
  71.2 0.8 %collective-permute-start.7 = (bf16[192,512]{1,0:T(8,128)(2,1)S(1)}, bf16[192,512]{1,0:T(8,128)(2,1)S(1)}, u32[]{:S(2)}, u32[]{:S(2)}) collective-permute-start(bf16[192,512]{1,0:T(8,128)(2,1)S(1)} %pad_maximum_fusion.3), channel_id=1, source_target_pairs={{0,2},{1,5},{2,0},{3,7},{4,6},{5,1},{6,4},{7,3},{8,10},{9,13},{10,... | collective-permute-start | bytes 589832 | tf_op jit(solution)/shard_map/ppermute | solution.py:401
  72.1 3.5 %collective-permute-done.12 = bf16[256,512]{1,0:T(8,128)(2,1)S(1)} collective-permute-done((bf16[256,512]{1,0:T(8,128)(2,1)S(1)}, bf16[256,512]{1,0:T(8,128)(2,1)S(1)}, u32[]{:S(2)}, u32[]{:S(2)}) %collective-permute-start.12) | collective-permute-done | bytes 262176 | tf_op jit(solution)/shard_map/ppermute | solution.py:401
  75.7 2.0 %collective-permute-done.7 = bf16[192,512]{1,0:T(8,128)(2,1)S(1)} collective-permute-done((bf16[192,512]{1,0:T(8,128)(2,1)S(1)}, bf16[192,512]{1,0:T(8,128)(2,1)S(1)}, u32[]{:S(2)}, u32[]{:S(2)}) %collective-permute-start.7) | collective-permute-done | bytes 196640 | tf_op jit(solution)/shard_map/ppermute | solution.py:401
  77.8 1.5 %unpack_rows.3 = (f32[512,512]{1,0:T(8,128)}, f32[512,512]{1,0:T(8,128)}) custom-call(bf16[512,512]{1,0:T(8,128)(2,1)S(1)} %pad_maximum_fusion.held, bf16[512,512]{1,0:T(8,128)(2,1)S(1)} %collective-permute-done.13.got), custom_call_target="tpu_custom_call" | custom-call | tf_op jit(solution)/shard_map/unpack_rows/pallas_call | solution.py:465
  79.3 0.2 collective-permute-done.8.got
  79.5 1.2 %unpack_rows.2 = (f32[512,512]{1,0:T(8,128)}, f32[227,512]{1,0:T(8,128)}, f32[2,512]{1,0:T(2,128)}) custom-call(bf16[384,512]{1,0:T(8,128)(2,1)S(1)} %pad_maximum_fusion.1.held, bf16[384,512]{1,0:T(8,128)(2,1)S(1)} %collective-permute-done.8.got), custom_call_target="tpu_custom_call" | custom-call | tf_op jit(solution)/shard_map/unpack_rows/pallas_call | solution.py:465
  (51 shorter events, 0.6 us)
Async XLA Ops:
  0.6 1.0 %copy-start.5 = (bf16[1024,227]{0,1:T(8,128)(2,1)S(1)}, bf16[1024,227]{0,1:T(8,128)(2,1)}, u32[]{:S(2)}) copy-start(bf16[1024,227]{0,1:T(8,128)(2,1)} %param.13) | copy-start | bytes 1394692
  1.7 0.7 copy-start.12
  2.3 14.7 %copy-start = (bf16[512,512]{1,0:T(8,128)(2,1)S(1)}, bf16[512,512]{1,0:T(8,128)(2,1)}, u32[]{:S(2)}) copy-start(bf16[512,512]{1,0:T(8,128)(2,1)} %w_dst.1) | copy-start | bytes 1572868
  2.3 14.7 %copy-start.1 = (bf16[512,512]{1,0:T(8,128)(2,1)S(1)}, bf16[512,512]{1,0:T(8,128)(2,1)}, u32[]{:S(2)}) copy-start(bf16[512,512]{1,0:T(8,128)(2,1)} %w_out.1) | copy-start | bytes 1572868
  2.3 14.7 %copy-start.2 = (bf16[512,512]{1,0:T(8,128)(2,1)S(1)}, bf16[512,512]{1,0:T(8,128)(2,1)}, u32[]{:S(2)}) copy-start(bf16[512,512]{1,0:T(8,128)(2,1)} %mesh.1) | copy-start | bytes 1572868
  2.3 14.7 %copy-start.3 = (bf16[512,512]{1,0:T(8,128)(2,1)S(1)}, bf16[512,512]{1,0:T(8,128)(2,1)}, u32[]{:S(2)}) copy-start(bf16[512,512]{1,0:T(8,128)(2,1)} %cot.1) | copy-start | bytes 1572868
  2.3 14.7 %copy-start.4 = (bf16[512,512]{1,0:T(8,128)(2,1)S(1)}, bf16[512,512]{1,0:T(8,128)(2,1)}, u32[]{:S(2)}) copy-start(bf16[512,512]{1,0:T(8,128)(2,1)} %w_src.3) | copy-start | bytes 1572868
  2.3 14.7 %copy-start.6 = (bf16[1024,227]{0,1:T(8,128)(2,1)S(1)}, bf16[1024,227]{0,1:T(8,128)(2,1)}, u32[]{:S(2)}) copy-start(bf16[1024,227]{0,1:T(8,128)(2,1)} %param.13) | copy-start | bytes 1394692
  2.3 14.7 %copy-start.7 = (bf16[227,512]{1,0:T(8,128)(2,1)S(1)}, bf16[227,512]{1,0:T(8,128)(2,1)}, u32[]{:S(2)}) copy-start(bf16[227,512]{1,0:T(8,128)(2,1)} %w_embed.1) | copy-start | bytes 697348
  2.4 14.7 %copy-start.8 = (s32[4,1024]{1,0:T(4,128)S(1)}, s32[4,1024]{1,0:T(4,128)}, u32[]{:S(2)}) copy-start(s32[4,1024]{1,0:T(4,128)} %dst.1) | copy-start | bytes 49156
  2.4 14.7 %copy-start.9 = (s32[4,1024]{1,0:T(4,128)S(1)}, s32[4,1024]{1,0:T(4,128)}, u32[]{:S(2)}) copy-start(s32[4,1024]{1,0:T(4,128)} %src.5) | copy-start | bytes 49156
  2.4 14.7 %copy-start.10 = (bf16[512]{0:T(512)(128)(2,1)S(1)}, bf16[512]{0:T(512)(128)(2,1)}, u32[]{:S(2)}) copy-start(bf16[512]{0:T(512)(128)(2,1)} %b_embed.1) | copy-start | bytes 3076
  2.4 14.7 %copy-start.11 = (bf16[512]{0:T(512)(128)(2,1)S(1)}, bf16[512]{0:T(512)(128)(2,1)}, u32[]{:S(2)}) copy-start(bf16[512]{0:T(512)(128)(2,1)} %b_hidden.1) | copy-start | bytes 3076
  2.4 14.7 %copy-start.13 = (s32[4]{0:T(128)S(1)}, s32[4]{0:T(128)}, u32[]{:S(2)}) copy-start(s32[4]{0:T(128)} %count.1) | copy-start | bytes 52
  32.8 2.5 %collective-permute-start = (bf16[512,512]{1,0:T(8,128)(2,1)S(1)}, bf16[512,512]{1,0:T(8,128)(2,1)S(1)}, u32[]{:S(2)}, u32[]{:S(2)}) collective-permute-start(bf16[512,512]{1,0:T(8,128)(2,1)S(1)} %get-tuple-element.29), channel_id=1, source_target_pairs={{0,1},{1,0},{2,3},{3,2},{4,5},{5,4},{6,7},{7,6},{8,9},{9,8},{10,11... | collective-permute-start | bytes 1572872 | tf_op jit(solution)/shard_map/ppermute | solution.py:401
  35.4 5.5 %copy-start.14 = (f32[512,512]{1,0:T(8,128)}, f32[512,512]{1,0:T(8,128)S(1)}, u32[]{:S(2)}) copy-start(f32[512,512]{1,0:T(8,128)S(1)} %convert_add_fusion) | copy-start | bytes 3145732
  35.5 6.4 %collective-permute-start.1 = (bf16[256,512]{1,0:T(8,128)(2,1)S(1)}, bf16[256,512]{1,0:T(8,128)(2,1)S(1)}, u32[]{:S(2)}, u32[]{:S(2)}) collective-permute-start(bf16[256,512]{1,0:T(8,128)(2,1)S(1)} %slice.55), channel_id=1, source_target_pairs={{0,2},{1,5},{2,0},{3,7},{4,6},{5,1},{6,4},{7,3},{8,10},{9,13},{10,... | collective-permute-start | bytes 786440 | tf_op jit(solution)/shard_map/ppermute | solution.py:401
  41.9 2.6 %slice-start = ((f32[512,512]{1,0:T(8,128)}), f32[256,512]{1,0:T(8,128)S(1)}, s32[]{:S(2)}) async-start(f32[512,512]{1,0:T(8,128)} %copy-done.14), calls=%async_computation.1 | async-start | bytes 1048576 | tf_op jit(solution)/shard_map/slice | solution.py:407
  41.9 1.7 %collective-permute-start.2 = (bf16[384,512]{1,0:T(8,128)(2,1)S(1)}, bf16[384,512]{1,0:T(8,128)(2,1)S(1)}, u32[]{:S(2)}, u32[]{:S(2)}) collective-permute-start(bf16[384,512]{1,0:T(8,128)(2,1)S(1)} %get-tuple-element.38), channel_id=1, source_target_pairs={{0,1},{1,0},{2,3},{3,2},{4,5},{5,4},{6,7},{7,6},{8,9},{9,8},{10,11... | collective-permute-start | bytes 1179656 | tf_op jit(solution)/shard_map/ppermute | solution.py:401
  43.8 7.0 %collective-permute-start.3 = (bf16[192,512]{1,0:T(8,128)(2,1)S(1)}, bf16[192,512]{1,0:T(8,128)(2,1)S(1)}, u32[]{:S(2)}, u32[]{:S(2)}) collective-permute-start(bf16[192,512]{1,0:T(8,128)(2,1)S(1)} %slice.56), channel_id=1, source_target_pairs={{0,2},{1,5},{2,0},{3,7},{4,6},{5,1},{6,4},{7,3},{8,10},{9,13},{10,... | collective-permute-start | bytes 589832 | tf_op jit(solution)/shard_map/ppermute | solution.py:401
  44.7 7.0 %collective-permute-start.9 = (bf16[128,512]{1,0:T(8,128)(2,1)S(1)}, bf16[128,512]{1,0:T(8,128)(2,1)S(1)}, u32[]{:S(2)}, u32[]{:S(2)}) collective-permute-start(bf16[128,512]{1,0:T(8,128)(2,1)S(1)} %slice.57), channel_id=1, source_target_pairs={{0,4},{1,3},{2,6},{3,1},{4,0},{5,7},{6,2},{7,5},{8,12},{9,11},{10,... | collective-permute-start | bytes 393224 | tf_op jit(solution)/shard_map/ppermute | solution.py:401
  50.9 5.3 %collective-permute-start.4 = (bf16[96,512]{1,0:T(8,128)(2,1)S(1)}, bf16[96,512]{1,0:T(8,128)(2,1)S(1)}, u32[]{:S(2)}, u32[]{:S(2)}) collective-permute-start(bf16[96,512]{1,0:T(8,128)(2,1)S(1)} %slice.58), channel_id=1, source_target_pairs={{0,4},{1,3},{2,6},{3,1},{4,0},{5,7},{6,2},{7,5},{8,12},{9,11},{10,... | collective-permute-start | bytes 294920 | tf_op jit(solution)/shard_map/ppermute | solution.py:401
  51.7 11.0 %collective-permute-start.10 = (bf16[128,512]{1,0:T(8,128)(2,1)S(1)}, bf16[128,512]{1,0:T(8,128)(2,1)S(1)}, u32[]{:S(2)}, u32[]{:S(2)}) collective-permute-start(bf16[128,512]{1,0:T(8,128)(2,1)S(1)} %fusion), channel_id=1, source_target_pairs={{0,8},{1,9},{2,10},{3,11},{4,12},{5,13},{6,14},{7,15},{8,0},{9,1},... | collective-permute-start | bytes 393224 | tf_op jit(solution)/shard_map/ppermute | solution.py:401
  56.2 7.5 %collective-permute-start.5 = (bf16[96,512]{1,0:T(8,128)(2,1)S(1)}, bf16[96,512]{1,0:T(8,128)(2,1)S(1)}, u32[]{:S(2)}, u32[]{:S(2)}) collective-permute-start(bf16[96,512]{1,0:T(8,128)(2,1)S(1)} %fusion.1), channel_id=1, source_target_pairs={{0,8},{1,9},{2,10},{3,11},{4,12},{5,13},{6,14},{7,15},{8,0},{9,1},... | collective-permute-start | bytes 294920 | tf_op jit(solution)/shard_map/ppermute | solution.py:401
  62.7 6.4 %collective-permute-start.11 = (bf16[128,512]{1,0:T(8,128)(2,1)S(1)}, bf16[128,512]{1,0:T(8,128)(2,1)S(1)}, u32[]{:S(2)}, u32[]{:S(2)}) collective-permute-start(bf16[128,512]{1,0:T(8,128)(2,1)S(1)} %add_convert_fusion), channel_id=1, source_target_pairs={{0,4},{1,3},{2,6},{3,1},{4,0},{5,7},{6,2},{7,5},{8,12},{9,11},{10,... | collective-permute-start | bytes 393224 | tf_op jit(solution)/shard_map/ppermute | solution.py:401
  63.8 7.5 %collective-permute-start.6 = (bf16[96,512]{1,0:T(8,128)(2,1)S(1)}, bf16[96,512]{1,0:T(8,128)(2,1)S(1)}, u32[]{:S(2)}, u32[]{:S(2)}) collective-permute-start(bf16[96,512]{1,0:T(8,128)(2,1)S(1)} %add_convert_fusion.1), channel_id=1, source_target_pairs={{0,4},{1,3},{2,6},{3,1},{4,0},{5,7},{6,2},{7,5},{8,12},{9,11},{10,... | collective-permute-start | bytes 294920 | tf_op jit(solution)/shard_map/ppermute | solution.py:401
  69.1 6.4 %collective-permute-start.12 = (bf16[256,512]{1,0:T(8,128)(2,1)S(1)}, bf16[256,512]{1,0:T(8,128)(2,1)S(1)}, u32[]{:S(2)}, u32[]{:S(2)}) collective-permute-start(bf16[256,512]{1,0:T(8,128)(2,1)S(1)} %pad_maximum_fusion.2), channel_id=1, source_target_pairs={{0,2},{1,5},{2,0},{3,7},{4,6},{5,1},{6,4},{7,3},{8,10},{9,13},{10,... | collective-permute-start | bytes 786440 | tf_op jit(solution)/shard_map/ppermute | solution.py:401
  71.2 6.4 %collective-permute-start.7 = (bf16[192,512]{1,0:T(8,128)(2,1)S(1)}, bf16[192,512]{1,0:T(8,128)(2,1)S(1)}, u32[]{:S(2)}, u32[]{:S(2)}) collective-permute-start(bf16[192,512]{1,0:T(8,128)(2,1)S(1)} %pad_maximum_fusion.3), channel_id=1, source_target_pairs={{0,2},{1,5},{2,0},{3,7},{4,6},{5,1},{6,4},{7,3},{8,10},{9,13},{10,... | collective-permute-start | bytes 589832 | tf_op jit(solution)/shard_map/ppermute | solution.py:401
  75.6 2.2 %collective-permute-start.13 = (bf16[512,512]{1,0:T(8,128)(2,1)S(1)}, bf16[512,512]{1,0:T(8,128)(2,1)S(1)}, u32[]{:S(2)}, u32[]{:S(2)}) collective-permute-start(bf16[512,512]{1,0:T(8,128)(2,1)S(1)} %pad_maximum_fusion.held), channel_id=1, source_target_pairs={{0,1},{1,0},{2,3},{3,2},{4,5},{5,4},{6,7},{7,6},{8,9},{9,8},{10,11... | collective-permute-start | bytes 1572872 | tf_op jit(solution)/shard_map/ppermute | solution.py:401
  77.7 1.8 %collective-permute-start.8 = (bf16[384,512]{1,0:T(8,128)(2,1)S(1)}, bf16[384,512]{1,0:T(8,128)(2,1)S(1)}, u32[]{:S(2)}, u32[]{:S(2)}) collective-permute-start(bf16[384,512]{1,0:T(8,128)(2,1)S(1)} %pad_maximum_fusion.1.held), channel_id=1, source_target_pairs={{0,1},{1,0},{2,3},{3,2},{4,5},{5,4},{6,7},{7,6},{8,9},{9,8},{10,11... | collective-permute-start | bytes 1179656 | tf_op jit(solution)/shard_map/ppermute | solution.py:401

commit v6 on v5

--- a/solution.py
+++ b/solution.py
@@ -19,6 +19,10 @@
 
 def sigmoid(values):
     return 0.5 * jnp.tanh(0.5 * values) + 0.5
+
+
+def halved(values):
+    return (0.5 * values.astype(F32)).astype(BF16)
 
 
 def round_up(value, step):
@@ -62,15 +66,15 @@
     return mask
 
 
-def place(device_count):
+def place(device_count, turn):
     me = lax.axis_index("dom")
-    first, second, _ = stage_bits(device_count)
-    masks = position_mask(me, first), position_mask(me, second)
-    return lax.rem(me, 2), masks, 1 << len(first)
-
-
-def split_pieces(device_count, grads, kept, sent):
-    core, masks, pieces = place(device_count)
+    orders = stage_bits(device_count)[:2]
+    masks = position_mask(me, orders[turn]), position_mask(me, orders[1 - turn])
+    return lax.rem(me, 2), masks, 1 << len(orders[0])
+
+
+def split_pieces(device_count, turn, grads, kept, sent):
+    core, masks, pieces = place(device_count, turn)
     mine = jnp.where(core == 0, masks[0], masks[1])
     theirs = jnp.where(core == 0, masks[1], masks[0])
     piece = kept.shape[0] // pieces
@@ -96,7 +100,7 @@
     w_out,
     mesh,
     cot,
-    mesh_out,
+    hid_sum,
     pgrad,
     latent,
     feat,
@@ -115,7 +119,6 @@
     near,
     back,
     node_sum,
-    hid_sum,
     grads,
 ):
     channels, own = feat_t.shape
@@ -146,15 +149,15 @@
         pre = mm(feat[r:end, :], w_pad[...])
         lat = (pre * sigmoid(pre)).astype(BF16)
         latent[r:end, :] = lat
-        table[block + r : block + end, :] = mm(lat, w_src[...]).astype(BF16)
-    near[...] = mm(mesh[...], w_dst[...]).astype(BF16)
-    full = mm(cot[...], w_out[...], 1, 1)
+        table[block + r : block + end, :] = halved(mm(lat, w_src[...]).astype(BF16))
+    near[...] = halved(mm(mesh[...], w_dst[...]).astype(BF16))
+    full = 0.5 * mm(cot[...], w_out[...], 1, 1)
     high = full.astype(BF16)
     back[0] = high
     back[1] = (full - high.astype(F32)).astype(BF16)
     tail = depth - slots - block
     tail_row = lax.broadcasted_iota(jnp.int32, (tail, width), 0)
-    bias_row = b_hidden[...].astype(F32).reshape(1, width)
+    bias_row = 0.5 * b_hidden[...].astype(F32).reshape(1, width)
     table[slots + block : depth, :] = jnp.where(
         tail_row == 0, jnp.broadcast_to(bias_row, (tail, width)), 0.0
     ).astype(BF16)
@@ -168,6 +171,7 @@
     dst_all = jnp.where(edge_lane < counts, dst[...], -1)
     columns = jnp.transpose(jnp.concatenate([src_all, dst_all], axis=0))
     bias_total = jnp.zeros((1, width), F32)
+    one, none = jnp.ones((), BF16), jnp.zeros((), BF16)
 
     for b in range(blocks):
         rows = slice(b * block, (b + 1) * block)
@@ -178,24 +182,27 @@
         for e in range(0, edges, step):
             src_col = columns[e : e + step, b : b + 1]
             dst_col = columns[e : e + step, blocks + b : blocks + b + 1]
-            lane = lax.broadcasted_iota(jnp.int32, (step, block), 1)
-            near_hot = jnp.where(lane == dst_col, 1.0, 0.0).astype(BF16)
+            src_wide = jnp.broadcast_to(src_col, (step, 128)).astype(jnp.int16)
+            dst_wide = jnp.broadcast_to(dst_col, (step, block)).astype(jnp.int16)
+            lane = lax.broadcasted_iota(jnp.int16, (step, block), 1)
+            near_hot = jnp.where(lane == dst_wide, one, none)
             one_hot[e : e + step, 0:block] = near_hot
             one_hot[e : e + step, block : 2 * block] = near_hot
             for k in range(0, depth - block, 128):
-                lane = lax.broadcasted_iota(jnp.int32, (step, 128), 1) + k
-                hot = lane == src_col
+                lane = lax.broadcasted_iota(jnp.int16, (step, 128), 1) + jnp.int16(k)
+                hot = lane == src_wide
                 if k <= slots < k + 128:
-                    hot = hot | (lane == slots)
-                hot = jnp.where(hot, 1.0, 0.0).astype(BF16)
+                    hot = hot | (lane == jnp.int16(slots))
+                hot = jnp.where(hot, one, none)
                 one_hot[e : e + step, 2 * block + k : 2 * block + k + 128] = hot
             pre = mm(one_hot[e : e + step, block : block + depth], table[...])
             grad = mm(one_hot[e : e + step, 0 : 2 * block], pair[...])
-            sig = sigmoid(pre)
-            act = pre * sig
+            bent = jnp.tanh(pre)
+            rise = 1.0 + bent
+            act = pre * rise
             hid[e : e + step, :] = act.astype(BF16)
             at = slice(b * edges + e, b * edges + e + step)
-            pgrad[at, :] = (grad * (sig + act * (1.0 - sig))).astype(BF16)
+            pgrad[at, :] = (grad * (rise + act * (1.0 - bent))).astype(BF16)
         sub = lax.broadcasted_iota(jnp.int32, (block, edges), 0)
         one_hot_t[...] = jnp.where(sub == dst_row, 1.0, 0.0).astype(BF16)
         node = mm(one_hot_t[...], pgrad[b * edges : (b + 1) * edges, :])
@@ -204,24 +211,26 @@
         hid_sum[rows, :] = mm(one_hot_t[...], hid[...]).astype(BF16)
 
     bias_sum[...] = jnp.broadcast_to(bias_total, bias_sum.shape)
-    total = hid_sum[...]
-    mesh_out[...] = (mesh[...].astype(F32) + mm(total, w_out[...])).astype(BF16)
-    grads[0:width, :] = mm(total, cot[...], 0, 0)
+    grads[0:width, :] = mm(hid_sum[...], cot[...], 0, 0)
     grads[width : 2 * width, :] = mm(mesh[...], node_sum[...], 0, 0)
-    split_pieces(device_count, grads, kept, sent)
+    split_pieces(device_count, 0, grads, kept, sent)
+
+
+def mesh_kernel(mesh, hid_sum, w_out, mesh_out):
+    mesh_out[...] = (mesh[...].astype(F32) + mm(hid_sum[...], w_out[...])).astype(BF16)
 
 
 def scatter_rows(src, pgrad, one_hot_t, first_block, block_count):
     edges = src.shape[1]
     slots = one_hot_t.shape[0]
-    parts = []
+    one, none = jnp.ones((), BF16), jnp.zeros((), BF16)
     for b in range(first_block, first_block + block_count):
         at = slice((b - first_block) * edges, (b - first_block + 1) * edges)
         for r in range(0, slots, 128):
             size = min(128, slots - r)
-            sub = lax.broadcasted_iota(jnp.int32, (size, edges), 0) + r
-            hot = jnp.where(sub == src[b : b + 1, :], 1.0, 0.0).astype(BF16)
-            one_hot_t[r : r + size, at] = hot
+            sub = lax.broadcasted_iota(jnp.int16, (size, edges), 0) + jnp.int16(r)
+            row = jnp.broadcast_to(src[b : b + 1, :], (size, edges)).astype(jnp.int16)
+            one_hot_t[r : r + size, at] = jnp.where(sub == row, one, none)
     rows = slice(first_block * edges, (first_block + block_count) * edges)
     return mm(one_hot_t[...], pgrad[rows, :])
 
@@ -262,11 +271,11 @@
     if grads.shape[0] > width + padded:
         spare = grads.shape[0] - width - padded
         grads[width + padded :, :] = jnp.zeros((spare, width), F32)
-    split_pieces(device_count, grads, kept, sent)
-
-
-def unpack_kernel(device_count, bounds, held, got, *targets):
-    core, masks, pieces = place(device_count)
+    split_pieces(device_count, 1, grads, kept, sent)
+
+
+def unpack_kernel(device_count, turn, bounds, held, got, *targets):
+    core, masks, pieces = place(device_count, turn)
     piece = held.shape[0] // pieces
     used = bounds[-1][1]
     for c in range(2 * pieces):
@@ -314,7 +323,7 @@
     mesh_rows = round_up(2 * width, 32 * pieces)
     grid_rows = round_up(width + padded, 32 * pieces)
     half_blocks = blocks // 2
-    stages = list(zip(first, second))
+    stages = list(zip(first, second)), list(zip(second, first))
 
     vmem = pl.BlockSpec(memory_space=pltpu.VMEM)
     smem = pl.BlockSpec(memory_space=pltpu.SMEM)
@@ -345,7 +354,7 @@
         + blocks * edges * width * (depth + 4 * block)
         + 5 * nodes * width * width
     )
-    mesh_out, pgrad, latent, feat, w_pad, bias_sum, kept_mesh, sent_mesh = pl.pallas_call(
+    hid_sum, pgrad, latent, feat, w_pad, bias_sum, kept_mesh, sent_mesh = pl.pallas_call(
         functools.partial(forward_kernel, device_count),
         out_shape=(
             shape((nodes, width), BF16),
@@ -370,7 +379,6 @@
             pltpu.VMEM((edges, width), BF16),
             pltpu.VMEM((nodes, width), BF16),
             pltpu.VMEM((2, nodes, width), BF16),
-            pltpu.VMEM((nodes, width), BF16),
             pltpu.VMEM((nodes, width), BF16),
             pltpu.VMEM((mesh_rows, width), F32),
         ],
@@ -409,14 +417,14 @@
     def pair_sum(kept, sent):
         return cut(kept + swap(sent, (0, 0)).astype(F32))
 
-    def reduce_pieces(held, got):
-        for bits in stages[1:]:
+    def reduce_pieces(turn, held, got, done=1):
+        for bits in stages[turn][done:]:
             held, sent = cut(held + got.astype(F32))
             got = swap(sent, bits)
         held = (held + got.astype(F32)).astype(BF16)
         got = swap(held, (last_bit, last_bit))
         held = (held.astype(F32) + got.astype(F32)).astype(BF16)
-        for bits in reversed(stages):
+        for bits in reversed(stages[turn]):
             held = jnp.concatenate([held, swap(held, bits)], axis=0)
         return held, swap(held, (0, 0))
 
@@ -437,7 +445,7 @@
     )(edge_src, pgrad)
 
     slot_half, held_mesh, next_mesh = lax.optimization_barrier((slot_half, held_mesh, next_mesh))
-    got_mesh = swap(next_mesh, stages[0])
+    got_mesh = swap(next_mesh, stages[0][0])
     kept_grid, sent_grid = pl.pallas_call(
         functools.partial(backward_kernel, channels, device_count),
         out_shape=(
@@ -461,9 +469,21 @@
 
     sent_grid, got_mesh = lax.optimization_barrier((sent_grid, got_mesh))
 
-    def unpack(pair, bounds):
+    mesh_out = pl.pallas_call(
+        mesh_kernel,
+        out_shape=shape((nodes, width), BF16),
+        in_specs=[vmem] * 3,
+        out_specs=vmem,
+        compiler_params=limit(16),
+        cost_estimate=pl.CostEstimate(
+            flops=2 * nodes * width * width, bytes_accessed=8 * nodes * width, transcendentals=0
+        ),
+        name="mesh_rows",
+    )(mesh_latent, hid_sum, w_out)
+
+    def unpack(turn, pair, bounds):
         return pl.pallas_call(
-            functools.partial(unpack_kernel, device_count, bounds),
+            functools.partial(unpack_kernel, device_count, turn, bounds),
             out_shape=tuple(shape((high - low, width), F32) for low, high in bounds),
             in_specs=[vmem] * 2,
             out_specs=(vmem,) * len(bounds),
@@ -471,12 +491,13 @@
             name="unpack_rows",
         )(*pair)
 
-    mesh_pair = reduce_pieces(held_mesh, got_mesh)
+    mesh_pair = reduce_pieces(0, held_mesh, got_mesh)
     held_grid, next_grid = pair_sum(kept_grid, sent_grid)
-    grid_pair = reduce_pieces(held_grid, swap(next_grid, stages[0]))
-    grad_out, grad_dst = unpack(mesh_pair, ((0, width), (width, 2 * width)))
+    mesh_out, next_grid = lax.optimization_barrier((mesh_out, next_grid))
+    grid_pair = reduce_pieces(1, held_grid, swap(next_grid, stages[1][0]))
+    grad_out, grad_dst = unpack(0, mesh_pair, ((0, width), (width, 2 * width)))
     end = width + channels
-    grad_src, grad_embed, biases = unpack(grid_pair, ((0, width), (width, end), (end, end + 2)))
+    grad_src, grad_embed, biases = unpack(1, grid_pair, ((0, width), (width, end), (end, end + 2)))
     return mesh_out, grad_embed, grad_src, grad_dst, grad_out, biases
 
 

time: 80.9 us -> 79.2 us (0.979)
  waiting for transfers between devices: 29.9 us -> 28.3 us
    pallas_call x1, Pallas kernels: 15.6 us -> 14 us  [shards(): pl.pallas_call(functools.partial(forward_kernel, device_count), out_shape...]
    ppermute x14, waiting for transfers between devices: 29.9 us -> 28.3 us  [swap(): lax.ppermute(values, 'dom', [(d, d ^ 1 << bits[d % 2]) for d in range(dev...]
    pallas_call x2 -> x3, Pallas kernels: 2.68 us -> 3.9 us  [the longest x2 2.66 us: unpack(): pl.pallas_call(functools.partial(unpack_kernel, device_count, turn, bound...]
  transfers between devices with their start and end apart: 14 -> 14, of which waited for: 11 -> 10; matrix products, arithmetic and copies ran while one was open for 0% -> 0% of each run, Pallas kernels for 11% -> 13%
where the time goes in v6:
time: 79.2 us; the launch traced here: 79 us
  waiting for transfers between devices  28.3 us (36%)
  Pallas kernels  26.2 us (33%)
  blocking collectives  13.9 us (18%)
  starting transfers between devices  7.19 us (9%)
  local copies, waits for them, and re-layouts  1.83 us (2%)
  between operations  0.99 us (1%)
    ppermute x14, waiting for transfers between devices, swap(): lax.ppermute(values, 'dom', [(d, d ^ 1 << bits[d % 2]) for d in range(dev...  28.3 us
    pallas_call x1, Pallas kernels, shards(): pl.pallas_call(functools.partial(forward_kernel, device_count), out_shape...  14 us
    all_to_all x1, blocking collectives, shards(): lax.all_to_all(send, 'dom', split_axis=0, concat_axis=0, tiled=True)  13.9 us
    ppermute x14, starting transfers between devices, swap(): lax.ppermute(values, 'dom', [(d, d ^ 1 << bits[d % 2]) for d in range(dev...  7.19 us
    pallas_call x1, Pallas kernels, shards(): pl.pallas_call(functools.partial(backward_kernel, channels, device_count)...  4.95 us
    pallas_call x1, Pallas kernels, shards(): pl.pallas_call(scatter_kernel, out_shape=shape((slots, width), F32), in_s...  2.68 us
    pallas_call x2, Pallas kernels, unpack(): pl.pallas_call(functools.partial(unpack_kernel, device_count, turn, bound...  2.66 us
    unnamed x30, local copies, waits for them, and re-layouts  1.73 us
  transfers between devices with their start and end apart: 14, of which 10 were waited for; matrix products, arithmetic and copies ran while one was open for 0% of the time, Pallas kernels for 13%

profile of v6, /device:TPU:0, one launch (start us, length us, event | category | flops | bytes accessed | tf_op | source)
XLA Modules:
  0.0 79.0 jit_solution(10289537749346191357)
XLA Ops:
  0.6 1.0 %copy-done.5 = bf16[1024,227]{0,1:T(8,128)(2,1)S(1)} copy-done((bf16[1024,227]{0,1:T(8,128)(2,1)S(1)}, bf16[1024,227]{0,1:T(8,128)(2,1)}, u32[]{:S(2)}) %copy-start.5) | copy-done | bytes 464920
  1.7 0.7 copy-done.12
  2.4 0.7 pick_rows.1
  3.1 13.9 %all_to_all.5.feat_in = bf16[16,4,256]{2,1,0:T(4,128)(2,1)S(1)} all-to-all(bf16[16,4,256]{2,1,0:T(4,128)(2,1)S(1)} %pick_rows.1), channel_id=1, replica_groups=mesh['ens'=2,'dom'=16] {'dom'}, dimensions={0} | all-to-all | bytes 65536 | tf_op jit(solution)/shard_map/all_to_all | solution.py:350
  17.1 14.0 %forward_rows.1 = (bf16[512,512]{1,0:T(8,128)(2,1)S(1)}, bf16[4096,512]{1,0:T(8,128)(2,1)S(1)}, bf16[1088,512]{1,0:T(8,128)(2,1)S(1)}, bf16[1088,256]{1,0:T(8,12...) custom-call(s32[4]{0:T(128)S(1)} %copy-done.13, ...), custom_call_target="tpu_custom_call" | custom-call | flops 9714008064 | bytes 8388608 | tf_op jit(solution)/shard_map/forward_rows/pallas_call | solution.py:357
  31.2 2.7 %scatter_rows.1.slot_half = f32[1088,512]{1,0:T(8,128)S(1)} custom-call(s32[4,1024]{1,0:T(4,128)S(1)} %copy-done.9, bf16[4096,512]{1,0:T(8,128)(2,1)S(1)} %get-tuple-element.29.pgrad), custom_call_target="tpu_custom_call" | custom-call | flops 2281701376 | bytes 2097152 | tf_op jit(solution)/shard_map/scatter_rows/pallas_call | solution.py:432
  33.9 0.2 convert_add_fusion
  34.1 0.5 collective-permute-start.1
  34.6 4.9 %backward_rows.1 = (f32[384,512]{1,0:T(8,128)S(1)}, bf16[384,512]{1,0:T(8,128)(2,1)S(1)}) custom-call(s32[4,1024]{1,0:T(4,128)S(1)} %copy-done.9, bf16[4096,512]{1,0:T(8,128)(2,1)S(1)} %get-tuple-element.29.pgrad, f32[1088,512]{1,0:T(8,128)S(1)} %scatter_rows.1.slot_half, bf16[1088,512]{1,0:T(8,128)(2,1)S(1)} %get-tuple-element.33.latent, ...), custom_call_target="tpu_custom_call" | custom-call | flops 3992977408 | bytes 2097152 | tf_op jit(solution)/shard_map/backward_rows/pallas_call | solution.py:449
  39.6 1.0 %collective-permute-done.1 = bf16[256,512]{1,0:T(8,128)(2,1)S(1)} collective-permute-done((bf16[256,512]{1,0:T(8,128)(2,1)S(1)}, bf16[256,512]{1,0:T(8,128)(2,1)S(1)}, u32[]{:S(2)}, u32[]{:S(2)}) %collective-permute-start.1) | collective-permute-done | bytes 262176 | tf_op jit(solution)/shard_map/ppermute | solution.py:409
  40.6 1.2 %mesh_rows.1 = bf16[512,512]{1,0:T(8,128)(2,1)} custom-call(bf16[512,512]{1,0:T(8,128)(2,1)S(1)} %copy-done, bf16[512,512]{1,0:T(8,128)(2,1)S(1)} %get-tuple-element.28.hid_sum, bf16[512,512]{1,0:T(8,128)(2,1)S(1)} %copy-done.1), custom_call_target="tpu_custom_call" | custom-call | flops 268435456 | bytes 2097152 | tf_op jit(solution)/shard_map/mesh_rows/pallas_call | solution.py:472
  41.8 0.5 collective-permute-done.2
  42.3 0.1 convert_add_fusion.1
  42.4 0.6 collective-permute-start.3
  43.0 0.1 convert_add_fusion.2
  43.1 1.6 %collective-permute-start.9 = (bf16[128,512]{1,0:T(8,128)(2,1)S(1)}, bf16[128,512]{1,0:T(8,128)(2,1)S(1)}, u32[]{:S(2)}, u32[]{:S(2)}) collective-permute-start(bf16[128,512]{1,0:T(8,128)(2,1)S(1)} %slice.57), channel_id=1, source_target_pairs={{0,4},{1,3},{2,6},{3,1},{4,0},{5,7},{6,2},{7,5},{8,12},{9,11},{10,... | collective-permute-start | bytes 393224 | tf_op jit(solution)/shard_map/ppermute | solution.py:409
  44.7 3.5 %collective-permute-done.3 = bf16[192,512]{1,0:T(8,128)(2,1)S(1)} collective-permute-done((bf16[192,512]{1,0:T(8,128)(2,1)S(1)}, bf16[192,512]{1,0:T(8,128)(2,1)S(1)}, u32[]{:S(2)}, u32[]{:S(2)}) %collective-permute-start.3) | collective-permute-done | bytes 196640 | tf_op jit(solution)/shard_map/ppermute | solution.py:409
  48.2 0.8 collective-permute-start.4
  49.0 0.6 collective-permute-done.9
  49.6 0.6 collective-permute-start.10
  50.2 2.8 %collective-permute-done.4 = bf16[96,512]{1,0:T(8,128)(2,1)S(1)} collective-permute-done((bf16[96,512]{1,0:T(8,128)(2,1)S(1)}, bf16[96,512]{1,0:T(8,128)(2,1)S(1)}, u32[]{:S(2)}, u32[]{:S(2)}) %collective-permute-start.4) | collective-permute-done | bytes 98336 | tf_op jit(solution)/shard_map/ppermute | solution.py:409
  52.9 0.6 collective-permute-start.5
  53.5 7.0 %collective-permute-done.10 = bf16[128,512]{1,0:T(8,128)(2,1)S(1)} collective-permute-done((bf16[128,512]{1,0:T(8,128)(2,1)S(1)}, bf16[128,512]{1,0:T(8,128)(2,1)S(1)}, u32[]{:S(2)}, u32[]{:S(2)}) %collective-permute-start.10) | collective-permute-done | bytes 131104 | tf_op jit(solution)/shard_map/ppermute | solution.py:409
  60.6 1.7 %collective-permute-done.5 = bf16[96,512]{1,0:T(8,128)(2,1)S(1)} collective-permute-done((bf16[96,512]{1,0:T(8,128)(2,1)S(1)}, bf16[96,512]{1,0:T(8,128)(2,1)S(1)}, u32[]{:S(2)}, u32[]{:S(2)}) %collective-permute-start.5) | collective-permute-done | bytes 98336 | tf_op jit(solution)/shard_map/ppermute | solution.py:409
  62.3 0.7 collective-permute-start.6
  63.0 3.4 %collective-permute-done.11 = bf16[128,512]{1,0:T(8,128)(2,1)S(1)} collective-permute-done((bf16[128,512]{1,0:T(8,128)(2,1)S(1)}, bf16[128,512]{1,0:T(8,128)(2,1)S(1)}, u32[]{:S(2)}, u32[]{:S(2)}) %collective-permute-start.11) | collective-permute-done | bytes 131104 | tf_op jit(solution)/shard_map/ppermute | solution.py:409
  66.4 1.1 %collective-permute-start.12 = (bf16[256,512]{1,0:T(8,128)(2,1)S(1)}, bf16[256,512]{1,0:T(8,128)(2,1)S(1)}, u32[]{:S(2)}, u32[]{:S(2)}) collective-permute-start(bf16[256,512]{1,0:T(8,128)(2,1)S(1)} %pad_maximum_fusion.2), channel_id=1, source_target_pairs={{0,2},{1,5},{2,0},{3,7},{4,6},{5,1},{6,4},{7,3},{8,10},{9,13},{10,... | collective-permute-start | bytes 786440 | tf_op jit(solution)/shard_map/ppermute | solution.py:409
  67.6 6.7 %collective-permute-done.12 = bf16[256,512]{1,0:T(8,128)(2,1)S(1)} collective-permute-done((bf16[256,512]{1,0:T(8,128)(2,1)S(1)}, bf16[256,512]{1,0:T(8,128)(2,1)S(1)}, u32[]{:S(2)}, u32[]{:S(2)}) %collective-permute-start.12) | collective-permute-done | bytes 262176 | tf_op jit(solution)/shard_map/ppermute | solution.py:409
  74.5 0.5 collective-permute-start.8
  75.0 1.3 %collective-permute-done.13.got = bf16[512,512]{1,0:T(8,128)(2,1)S(1)} collective-permute-done((bf16[512,512]{1,0:T(8,128)(2,1)S(1)}, bf16[512,512]{1,0:T(8,128)(2,1)S(1)}, u32[]{:S(2)}, u32[]{:S(2)}) %collective-permute-start.13) | collective-permute-done | bytes 524320 | tf_op jit(solution)/shard_map/ppermute | solution.py:409
  76.3 1.4 %unpack_rows.3 = (f32[512,512]{1,0:T(8,128)}, f32[512,512]{1,0:T(8,128)}) custom-call(bf16[512,512]{1,0:T(8,128)(2,1)S(1)} %pad_maximum_fusion.held, bf16[512,512]{1,0:T(8,128)(2,1)S(1)} %collective-permute-done.13.got), custom_call_target="tpu_custom_call" | custom-call | tf_op jit(solution)/shard_map/unpack_rows/pallas_call | solution.py:485
  77.8 1.2 %unpack_rows.2 = (f32[512,512]{1,0:T(8,128)}, f32[227,512]{1,0:T(8,128)}, f32[2,512]{1,0:T(2,128)}) custom-call(bf16[384,512]{1,0:T(8,128)(2,1)S(1)} %pad_maximum_fusion.1.held, bf16[384,512]{1,0:T(8,128)(2,1)S(1)} %collective-permute-done.8.got), custom_call_target="tpu_custom_call" | custom-call | tf_op jit(solution)/shard_map/unpack_rows/pallas_call | solution.py:485
  (52 shorter events, 0.7 us)
Async XLA Ops:
  0.6 1.0 %copy-start.5 = (bf16[1024,227]{0,1:T(8,128)(2,1)S(1)}, bf16[1024,227]{0,1:T(8,128)(2,1)}, u32[]{:S(2)}) copy-start(bf16[1024,227]{0,1:T(8,128)(2,1)} %param.13) | copy-start | bytes 1394692
  1.7 0.7 copy-start.12
  2.3 14.7 %copy-start = (bf16[512,512]{1,0:T(8,128)(2,1)S(1)}, bf16[512,512]{1,0:T(8,128)(2,1)}, u32[]{:S(2)}) copy-start(bf16[512,512]{1,0:T(8,128)(2,1)} %mesh.3) | copy-start | bytes 1572868
  2.3 14.7 %copy-start.1 = (bf16[512,512]{1,0:T(8,128)(2,1)S(1)}, bf16[512,512]{1,0:T(8,128)(2,1)}, u32[]{:S(2)}) copy-start(bf16[512,512]{1,0:T(8,128)(2,1)} %w_out.3) | copy-start | bytes 1572868
  2.3 14.7 %copy-start.2 = (bf16[512,512]{1,0:T(8,128)(2,1)S(1)}, bf16[512,512]{1,0:T(8,128)(2,1)}, u32[]{:S(2)}) copy-start(bf16[512,512]{1,0:T(8,128)(2,1)} %w_dst.1) | copy-start | bytes 1572868
  2.3 14.7 %copy-start.3 = (bf16[512,512]{1,0:T(8,128)(2,1)S(1)}, bf16[512,512]{1,0:T(8,128)(2,1)}, u32[]{:S(2)}) copy-start(bf16[512,512]{1,0:T(8,128)(2,1)} %cot.1) | copy-start | bytes 1572868
  2.3 14.7 %copy-start.4 = (bf16[512,512]{1,0:T(8,128)(2,1)S(1)}, bf16[512,512]{1,0:T(8,128)(2,1)}, u32[]{:S(2)}) copy-start(bf16[512,512]{1,0:T(8,128)(2,1)} %w_src.3) | copy-start | bytes 1572868
  2.3 14.7 %copy-start.6 = (bf16[1024,227]{0,1:T(8,128)(2,1)S(1)}, bf16[1024,227]{0,1:T(8,128)(2,1)}, u32[]{:S(2)}) copy-start(bf16[1024,227]{0,1:T(8,128)(2,1)} %param.13) | copy-start | bytes 1394692
  2.3 14.7 %copy-start.7 = (bf16[227,512]{1,0:T(8,128)(2,1)S(1)}, bf16[227,512]{1,0:T(8,128)(2,1)}, u32[]{:S(2)}) copy-start(bf16[227,512]{1,0:T(8,128)(2,1)} %w_embed.1) | copy-start | bytes 697348
  2.4 14.7 %copy-start.8 = (s32[4,1024]{1,0:T(4,128)S(1)}, s32[4,1024]{1,0:T(4,128)}, u32[]{:S(2)}) copy-start(s32[4,1024]{1,0:T(4,128)} %dst.1) | copy-start | bytes 49156
  2.4 14.7 %copy-start.9 = (s32[4,1024]{1,0:T(4,128)S(1)}, s32[4,1024]{1,0:T(4,128)}, u32[]{:S(2)}) copy-start(s32[4,1024]{1,0:T(4,128)} %src.5) | copy-start | bytes 49156
  2.4 14.7 %copy-start.10 = (bf16[512]{0:T(512)(128)(2,1)S(1)}, bf16[512]{0:T(512)(128)(2,1)}, u32[]{:S(2)}) copy-start(bf16[512]{0:T(512)(128)(2,1)} %b_embed.1) | copy-start | bytes 3076
  2.4 14.7 %copy-start.11 = (bf16[512]{0:T(512)(128)(2,1)S(1)}, bf16[512]{0:T(512)(128)(2,1)}, u32[]{:S(2)}) copy-start(bf16[512]{0:T(512)(128)(2,1)} %b_hidden.1) | copy-start | bytes 3076
  2.4 14.7 %copy-start.13 = (s32[4]{0:T(128)S(1)}, s32[4]{0:T(128)}, u32[]{:S(2)}) copy-start(s32[4]{0:T(128)} %count.1) | copy-start | bytes 52
  31.1 2.8 %collective-permute-start = (bf16[512,512]{1,0:T(8,128)(2,1)S(1)}, bf16[512,512]{1,0:T(8,128)(2,1)S(1)}, u32[]{:S(2)}, u32[]{:S(2)}) collective-permute-start(bf16[512,512]{1,0:T(8,128)(2,1)S(1)} %get-tuple-element.31), channel_id=1, source_target_pairs={{0,1},{1,0},{2,3},{3,2},{4,5},{5,4},{6,7},{7,6},{8,9},{9,8},{10,11... | collective-permute-start | bytes 1572872 | tf_op jit(solution)/shard_map/ppermute | solution.py:409
  34.1 5.5 %copy-start.14 = (f32[512,512]{1,0:T(8,128)}, f32[512,512]{1,0:T(8,128)S(1)}, u32[]{:S(2)}) copy-start(f32[512,512]{1,0:T(8,128)S(1)} %convert_add_fusion) | copy-start | bytes 3145732
  34.1 6.4 %collective-permute-start.1 = (bf16[256,512]{1,0:T(8,128)(2,1)S(1)}, bf16[256,512]{1,0:T(8,128)(2,1)S(1)}, u32[]{:S(2)}, u32[]{:S(2)}) collective-permute-start(bf16[256,512]{1,0:T(8,128)(2,1)S(1)} %slice.55), channel_id=1, source_target_pairs={{0,2},{1,5},{2,0},{3,7},{4,6},{5,1},{6,4},{7,3},{8,10},{9,13},{10,... | collective-permute-start | bytes 786440 | tf_op jit(solution)/shard_map/ppermute | solution.py:409
  40.5 1.7 %collective-permute-start.2 = (bf16[384,512]{1,0:T(8,128)(2,1)S(1)}, bf16[384,512]{1,0:T(8,128)(2,1)S(1)}, u32[]{:S(2)}, u32[]{:S(2)}) collective-permute-start(bf16[384,512]{1,0:T(8,128)(2,1)S(1)} %get-tuple-element.40), channel_id=1, source_target_pairs={{0,1},{1,0},{2,3},{3,2},{4,5},{5,4},{6,7},{7,6},{8,9},{9,8},{10,11... | collective-permute-start | bytes 1179656 | tf_op jit(solution)/shard_map/ppermute | solution.py:409
  40.5 2.5 %slice-start = ((f32[512,512]{1,0:T(8,128)}), f32[256,512]{1,0:T(8,128)S(1)}, s32[]{:S(2)}) async-start(f32[512,512]{1,0:T(8,128)} %copy-done.14), calls=%async_computation.1 | async-start | bytes 1048576 | tf_op jit(solution)/shard_map/slice | solution.py:415
  42.4 5.7 %collective-permute-start.3 = (bf16[192,512]{1,0:T(8,128)(2,1)S(1)}, bf16[192,512]{1,0:T(8,128)(2,1)S(1)}, u32[]{:S(2)}, u32[]{:S(2)}) collective-permute-start(bf16[192,512]{1,0:T(8,128)(2,1)S(1)} %slice.56), channel_id=1, source_target_pairs={{0,4},{1,3},{2,6},{3,1},{4,0},{5,7},{6,2},{7,5},{8,12},{9,11},{10,... | collective-permute-start | bytes 589832 | tf_op jit(solution)/shard_map/ppermute | solution.py:409
  43.1 6.4 %collective-permute-start.9 = (bf16[128,512]{1,0:T(8,128)(2,1)S(1)}, bf16[128,512]{1,0:T(8,128)(2,1)S(1)}, u32[]{:S(2)}, u32[]{:S(2)}) collective-permute-start(bf16[128,512]{1,0:T(8,128)(2,1)S(1)} %slice.57), channel_id=1, source_target_pairs={{0,4},{1,3},{2,6},{3,1},{4,0},{5,7},{6,2},{7,5},{8,12},{9,11},{10,... | collective-permute-start | bytes 393224 | tf_op jit(solution)/shard_map/ppermute | solution.py:409
  48.2 4.7 %collective-permute-start.4 = (bf16[96,512]{1,0:T(8,128)(2,1)S(1)}, bf16[96,512]{1,0:T(8,128)(2,1)S(1)}, u32[]{:S(2)}, u32[]{:S(2)}) collective-permute-start(bf16[96,512]{1,0:T(8,128)(2,1)S(1)} %slice.58), channel_id=1, source_target_pairs={{0,2},{1,5},{2,0},{3,7},{4,6},{5,1},{6,4},{7,3},{8,10},{9,13},{10,... | collective-permute-start | bytes 294920 | tf_op jit(solution)/shard_map/ppermute | solution.py:409
  49.6 10.9 %collective-permute-start.10 = (bf16[128,512]{1,0:T(8,128)(2,1)S(1)}, bf16[128,512]{1,0:T(8,128)(2,1)S(1)}, u32[]{:S(2)}, u32[]{:S(2)}) collective-permute-start(bf16[128,512]{1,0:T(8,128)(2,1)S(1)} %fusion), channel_id=1, source_target_pairs={{0,8},{1,9},{2,10},{3,11},{4,12},{5,13},{6,14},{7,15},{8,0},{9,1},... | collective-permute-start | bytes 393224 | tf_op jit(solution)/shard_map/ppermute | solution.py:409
  52.9 9.3 %collective-permute-start.5 = (bf16[96,512]{1,0:T(8,128)(2,1)S(1)}, bf16[96,512]{1,0:T(8,128)(2,1)S(1)}, u32[]{:S(2)}, u32[]{:S(2)}) collective-permute-start(bf16[96,512]{1,0:T(8,128)(2,1)S(1)} %fusion.1), channel_id=1, source_target_pairs={{0,8},{1,9},{2,10},{3,11},{4,12},{5,13},{6,14},{7,15},{8,0},{9,1},... | collective-permute-start | bytes 294920 | tf_op jit(solution)/shard_map/ppermute | solution.py:409
  60.5 5.9 %collective-permute-start.11 = (bf16[128,512]{1,0:T(8,128)(2,1)S(1)}, bf16[128,512]{1,0:T(8,128)(2,1)S(1)}, u32[]{:S(2)}, u32[]{:S(2)}) collective-permute-start(bf16[128,512]{1,0:T(8,128)(2,1)S(1)} %add_convert_fusion), channel_id=1, source_target_pairs={{0,4},{1,3},{2,6},{3,1},{4,0},{5,7},{6,2},{7,5},{8,12},{9,11},{10,... | collective-permute-start | bytes 393224 | tf_op jit(solution)/shard_map/ppermute | solution.py:409
  62.3 5.2 %collective-permute-start.6 = (bf16[96,512]{1,0:T(8,128)(2,1)S(1)}, bf16[96,512]{1,0:T(8,128)(2,1)S(1)}, u32[]{:S(2)}, u32[]{:S(2)}) collective-permute-start(bf16[96,512]{1,0:T(8,128)(2,1)S(1)} %add_convert_fusion.1), channel_id=1, source_target_pairs={{0,2},{1,5},{2,0},{3,7},{4,6},{5,1},{6,4},{7,3},{8,10},{9,13},{10,... | collective-permute-start | bytes 294920 | tf_op jit(solution)/shard_map/ppermute | solution.py:409
  66.4 7.9 %collective-permute-start.12 = (bf16[256,512]{1,0:T(8,128)(2,1)S(1)}, bf16[256,512]{1,0:T(8,128)(2,1)S(1)}, u32[]{:S(2)}, u32[]{:S(2)}) collective-permute-start(bf16[256,512]{1,0:T(8,128)(2,1)S(1)} %pad_maximum_fusion.2), channel_id=1, source_target_pairs={{0,2},{1,5},{2,0},{3,7},{4,6},{5,1},{6,4},{7,3},{8,10},{9,13},{10,... | collective-permute-start | bytes 786440 | tf_op jit(solution)/shard_map/ppermute | solution.py:409
  67.5 6.9 %collective-permute-start.7 = (bf16[192,512]{1,0:T(8,128)(2,1)S(1)}, bf16[192,512]{1,0:T(8,128)(2,1)S(1)}, u32[]{:S(2)}, u32[]{:S(2)}) collective-permute-start(bf16[192,512]{1,0:T(8,128)(2,1)S(1)} %pad_maximum_fusion.3), channel_id=1, source_target_pairs={{0,4},{1,3},{2,6},{3,1},{4,0},{5,7},{6,2},{7,5},{8,12},{9,11},{10,... | collective-permute-start | bytes 589832 | tf_op jit(solution)/shard_map/ppermute | solution.py:409
  74.3 2.0 %collective-permute-start.13 = (bf16[512,512]{1,0:T(8,128)(2,1)S(1)}, bf16[512,512]{1,0:T(8,128)(2,1)S(1)}, u32[]{:S(2)}, u32[]{:S(2)}) collective-permute-start(bf16[512,512]{1,0:T(8,128)(2,1)S(1)} %pad_maximum_fusion.held), channel_id=1, source_target_pairs={{0,1},{1,0},{2,3},{3,2},{4,5},{5,4},{6,7},{7,6},{8,9},{9,8},{10,11... | collective-permute-start | bytes 1572872 | tf_op jit(solution)/shard_map/ppermute | solution.py:409
  74.5 3.3 %collective-permute-start.8 = (bf16[384,512]{1,0:T(8,128)(2,1)S(1)}, bf16[384,512]{1,0:T(8,128)(2,1)S(1)}, u32[]{:S(2)}, u32[]{:S(2)}) collective-permute-start(bf16[384,512]{1,0:T(8,128)(2,1)S(1)} %pad_maximum_fusion.1.held), channel_id=1, source_target_pairs={{0,1},{1,0},{2,3},{3,2},{4,5},{5,4},{6,7},{7,6},{8,9},{9,8},{10,11... | collective-permute-start | bytes 1179656 | tf_op jit(solution)/shard_map/ppermute | solution.py:409

commit v7 on v6

--- a/solution.py
+++ b/solution.py
@@ -104,10 +104,11 @@
     pgrad,
     latent,
     feat,
-    w_pad,
+    slope,
     bias_sum,
     kept,
     sent,
+    w_pad,
     table,
     pair,
     wide,
@@ -147,8 +148,10 @@
     for r in range(0, slots, step):
         end = min(r + step, slots)
         pre = mm(feat[r:end, :], w_pad[...])
-        lat = (pre * sigmoid(pre)).astype(BF16)
+        sig = sigmoid(pre)
+        lat = (pre * sig).astype(BF16)
         latent[r:end, :] = lat
+        slope[r:end, :] = sig * (1.0 + pre * (1.0 - sig))
         table[block + r : block + end, :] = halved(mm(lat, w_src[...]).astype(BF16))
     near[...] = halved(mm(mesh[...], w_dst[...]).astype(BF16))
     full = 0.5 * mm(cot[...], w_out[...], 1, 1)
@@ -247,7 +250,7 @@
     slot_half,
     latent,
     feat,
-    w_pad,
+    slope,
     w_src,
     bias_sum,
     kept,
@@ -263,9 +266,7 @@
     slot_grad = slot_sum.astype(BF16)
     grads[0:width, :] = mm(latent[...], slot_grad, 0, 0)
     buffer_grad = mm(slot_grad, w_src[...], 1, 1)
-    pre = mm(feat[...], w_pad[...])
-    sig = sigmoid(pre)
-    embed = (buffer_grad * (sig * (1.0 + pre * (1.0 - sig)))).astype(BF16)
+    embed = (buffer_grad * slope[...]).astype(BF16)
     grads[width : width + padded, :] = mm(feat[...], embed, 0, 0)
     grads[width + channels + 1 : width + channels + 2, :] = bias_sum[0:1, :]
     if grads.shape[0] > width + padded:
@@ -274,22 +275,57 @@
     split_pieces(device_count, 1, grads, kept, sent)
 
 
-def unpack_kernel(device_count, turn, bounds, held, got, *targets):
-    core, masks, pieces = place(device_count, turn)
-    piece = held.shape[0] // pieces
-    used = bounds[-1][1]
-    for c in range(2 * pieces):
-        half = c // pieces
-        begin, end = c * piece, (c + 1) * piece
-        if begin >= used:
-            continue
-        slot = (c % pieces) ^ masks[half]
-        at = pl.ds(pl.multiple_of(slot * piece, 16), piece)
-        values = jnp.where(core == half, held[at, :].astype(F32), got[at, :].astype(F32))
-        for (low, high), target in zip(bounds, targets):
-            lo, hi = max(low, begin), min(high, end)
-            if lo < hi:
-                target[lo - low : hi - low, :] = values[lo - begin : hi - begin, :]
+def segments(bounds, half_rows):
+    found = []
+    for half in range(2):
+        for index, (low, high) in enumerate(bounds):
+            begin, end = max(low, half * half_rows), min(high, (half + 1) * half_rows)
+            if begin < end:
+                found.append((half, index, begin, end))
+    return found
+
+
+def unpack_kernel(device_count, chains, own_half, *refs):
+    count = sum(len(bounds) for _, bounds in chains)
+    chain_rows, refs = refs[0 : len(chains)], refs[len(chains) :]
+    targets = refs[0:count] if own_half else refs[count : 2 * count]
+    buffers, sems = refs[count if own_half else 2 * count : -1], refs[-1]
+
+    def move(half, turn, bounds, rows, base, skip):
+        _, masks, pieces = place(device_count, turn)
+        parts = segments(bounds, rows.shape[0])
+        piece = rows.shape[0] // pieces
+        for p in range(pieces):
+            begin = half * rows.shape[0] + p * piece
+            at = pl.ds(pl.multiple_of((p ^ masks[half]) * piece, 16), piece)
+            values = rows[at, :].astype(F32)
+            for k, (owner, _, low, high) in enumerate(parts):
+                lo, hi = max(low, begin), min(high, begin + piece)
+                if owner == half and lo < hi:
+                    buffers[skip + k][lo - low : hi - low, :] = values[lo - begin : hi - begin, :]
+        copies = []
+        for k, (owner, index, low, high) in enumerate(parts):
+            if owner == half:
+                target = targets[base + index]
+                if high - low < target.shape[0]:
+                    first = low - bounds[index][0]
+                    target = target.at[first : first + high - low, :]
+                copies.append(fetch(buffers[skip + k], target, sems, skip + k))
+        return copies
+
+    def move_all(half):
+        base, skip, copies = 0, 0, []
+        for (turn, bounds), rows in zip(chains, chain_rows):
+            copies += move(half, turn, bounds, rows, base, skip)
+            base += len(bounds)
+            skip += len(segments(bounds, rows.shape[0]))
+        for copy in copies:
+            copy.wait()
+
+    core = lax.rem(lax.axis_index("dom"), 2)
+    which = core if own_half else 1 - core
+    for half in range(2):
+        pl.when(which == half)(functools.partial(move_all, half))
 
 
 def shards(
@@ -354,14 +390,14 @@
         + blocks * edges * width * (depth + 4 * block)
         + 5 * nodes * width * width
     )
-    hid_sum, pgrad, latent, feat, w_pad, bias_sum, kept_mesh, sent_mesh = pl.pallas_call(
+    hid_sum, pgrad, latent, feat, slope, bias_sum, kept_mesh, sent_mesh = pl.pallas_call(
         functools.partial(forward_kernel, device_count),
         out_shape=(
             shape((nodes, width), BF16),
             shape((blocks * edges, width), BF16),
             shape((slots, width), BF16),
             shape((slots, padded), BF16),
-            shape((padded, width), BF16),
+            shape((slots, width), F32),
             shape((8, width), F32),
             shape((mesh_rows // 2, width), F32),
             shape((mesh_rows // 2, width), BF16),
@@ -369,6 +405,7 @@
         in_specs=[smem] + [vmem] * 12,
         out_specs=(vmem,) * 8,
         scratch_shapes=[
+            pltpu.VMEM((padded, width), BF16),
             pltpu.VMEM((depth, width), BF16),
             pltpu.VMEM((2 * block, width), BF16),
             pltpu.VMEM((padded, width), F32),
@@ -465,9 +502,8 @@
             transcendentals=slots * width,
         ),
         name="backward_rows",
-    )(edge_src, pgrad, slot_half, latent, feat, w_pad, w_src, bias_sum)
-
-    sent_grid, got_mesh = lax.optimization_barrier((sent_grid, got_mesh))
+    )(edge_src, pgrad, slot_half, latent, feat, slope, w_src, bias_sum)
+
 
     mesh_out = pl.pallas_call(
         mesh_kernel,
@@ -481,23 +517,41 @@
         name="mesh_rows",
     )(mesh_latent, hid_sum, w_out)
 
-    def unpack(turn, pair, bounds):
-        return pl.pallas_call(
-            functools.partial(unpack_kernel, device_count, turn, bounds),
-            out_shape=tuple(shape((high - low, width), F32) for low, high in bounds),
-            in_specs=[vmem] * 2,
-            out_specs=(vmem,) * len(bounds),
-            compiler_params=limit(16),
-            name="unpack_rows",
-        )(*pair)
-
-    mesh_pair = reduce_pieces(0, held_mesh, got_mesh)
+    def unpack(chains, pairs):
+        sizes = [high - low for _, bounds in chains for low, high in bounds]
+        parts = [
+            high - low
+            for (_, bounds), (rows, _) in zip(chains, pairs)
+            for _, _, low, high in segments(bounds, rows.shape[0])
+        ]
+        targets = ()
+        for own_half, chain_rows in zip((True, False), zip(*pairs)):
+            targets = pl.pallas_call(
+                functools.partial(unpack_kernel, device_count, chains, own_half),
+                out_shape=tuple(shape((size, width), F32) for size in sizes),
+                in_specs=[vmem] * len(chains) + [hbm] * len(targets),
+                out_specs=(hbm,) * len(sizes),
+                scratch_shapes=[pltpu.VMEM((size, width), F32) for size in parts]
+                + [dma((len(parts),))],
+                input_output_aliases={len(chains) + k: k for k in range(len(targets))},
+                compiler_params=limit(12),
+                name="unpack_rows",
+            )(*chain_rows, *targets)
+        return targets
+
+    mesh_out, got_mesh = lax.optimization_barrier((mesh_out, got_mesh))
+    held_mesh, next_mesh = cut(held_mesh + got_mesh.astype(F32))
     held_grid, next_grid = pair_sum(kept_grid, sent_grid)
-    mesh_out, next_grid = lax.optimization_barrier((mesh_out, next_grid))
+    next_grid, next_mesh = lax.optimization_barrier((next_grid, next_mesh))
+    got_mesh = swap(next_mesh, stages[0][1])
+    mesh_pair = reduce_pieces(0, held_mesh, got_mesh, 2)
     grid_pair = reduce_pieces(1, held_grid, swap(next_grid, stages[1][0]))
-    grad_out, grad_dst = unpack(0, mesh_pair, ((0, width), (width, 2 * width)))
     end = width + channels
-    grad_src, grad_embed, biases = unpack(1, grid_pair, ((0, width), (width, end), (end, end + 2)))
+    mesh_bounds = ((0, width), (width, 2 * width))
+    grid_bounds = ((0, width), (width, end), (end, end + 2))
+    grad_out, grad_dst, grad_src, grad_embed, biases = unpack(
+        ((0, mesh_bounds), (1, grid_bounds)), (mesh_pair, grid_pair)
+    )
     return mesh_out, grad_embed, grad_src, grad_dst, grad_out, biases
 
 

time: 79.2 us -> 77.1 us (0.973)
  waiting for transfers between devices: 28.3 us -> 24.1 us
  starting transfers between devices: 7.19 us -> 9.5 us
    ppermute x14, waiting for transfers between devices: 28.3 us -> 24.1 us  [swap(): lax.ppermute(values, 'dom', [(d, d ^ 1 << bits[d % 2]) for d in range(dev...]
    ppermute x14, starting transfers between devices: 7.19 us -> 9.5 us  [swap(): lax.ppermute(values, 'dom', [(d, d ^ 1 << bits[d % 2]) for d in range(dev...]
  transfers between devices with their start and end apart: 14 -> 14, of which waited for: 10 -> 8; matrix products, arithmetic and copies ran while one was open for 0% -> 0% of each run, Pallas kernels for 13% -> 12%
where the time goes in v7:
time: 77.1 us; the launch traced here: 76.9 us
  Pallas kernels  25.7 us (33%)
  waiting for transfers between devices  24.1 us (31%)
  blocking collectives  13.9 us (18%)
  starting transfers between devices  9.5 us (12%)
  local copies, waits for them, and re-layouts  1.83 us (2%)
  between operations  1.17 us (2%)
    ppermute x14, waiting for transfers between devices, swap(): lax.ppermute(values, 'dom', [(d, d ^ 1 << bits[d % 2]) for d in range(dev...  24.1 us
    pallas_call x1, Pallas kernels, shards(): pl.pallas_call(functools.partial(forward_kernel, device_count), out_shape...  14.2 us
    all_to_all x1, blocking collectives, shards(): lax.all_to_all(send, 'dom', split_axis=0, concat_axis=0, tiled=True)  13.9 us
    ppermute x14, starting transfers between devices, swap(): lax.ppermute(values, 'dom', [(d, d ^ 1 << bits[d % 2]) for d in range(dev...  9.5 us
    pallas_call x1, Pallas kernels, shards(): pl.pallas_call(functools.partial(backward_kernel, channels, device_count)...  4.24 us
    pallas_call x1, Pallas kernels, shards(): pl.pallas_call(scatter_kernel, out_shape=shape((slots, width), F32), in_s...  2.68 us
    pallas_call x2, Pallas kernels, unpack(): pl.pallas_call(functools.partial(unpack_kernel, device_count, chains, own...  2.67 us
    unnamed x30, local copies, waits for them, and re-layouts  1.73 us
  transfers between devices with their start and end apart: 14, of which 8 were waited for; matrix products, arithmetic and copies ran while one was open for 0% of the time, Pallas kernels for 12%

profile of v7, /device:TPU:0, one launch (start us, length us, event | category | flops | bytes accessed | tf_op | source)
XLA Modules:
  0.0 76.9 jit_solution(13128617132769156506)
XLA Ops:
  0.6 1.0 %copy-done.5 = bf16[1024,227]{0,1:T(8,128)(2,1)S(1)} copy-done((bf16[1024,227]{0,1:T(8,128)(2,1)S(1)}, bf16[1024,227]{0,1:T(8,128)(2,1)}, u32[]{:S(2)}) %copy-start.5) | copy-done | bytes 464920
  1.7 0.7 copy-done.12
  2.4 0.7 pick_rows.1
  3.1 13.9 %all_to_all.5.feat_in = bf16[16,4,256]{2,1,0:T(4,128)(2,1)S(1)} all-to-all(bf16[16,4,256]{2,1,0:T(4,128)(2,1)S(1)} %pick_rows.1), channel_id=1, replica_groups=mesh['ens'=2,'dom'=16] {'dom'}, dimensions={0} | all-to-all | bytes 65536 | tf_op jit(solution)/shard_map/all_to_all | solution.py:386
  17.1 14.2 %forward_rows.1 = (bf16[512,512]{1,0:T(8,128)(2,1)S(1)}, bf16[4096,512]{1,0:T(8,128)(2,1)S(1)}, bf16[1088,512]{1,0:T(8,128)(2,1)S(1)}, bf16[1088,256]{1,0:T(8,12...) custom-call(s32[4]{0:T(128)S(1)} %copy-done.13, ...), custom_call_target="tpu_custom_call" | custom-call | flops 9714008064 | bytes 8388608 | tf_op jit(solution)/shard_map/forward_rows/pallas_call | solution.py:393
  31.4 2.7 %scatter_rows.1.slot_half = f32[1088,512]{1,0:T(8,128)S(1)} custom-call(s32[4,1024]{1,0:T(4,128)S(1)} %copy-done.9, bf16[4096,512]{1,0:T(8,128)(2,1)S(1)} %get-tuple-element.34.pgrad), custom_call_target="tpu_custom_call" | custom-call | flops 2281701376 | bytes 2097152 | tf_op jit(solution)/shard_map/scatter_rows/pallas_call | solution.py:469
  34.1 0.2 convert_add_fusion
  34.3 0.5 collective-permute-start.1
  34.8 4.2 %backward_rows.1 = (f32[384,512]{1,0:T(8,128)S(1)}, bf16[384,512]{1,0:T(8,128)(2,1)S(1)}) custom-call(s32[4,1024]{1,0:T(4,128)S(1)} %copy-done.9, bf16[4096,512]{1,0:T(8,128)(2,1)S(1)} %get-tuple-element.34.pgrad, f32[1088,512]{1,0:T(8,128)S(1)} %scatter_rows.1.slot_half, bf16[1088,512]{1,0:T(8,128)(2,1)S(1)} %get-tuple-element.42.latent, ...), custom_call_target="tpu_custom_call" | custom-call | flops 3992977408 | bytes 2097152 | tf_op jit(solution)/shard_map/backward_rows/pallas_call | solution.py:486
  39.1 0.2 collective-permute-start.2
  39.3 1.2 %mesh_rows.1 = bf16[512,512]{1,0:T(8,128)(2,1)} custom-call(bf16[512,512]{1,0:T(8,128)(2,1)S(1)} %copy-done, bf16[512,512]{1,0:T(8,128)(2,1)S(1)} %get-tuple-element.33.hid_sum, bf16[512,512]{1,0:T(8,128)(2,1)S(1)} %copy-done.1), custom_call_target="tpu_custom_call" | custom-call | flops 268435456 | bytes 2097152 | tf_op jit(solution)/shard_map/mesh_rows/pallas_call | solution.py:508
  40.5 0.3 collective-permute-done.1
  40.8 0.1 convert_add_fusion.2
  40.9 0.1 convert_add_fusion.1
  41.0 1.5 %collective-permute-start.8 = (bf16[192,512]{1,0:T(8,128)(2,1)S(1)}, bf16[192,512]{1,0:T(8,128)(2,1)S(1)}, u32[]{:S(2)}, u32[]{:S(2)}) collective-permute-start(bf16[192,512]{1,0:T(8,128)(2,1)S(1)} %slice.56), channel_id=1, source_target_pairs={{0,4},{1,3},{2,6},{3,1},{4,0},{5,7},{6,2},{7,5},{8,12},{9,11},{10,... | collective-permute-start | bytes 589832 | tf_op jit(solution)/shard_map/ppermute | solution.py:446
  42.6 0.6 collective-permute-start.3
  43.1 3.6 %collective-permute-done.8 = bf16[192,512]{1,0:T(8,128)(2,1)S(1)} collective-permute-done((bf16[192,512]{1,0:T(8,128)(2,1)S(1)}, bf16[192,512]{1,0:T(8,128)(2,1)S(1)}, u32[]{:S(2)}, u32[]{:S(2)}) %collective-permute-start.8) | collective-permute-done | bytes 196640 | tf_op jit(solution)/shard_map/ppermute | solution.py:446
  46.9 1.6 %collective-permute-start.9 = (bf16[96,512]{1,0:T(8,128)(2,1)S(1)}, bf16[96,512]{1,0:T(8,128)(2,1)S(1)}, u32[]{:S(2)}, u32[]{:S(2)}) collective-permute-start(bf16[96,512]{1,0:T(8,128)(2,1)S(1)} %slice.58), channel_id=1, source_target_pairs={{0,2},{1,5},{2,0},{3,7},{4,6},{5,1},{6,4},{7,3},{8,10},{9,13},{10,... | collective-permute-start | bytes 294920 | tf_op jit(solution)/shard_map/ppermute | solution.py:446
  48.6 0.5 collective-permute-start.4
  49.1 2.4 %collective-permute-done.9 = bf16[96,512]{1,0:T(8,128)(2,1)S(1)} collective-permute-done((bf16[96,512]{1,0:T(8,128)(2,1)S(1)}, bf16[96,512]{1,0:T(8,128)(2,1)S(1)}, u32[]{:S(2)}, u32[]{:S(2)}) %collective-permute-start.9) | collective-permute-done | bytes 98336 | tf_op jit(solution)/shard_map/ppermute | solution.py:446
  51.6 0.7 collective-permute-start.10
  52.3 7.7 %collective-permute-done.4 = bf16[128,512]{1,0:T(8,128)(2,1)S(1)} collective-permute-done((bf16[128,512]{1,0:T(8,128)(2,1)S(1)}, bf16[128,512]{1,0:T(8,128)(2,1)S(1)}, u32[]{:S(2)}, u32[]{:S(2)}) %collective-permute-start.4) | collective-permute-done | bytes 131104 | tf_op jit(solution)/shard_map/ppermute | solution.py:446
  60.0 0.1 collective-permute-start.5
  60.1 0.9 %collective-permute-done.10 = bf16[96,512]{1,0:T(8,128)(2,1)S(1)} collective-permute-done((bf16[96,512]{1,0:T(8,128)(2,1)S(1)}, bf16[96,512]{1,0:T(8,128)(2,1)S(1)}, u32[]{:S(2)}, u32[]{:S(2)}) %collective-permute-start.10) | collective-permute-done | bytes 98336 | tf_op jit(solution)/shard_map/ppermute | solution.py:446
  61.1 1.5 %collective-permute-start.11 = (bf16[96,512]{1,0:T(8,128)(2,1)S(1)}, bf16[96,512]{1,0:T(8,128)(2,1)S(1)}, u32[]{:S(2)}, u32[]{:S(2)}) collective-permute-start(bf16[96,512]{1,0:T(8,128)(2,1)S(1)} %add_convert_fusion.1), channel_id=1, source_target_pairs={{0,2},{1,5},{2,0},{3,7},{4,6},{5,1},{6,4},{7,3},{8,10},{9,13},{10,... | collective-permute-start | bytes 294920 | tf_op jit(solution)/shard_map/ppermute | solution.py:446
  62.5 2.9 %collective-permute-done.5 = bf16[128,512]{1,0:T(8,128)(2,1)S(1)} collective-permute-done((bf16[128,512]{1,0:T(8,128)(2,1)S(1)}, bf16[128,512]{1,0:T(8,128)(2,1)S(1)}, u32[]{:S(2)}, u32[]{:S(2)}) %collective-permute-start.5) | collective-permute-done | bytes 131104 | tf_op jit(solution)/shard_map/ppermute | solution.py:446
  65.4 1.5 %collective-permute-start.6 = (bf16[256,512]{1,0:T(8,128)(2,1)S(1)}, bf16[256,512]{1,0:T(8,128)(2,1)S(1)}, u32[]{:S(2)}, u32[]{:S(2)}) collective-permute-start(bf16[256,512]{1,0:T(8,128)(2,1)S(1)} %pad_maximum_fusion.2), channel_id=1, source_target_pairs={{0,2},{1,5},{2,0},{3,7},{4,6},{5,1},{6,4},{7,3},{8,10},{9,13},{10,... | collective-permute-start | bytes 786440 | tf_op jit(solution)/shard_map/ppermute | solution.py:446
  67.1 5.7 %collective-permute-done.6 = bf16[256,512]{1,0:T(8,128)(2,1)S(1)} collective-permute-done((bf16[256,512]{1,0:T(8,128)(2,1)S(1)}, bf16[256,512]{1,0:T(8,128)(2,1)S(1)}, u32[]{:S(2)}, u32[]{:S(2)}) %collective-permute-start.6) | collective-permute-done | bytes 262176 | tf_op jit(solution)/shard_map/ppermute | solution.py:446
  73.0 0.5 collective-permute-start.13
  73.5 1.3 %unpack_rows.2 = (f32[512,512]{1,0:T(8,128)}, f32[512,512]{1,0:T(8,128)}, f32[512,512]{1,0:T(8,128)}, f32[227,512]{1,0:T(8,128)}, f32[2,512]{1,0:T(2,128)}) custom-call(bf16[512,512]{1,0:T(8,128)(2,1)S(1)} %pad_maximum_fusion.refs_0_, bf16[384,512]{1,0:T(8,128)(2,1)S(1)} %pad_maximum_fusion.1.refs_1_), custom_call_target="tpu_custom_call" | custom-call | tf_op jit(solution)/shard_map/unpack_rows/pallas_call | solution.py:529
  74.9 0.5 collective-permute-done.13.refs_1_
  75.4 1.3 %unpack_rows.3 = (f32[512,512]{1,0:T(8,128)}, f32[512,512]{1,0:T(8,128)}, f32[512,512]{1,0:T(8,128)}, f32[227,512]{1,0:T(8,128)}, f32[2,512]{1,0:T(2,128)}) custom-call(bf16[512,512]{1,0:T(8,128)(2,1)S(1)} %collective-permute-done.7.refs_0_, ...), custom_call_target="tpu_custom_call", output_to_operand_aliasing={{0}: (2, {}), {1}: (3, {}), {2}: (4, {}), {3}: (5, {}), {4}... | custom-call | tf_op jit(solution)/shard_map/unpack_rows/pallas_call | solution.py:529
  (52 shorter events, 0.7 us)
Async XLA Ops:
  0.6 1.0 %copy-start.5 = (bf16[1024,227]{0,1:T(8,128)(2,1)S(1)}, bf16[1024,227]{0,1:T(8,128)(2,1)}, u32[]{:S(2)}) copy-start(bf16[1024,227]{0,1:T(8,128)(2,1)} %param.13) | copy-start | bytes 1394692
  1.7 0.7 copy-start.12
  2.3 14.7 %copy-start = (bf16[512,512]{1,0:T(8,128)(2,1)S(1)}, bf16[512,512]{1,0:T(8,128)(2,1)}, u32[]{:S(2)}) copy-start(bf16[512,512]{1,0:T(8,128)(2,1)} %mesh.3) | copy-start | bytes 1572868
  2.3 14.7 %copy-start.1 = (bf16[512,512]{1,0:T(8,128)(2,1)S(1)}, bf16[512,512]{1,0:T(8,128)(2,1)}, u32[]{:S(2)}) copy-start(bf16[512,512]{1,0:T(8,128)(2,1)} %w_out.3) | copy-start | bytes 1572868
  2.3 14.7 %copy-start.2 = (bf16[512,512]{1,0:T(8,128)(2,1)S(1)}, bf16[512,512]{1,0:T(8,128)(2,1)}, u32[]{:S(2)}) copy-start(bf16[512,512]{1,0:T(8,128)(2,1)} %w_dst.1) | copy-start | bytes 1572868
  2.3 14.7 %copy-start.3 = (bf16[512,512]{1,0:T(8,128)(2,1)S(1)}, bf16[512,512]{1,0:T(8,128)(2,1)}, u32[]{:S(2)}) copy-start(bf16[512,512]{1,0:T(8,128)(2,1)} %cot.1) | copy-start | bytes 1572868
  2.3 14.7 %copy-start.4 = (bf16[512,512]{1,0:T(8,128)(2,1)S(1)}, bf16[512,512]{1,0:T(8,128)(2,1)}, u32[]{:S(2)}) copy-start(bf16[512,512]{1,0:T(8,128)(2,1)} %w_src.3) | copy-start | bytes 1572868
  2.3 14.7 %copy-start.6 = (bf16[1024,227]{0,1:T(8,128)(2,1)S(1)}, bf16[1024,227]{0,1:T(8,128)(2,1)}, u32[]{:S(2)}) copy-start(bf16[1024,227]{0,1:T(8,128)(2,1)} %param.13) | copy-start | bytes 1394692
  2.3 14.7 %copy-start.7 = (bf16[227,512]{1,0:T(8,128)(2,1)S(1)}, bf16[227,512]{1,0:T(8,128)(2,1)}, u32[]{:S(2)}) copy-start(bf16[227,512]{1,0:T(8,128)(2,1)} %w_embed.1) | copy-start | bytes 697348
  2.4 14.7 %copy-start.8 = (s32[4,1024]{1,0:T(4,128)S(1)}, s32[4,1024]{1,0:T(4,128)}, u32[]{:S(2)}) copy-start(s32[4,1024]{1,0:T(4,128)} %dst.1) | copy-start | bytes 49156
  2.4 14.7 %copy-start.9 = (s32[4,1024]{1,0:T(4,128)S(1)}, s32[4,1024]{1,0:T(4,128)}, u32[]{:S(2)}) copy-start(s32[4,1024]{1,0:T(4,128)} %src.5) | copy-start | bytes 49156
  2.4 14.7 %copy-start.10 = (bf16[512]{0:T(512)(128)(2,1)S(1)}, bf16[512]{0:T(512)(128)(2,1)}, u32[]{:S(2)}) copy-start(bf16[512]{0:T(512)(128)(2,1)} %b_embed.1) | copy-start | bytes 3076
  2.4 14.7 %copy-start.11 = (bf16[512]{0:T(512)(128)(2,1)S(1)}, bf16[512]{0:T(512)(128)(2,1)}, u32[]{:S(2)}) copy-start(bf16[512]{0:T(512)(128)(2,1)} %b_hidden.1) | copy-start | bytes 3076
  2.4 14.7 %copy-start.13 = (s32[4]{0:T(128)S(1)}, s32[4]{0:T(128)}, u32[]{:S(2)}) copy-start(s32[4]{0:T(128)} %count.1) | copy-start | bytes 52
  31.3 2.8 %collective-permute-start = (bf16[512,512]{1,0:T(8,128)(2,1)S(1)}, bf16[512,512]{1,0:T(8,128)(2,1)S(1)}, u32[]{:S(2)}, u32[]{:S(2)}) collective-permute-start(bf16[512,512]{1,0:T(8,128)(2,1)S(1)} %get-tuple-element.36), channel_id=1, source_target_pairs={{0,1},{1,0},{2,3},{3,2},{4,5},{5,4},{6,7},{7,6},{8,9},{9,8},{10,11... | collective-permute-start | bytes 1572872 | tf_op jit(solution)/shard_map/ppermute | solution.py:446
  34.3 4.8 %copy-start.14 = (f32[512,512]{1,0:T(8,128)}, f32[512,512]{1,0:T(8,128)S(1)}, u32[]{:S(2)}) copy-start(f32[512,512]{1,0:T(8,128)S(1)} %convert_add_fusion) | copy-start | bytes 3145732
  34.3 6.4 %collective-permute-start.1 = (bf16[256,512]{1,0:T(8,128)(2,1)S(1)}, bf16[256,512]{1,0:T(8,128)(2,1)S(1)}, u32[]{:S(2)}, u32[]{:S(2)}) collective-permute-start(bf16[256,512]{1,0:T(8,128)(2,1)S(1)} %slice.55), channel_id=1, source_target_pairs={{0,2},{1,5},{2,0},{3,7},{4,6},{5,1},{6,4},{7,3},{8,10},{9,13},{10,... | collective-permute-start | bytes 786440 | tf_op jit(solution)/shard_map/ppermute | solution.py:446
  39.1 1.7 %slice-start = ((f32[512,512]{1,0:T(8,128)}), f32[256,512]{1,0:T(8,128)S(1)}, s32[]{:S(2)}) async-start(f32[512,512]{1,0:T(8,128)} %copy-done.14), calls=%async_computation.1 | async-start | bytes 1048576 | tf_op jit(solution)/shard_map/slice | solution.py:452
  39.1 1.8 %collective-permute-start.2 = (bf16[384,512]{1,0:T(8,128)(2,1)S(1)}, bf16[384,512]{1,0:T(8,128)(2,1)S(1)}, u32[]{:S(2)}, u32[]{:S(2)}) collective-permute-start(bf16[384,512]{1,0:T(8,128)(2,1)S(1)} %get-tuple-element.47), channel_id=1, source_target_pairs={{0,1},{1,0},{2,3},{3,2},{4,5},{5,4},{6,7},{7,6},{8,9},{9,8},{10,11... | collective-permute-start | bytes 1179656 | tf_op jit(solution)/shard_map/ppermute | solution.py:446
  41.0 5.7 %collective-permute-start.8 = (bf16[192,512]{1,0:T(8,128)(2,1)S(1)}, bf16[192,512]{1,0:T(8,128)(2,1)S(1)}, u32[]{:S(2)}, u32[]{:S(2)}) collective-permute-start(bf16[192,512]{1,0:T(8,128)(2,1)S(1)} %slice.56), channel_id=1, source_target_pairs={{0,4},{1,3},{2,6},{3,1},{4,0},{5,7},{6,2},{7,5},{8,12},{9,11},{10,... | collective-permute-start | bytes 589832 | tf_op jit(solution)/shard_map/ppermute | solution.py:446
  42.6 6.0 %collective-permute-start.3 = (bf16[128,512]{1,0:T(8,128)(2,1)S(1)}, bf16[128,512]{1,0:T(8,128)(2,1)S(1)}, u32[]{:S(2)}, u32[]{:S(2)}) collective-permute-start(bf16[128,512]{1,0:T(8,128)(2,1)S(1)} %slice.57), channel_id=1, source_target_pairs={{0,4},{1,3},{2,6},{3,1},{4,0},{5,7},{6,2},{7,5},{8,12},{9,11},{10,... | collective-permute-start | bytes 393224 | tf_op jit(solution)/shard_map/ppermute | solution.py:446
  46.9 4.7 %collective-permute-start.9 = (bf16[96,512]{1,0:T(8,128)(2,1)S(1)}, bf16[96,512]{1,0:T(8,128)(2,1)S(1)}, u32[]{:S(2)}, u32[]{:S(2)}) collective-permute-start(bf16[96,512]{1,0:T(8,128)(2,1)S(1)} %slice.58), channel_id=1, source_target_pairs={{0,2},{1,5},{2,0},{3,7},{4,6},{5,1},{6,4},{7,3},{8,10},{9,13},{10,... | collective-permute-start | bytes 294920 | tf_op jit(solution)/shard_map/ppermute | solution.py:446
  48.6 11.4 %collective-permute-start.4 = (bf16[128,512]{1,0:T(8,128)(2,1)S(1)}, bf16[128,512]{1,0:T(8,128)(2,1)S(1)}, u32[]{:S(2)}, u32[]{:S(2)}) collective-permute-start(bf16[128,512]{1,0:T(8,128)(2,1)S(1)} %fusion), channel_id=1, source_target_pairs={{0,8},{1,9},{2,10},{3,11},{4,12},{5,13},{6,14},{7,15},{8,0},{9,1},... | collective-permute-start | bytes 393224 | tf_op jit(solution)/shard_map/ppermute | solution.py:446
  51.6 9.5 %collective-permute-start.10 = (bf16[96,512]{1,0:T(8,128)(2,1)S(1)}, bf16[96,512]{1,0:T(8,128)(2,1)S(1)}, u32[]{:S(2)}, u32[]{:S(2)}) collective-permute-start(bf16[96,512]{1,0:T(8,128)(2,1)S(1)} %fusion.1), channel_id=1, source_target_pairs={{0,8},{1,9},{2,10},{3,11},{4,12},{5,13},{6,14},{7,15},{8,0},{9,1},... | collective-permute-start | bytes 294920 | tf_op jit(solution)/shard_map/ppermute | solution.py:446
  60.0 5.4 %collective-permute-start.5 = (bf16[128,512]{1,0:T(8,128)(2,1)S(1)}, bf16[128,512]{1,0:T(8,128)(2,1)S(1)}, u32[]{:S(2)}, u32[]{:S(2)}) collective-permute-start(bf16[128,512]{1,0:T(8,128)(2,1)S(1)} %add_convert_fusion), channel_id=1, source_target_pairs={{0,4},{1,3},{2,6},{3,1},{4,0},{5,7},{6,2},{7,5},{8,12},{9,11},{10,... | collective-permute-start | bytes 393224 | tf_op jit(solution)/shard_map/ppermute | solution.py:446
  61.1 5.9 %collective-permute-start.11 = (bf16[96,512]{1,0:T(8,128)(2,1)S(1)}, bf16[96,512]{1,0:T(8,128)(2,1)S(1)}, u32[]{:S(2)}, u32[]{:S(2)}) collective-permute-start(bf16[96,512]{1,0:T(8,128)(2,1)S(1)} %add_convert_fusion.1), channel_id=1, source_target_pairs={{0,2},{1,5},{2,0},{3,7},{4,6},{5,1},{6,4},{7,3},{8,10},{9,13},{10,... | collective-permute-start | bytes 294920 | tf_op jit(solution)/shard_map/ppermute | solution.py:446
  65.4 7.4 %collective-permute-start.6 = (bf16[256,512]{1,0:T(8,128)(2,1)S(1)}, bf16[256,512]{1,0:T(8,128)(2,1)S(1)}, u32[]{:S(2)}, u32[]{:S(2)}) collective-permute-start(bf16[256,512]{1,0:T(8,128)(2,1)S(1)} %pad_maximum_fusion.2), channel_id=1, source_target_pairs={{0,2},{1,5},{2,0},{3,7},{4,6},{5,1},{6,4},{7,3},{8,10},{9,13},{10,... | collective-permute-start | bytes 786440 | tf_op jit(solution)/shard_map/ppermute | solution.py:446
  67.0 5.9 %collective-permute-start.12 = (bf16[192,512]{1,0:T(8,128)(2,1)S(1)}, bf16[192,512]{1,0:T(8,128)(2,1)S(1)}, u32[]{:S(2)}, u32[]{:S(2)}) collective-permute-start(bf16[192,512]{1,0:T(8,128)(2,1)S(1)} %pad_maximum_fusion.3), channel_id=1, source_target_pairs={{0,4},{1,3},{2,6},{3,1},{4,0},{5,7},{6,2},{7,5},{8,12},{9,11},{10,... | collective-permute-start | bytes 589832 | tf_op jit(solution)/shard_map/ppermute | solution.py:446
  72.8 2.5 %collective-permute-start.7 = (bf16[512,512]{1,0:T(8,128)(2,1)S(1)}, bf16[512,512]{1,0:T(8,128)(2,1)S(1)}, u32[]{:S(2)}, u32[]{:S(2)}) collective-permute-start(bf16[512,512]{1,0:T(8,128)(2,1)S(1)} %pad_maximum_fusion.refs_0_), channel_id=1, source_target_pairs={{0,1},{1,0},{2,3},{3,2},{4,5},{5,4},{6,7},{7,6},{8,9},{9,8},{10,11... | collective-permute-start | bytes 1572872 | tf_op jit(solution)/shard_map/ppermute | solution.py:446
  73.0 2.4 %collective-permute-start.13 = (bf16[384,512]{1,0:T(8,128)(2,1)S(1)}, bf16[384,512]{1,0:T(8,128)(2,1)S(1)}, u32[]{:S(2)}, u32[]{:S(2)}) collective-permute-start(bf16[384,512]{1,0:T(8,128)(2,1)S(1)} %pad_maximum_fusion.1.refs_1_), channel_id=1, source_target_pairs={{0,1},{1,0},{2,3},{3,2},{4,5},{5,4},{6,7},{7,6},{8,9},{9,8},{10,11... | collective-permute-start | bytes 1179656 | tf_op jit(solution)/shard_map/ppermute | solution.py:446

commit v8 on v7

--- a/solution.py
+++ b/solution.py
@@ -35,8 +35,11 @@
     return copy
 
 
-def pick_kernel(row_pack, feat_hbm, send, feat_t, sems):
-    rows_copy = fetch(feat_hbm, feat_t, sems, 0)
+def begin_kernel(flag):
+    flag[...] = jnp.zeros_like(flag)
+
+
+def pick_kernel(flag, row_pack, feat_t, send):
     channels, own = feat_t.shape
     peers, peer_slots, padded = send.shape
     row = lax.broadcasted_iota(jnp.int32, (own, peers * peer_slots), 0)
@@ -44,7 +47,6 @@
     last = padded - 128
     lane = lax.broadcasted_iota(jnp.int32, (peers * peer_slots, 128), 1) + last
     ones = jnp.where(lane == channels, 1.0, 0.0).astype(BF16)
-    rows_copy.wait()
     rows = mm(pick, feat_t[...], 0, 1)
     for j in range(peers):
         part = slice(j * peer_slots, (j + 1) * peer_slots)
@@ -371,18 +373,27 @@
 
     feat_t = grid_feat.T
     dma = pltpu.SemaphoreType.DMA
+    flag = pl.pallas_call(
+        begin_kernel,
+        out_shape=shape((8, 128), F32),
+        out_specs=vmem,
+        compiler_params=limit(1),
+        cost_estimate=pl.CostEstimate(
+            flops=20_000_000_000, bytes_accessed=own * padded * 2, transcendentals=0
+        ),
+        name="begin",
+    )()
     send = pl.pallas_call(
         pick_kernel,
         out_shape=shape((device_count, peer_slots, padded), BF16),
-        in_specs=[vmem, hbm],
+        in_specs=[vmem] * 3,
         out_specs=vmem,
-        scratch_shapes=[pltpu.VMEM((channels, own), BF16), dma((1,))],
         compiler_params=limit(16),
         cost_estimate=pl.CostEstimate(
             flops=20_000_000_000, bytes_accessed=own * padded * 2, transcendentals=0
         ),
         name="pick_rows",
-    )(row_pack[None, :], feat_t)
+    )(flag, row_pack[None, :], feat_t)
     feat_in = lax.all_to_all(send, "dom", split_axis=0, concat_axis=0, tiled=True)
 
     forward_macs = (

time: 77.1 us -> 75.9 us (0.984)
    unnamed x30 -> x28, local copies, waits for them, and re-layouts: 1.73 us -> 1.08 us
  transfers between devices with their start and end apart: 14 -> 14, of which waited for: 8 -> 8; matrix products, arithmetic and copies ran while one was open for 0% -> 0% of each run, Pallas kernels for 12% -> 13%
where the time goes in v8:
time: 75.9 us; the launch traced here: 75.8 us
  Pallas kernels  25.3 us (33%)
  waiting for transfers between devices  24.1 us (32%)
  blocking collectives  13.9 us (18%)
  starting transfers between devices  9.49 us (13%)
  local copies, waits for them, and re-layouts  1.18 us (2%)
  between operations  1.16 us (2%)
    ppermute x14, waiting for transfers between devices, swap(): lax.ppermute(values, 'dom', [(d, d ^ 1 << bits[d % 2]) for d in range(dev...  24.1 us
    pallas_call x1, Pallas kernels, shards(): pl.pallas_call(functools.partial(forward_kernel, device_count), out_shape...  14.2 us
    all_to_all x1, blocking collectives, shards(): lax.all_to_all(send, 'dom', split_axis=0, concat_axis=0, tiled=True)  13.9 us
    ppermute x14, starting transfers between devices, swap(): lax.ppermute(values, 'dom', [(d, d ^ 1 << bits[d % 2]) for d in range(dev...  9.49 us
    pallas_call x1, Pallas kernels, shards(): pl.pallas_call(functools.partial(backward_kernel, channels, device_count)...  4.24 us
    pallas_call x1, Pallas kernels, shards(): pl.pallas_call(scatter_kernel, out_shape=shape((slots, width), F32), in_s...  2.68 us
    pallas_call x2, Pallas kernels, unpack(): pl.pallas_call(functools.partial(unpack_kernel, device_count, chains, own...  2.67 us
  transfers between devices with their start and end apart: 14, of which 8 were waited for; matrix products, arithmetic and copies ran while one was open for 0% of the time, Pallas kernels for 13%

profile of v8, /device:TPU:0, one launch (start us, length us, event | category | flops | bytes accessed | tf_op | source)
XLA Modules:
  0.0 75.8 jit_solution(2092993392793375118)
XLA Ops:
  0.7 0.6 copy-done.11
  1.3 0.4 copy-done.5
  1.8 0.3 pick_rows.1
  2.1 13.9 %all_to_all.5.feat_in = bf16[16,4,256]{2,1,0:T(4,128)(2,1)S(1)} all-to-all(bf16[16,4,256]{2,1,0:T(4,128)(2,1)S(1)} %pick_rows.1), channel_id=1, replica_groups=mesh['ens'=2,'dom'=16] {'dom'}, dimensions={0} | all-to-all | bytes 65536 | tf_op jit(solution)/shard_map/all_to_all | solution.py:397
  16.1 14.2 %forward_rows.1 = (bf16[512,512]{1,0:T(8,128)(2,1)S(1)}, bf16[4096,512]{1,0:T(8,128)(2,1)S(1)}, bf16[1088,512]{1,0:T(8,128)(2,1)S(1)}, bf16[1088,256]{1,0:T(8,12...) custom-call(s32[4]{0:T(128)S(1)} %copy-done.12, ...), custom_call_target="tpu_custom_call" | custom-call | flops 9714008064 | bytes 8388608 | tf_op jit(solution)/shard_map/forward_rows/pallas_call | solution.py:404
  30.2 0.1 collective-permute-start
  30.3 2.7 %scatter_rows.1.slot_half = f32[1088,512]{1,0:T(8,128)S(1)} custom-call(s32[4,1024]{1,0:T(4,128)S(1)} %copy-done.8, bf16[4096,512]{1,0:T(8,128)(2,1)S(1)} %get-tuple-element.34.pgrad), custom_call_target="tpu_custom_call" | custom-call | flops 2281701376 | bytes 2097152 | tf_op jit(solution)/shard_map/scatter_rows/pallas_call | solution.py:480
  33.0 0.2 convert_add_fusion
  33.2 0.5 collective-permute-start.1
  33.8 4.2 %backward_rows.1 = (f32[384,512]{1,0:T(8,128)S(1)}, bf16[384,512]{1,0:T(8,128)(2,1)S(1)}) custom-call(s32[4,1024]{1,0:T(4,128)S(1)} %copy-done.8, bf16[4096,512]{1,0:T(8,128)(2,1)S(1)} %get-tuple-element.34.pgrad, f32[1088,512]{1,0:T(8,128)S(1)} %scatter_rows.1.slot_half, bf16[1088,512]{1,0:T(8,128)(2,1)S(1)} %get-tuple-element.42.latent, ...), custom_call_target="tpu_custom_call" | custom-call | flops 3992977408 | bytes 2097152 | tf_op jit(solution)/shard_map/backward_rows/pallas_call | solution.py:497
  38.0 0.2 collective-permute-start.2
  38.2 1.2 %mesh_rows.1 = bf16[512,512]{1,0:T(8,128)(2,1)} custom-call(bf16[512,512]{1,0:T(8,128)(2,1)S(1)} %copy-done, bf16[512,512]{1,0:T(8,128)(2,1)S(1)} %get-tuple-element.33.hid_sum, bf16[512,512]{1,0:T(8,128)(2,1)S(1)} %copy-done.1), custom_call_target="tpu_custom_call" | custom-call | flops 268435456 | bytes 2097152 | tf_op jit(solution)/shard_map/mesh_rows/pallas_call | solution.py:519
  39.4 0.3 collective-permute-done.1
  39.7 0.1 convert_add_fusion.2
  39.8 0.1 convert_add_fusion.1
  40.0 1.5 %collective-permute-start.8 = (bf16[192,512]{1,0:T(8,128)(2,1)S(1)}, bf16[192,512]{1,0:T(8,128)(2,1)S(1)}, u32[]{:S(2)}, u32[]{:S(2)}) collective-permute-start(bf16[192,512]{1,0:T(8,128)(2,1)S(1)} %slice.56), channel_id=1, source_target_pairs={{0,4},{1,3},{2,6},{3,1},{4,0},{5,7},{6,2},{7,5},{8,12},{9,11},{10,... | collective-permute-start | bytes 589832 | tf_op jit(solution)/shard_map/ppermute | solution.py:457
  41.4 0.6 collective-permute-start.3
  42.1 3.6 %collective-permute-done.8 = bf16[192,512]{1,0:T(8,128)(2,1)S(1)} collective-permute-done((bf16[192,512]{1,0:T(8,128)(2,1)S(1)}, bf16[192,512]{1,0:T(8,128)(2,1)S(1)}, u32[]{:S(2)}, u32[]{:S(2)}) %collective-permute-start.8) | collective-permute-done | bytes 196640 | tf_op jit(solution)/shard_map/ppermute | solution.py:457
  45.8 1.6 %collective-permute-start.9 = (bf16[96,512]{1,0:T(8,128)(2,1)S(1)}, bf16[96,512]{1,0:T(8,128)(2,1)S(1)}, u32[]{:S(2)}, u32[]{:S(2)}) collective-permute-start(bf16[96,512]{1,0:T(8,128)(2,1)S(1)} %slice.58), channel_id=1, source_target_pairs={{0,2},{1,5},{2,0},{3,7},{4,6},{5,1},{6,4},{7,3},{8,10},{9,13},{10,... | collective-permute-start | bytes 294920 | tf_op jit(solution)/shard_map/ppermute | solution.py:457
  47.5 0.6 collective-permute-start.4
  48.0 2.4 %collective-permute-done.9 = bf16[96,512]{1,0:T(8,128)(2,1)S(1)} collective-permute-done((bf16[96,512]{1,0:T(8,128)(2,1)S(1)}, bf16[96,512]{1,0:T(8,128)(2,1)S(1)}, u32[]{:S(2)}, u32[]{:S(2)}) %collective-permute-start.9) | collective-permute-done | bytes 98336 | tf_op jit(solution)/shard_map/ppermute | solution.py:457
  50.5 0.7 collective-permute-start.10
  51.2 7.7 %collective-permute-done.4 = bf16[128,512]{1,0:T(8,128)(2,1)S(1)} collective-permute-done((bf16[128,512]{1,0:T(8,128)(2,1)S(1)}, bf16[128,512]{1,0:T(8,128)(2,1)S(1)}, u32[]{:S(2)}, u32[]{:S(2)}) %collective-permute-start.4) | collective-permute-done | bytes 131104 | tf_op jit(solution)/shard_map/ppermute | solution.py:457
  59.0 0.9 %collective-permute-done.10 = bf16[96,512]{1,0:T(8,128)(2,1)S(1)} collective-permute-done((bf16[96,512]{1,0:T(8,128)(2,1)S(1)}, bf16[96,512]{1,0:T(8,128)(2,1)S(1)}, u32[]{:S(2)}, u32[]{:S(2)}) %collective-permute-start.10) | collective-permute-done | bytes 98336 | tf_op jit(solution)/shard_map/ppermute | solution.py:457
  59.9 1.5 %collective-permute-start.11 = (bf16[96,512]{1,0:T(8,128)(2,1)S(1)}, bf16[96,512]{1,0:T(8,128)(2,1)S(1)}, u32[]{:S(2)}, u32[]{:S(2)}) collective-permute-start(bf16[96,512]{1,0:T(8,128)(2,1)S(1)} %add_convert_fusion.1), channel_id=1, source_target_pairs={{0,2},{1,5},{2,0},{3,7},{4,6},{5,1},{6,4},{7,3},{8,10},{9,13},{10,... | collective-permute-start | bytes 294920 | tf_op jit(solution)/shard_map/ppermute | solution.py:457
  61.4 2.9 %collective-permute-done.5 = bf16[128,512]{1,0:T(8,128)(2,1)S(1)} collective-permute-done((bf16[128,512]{1,0:T(8,128)(2,1)S(1)}, bf16[128,512]{1,0:T(8,128)(2,1)S(1)}, u32[]{:S(2)}, u32[]{:S(2)}) %collective-permute-start.5) | collective-permute-done | bytes 131104 | tf_op jit(solution)/shard_map/ppermute | solution.py:457
  64.3 1.5 %collective-permute-start.6 = (bf16[256,512]{1,0:T(8,128)(2,1)S(1)}, bf16[256,512]{1,0:T(8,128)(2,1)S(1)}, u32[]{:S(2)}, u32[]{:S(2)}) collective-permute-start(bf16[256,512]{1,0:T(8,128)(2,1)S(1)} %pad_maximum_fusion.2), channel_id=1, source_target_pairs={{0,2},{1,5},{2,0},{3,7},{4,6},{5,1},{6,4},{7,3},{8,10},{9,13},{10,... | collective-permute-start | bytes 786440 | tf_op jit(solution)/shard_map/ppermute | solution.py:457
  65.9 5.7 %collective-permute-done.6 = bf16[256,512]{1,0:T(8,128)(2,1)S(1)} collective-permute-done((bf16[256,512]{1,0:T(8,128)(2,1)S(1)}, bf16[256,512]{1,0:T(8,128)(2,1)S(1)}, u32[]{:S(2)}, u32[]{:S(2)}) %collective-permute-start.6) | collective-permute-done | bytes 262176 | tf_op jit(solution)/shard_map/ppermute | solution.py:457
  71.9 0.5 collective-permute-start.13
  72.4 1.3 %unpack_rows.2 = (f32[512,512]{1,0:T(8,128)}, f32[512,512]{1,0:T(8,128)}, f32[512,512]{1,0:T(8,128)}, f32[227,512]{1,0:T(8,128)}, f32[2,512]{1,0:T(2,128)}) custom-call(bf16[512,512]{1,0:T(8,128)(2,1)S(1)} %pad_maximum_fusion.refs_0_, bf16[384,512]{1,0:T(8,128)(2,1)S(1)} %pad_maximum_fusion.1.refs_1_), custom_call_target="tpu_custom_call" | custom-call | tf_op jit(solution)/shard_map/unpack_rows/pallas_call | solution.py:540
  73.8 0.5 collective-permute-done.13.refs_1_
  74.3 1.3 %unpack_rows.3 = (f32[512,512]{1,0:T(8,128)}, f32[512,512]{1,0:T(8,128)}, f32[512,512]{1,0:T(8,128)}, f32[227,512]{1,0:T(8,128)}, f32[2,512]{1,0:T(2,128)}) custom-call(bf16[512,512]{1,0:T(8,128)(2,1)S(1)} %collective-permute-done.7.refs_0_, ...), custom_call_target="tpu_custom_call", output_to_operand_aliasing={{0}: (2, {}), {1}: (3, {}), {2}: (4, {}), {3}: (5, {}), {4}... | custom-call | tf_op jit(solution)/shard_map/unpack_rows/pallas_call | solution.py:540
  (51 shorter events, 0.7 us)
Async XLA Ops:
  0.6 0.7 copy-start.11
  0.6 1.0 %copy-start.5 = (bf16[1024,227]{0,1:T(8,128)(2,1)S(1)}, bf16[1024,227]{0,1:T(8,128)(2,1)}, u32[]{:S(2)}) copy-start(bf16[1024,227]{0,1:T(8,128)(2,1)} %param.13) | copy-start | bytes 1394692
  1.7 14.3 %copy-start = (bf16[512,512]{1,0:T(8,128)(2,1)S(1)}, bf16[512,512]{1,0:T(8,128)(2,1)}, u32[]{:S(2)}) copy-start(bf16[512,512]{1,0:T(8,128)(2,1)} %mesh.3) | copy-start | bytes 1572868
  1.7 14.3 %copy-start.1 = (bf16[512,512]{1,0:T(8,128)(2,1)S(1)}, bf16[512,512]{1,0:T(8,128)(2,1)}, u32[]{:S(2)}) copy-start(bf16[512,512]{1,0:T(8,128)(2,1)} %w_out.3) | copy-start | bytes 1572868
  1.7 14.3 %copy-start.2 = (bf16[512,512]{1,0:T(8,128)(2,1)S(1)}, bf16[512,512]{1,0:T(8,128)(2,1)}, u32[]{:S(2)}) copy-start(bf16[512,512]{1,0:T(8,128)(2,1)} %w_dst.1) | copy-start | bytes 1572868
  1.7 14.3 %copy-start.3 = (bf16[512,512]{1,0:T(8,128)(2,1)S(1)}, bf16[512,512]{1,0:T(8,128)(2,1)}, u32[]{:S(2)}) copy-start(bf16[512,512]{1,0:T(8,128)(2,1)} %cot.1) | copy-start | bytes 1572868
  1.7 14.3 %copy-start.4 = (bf16[512,512]{1,0:T(8,128)(2,1)S(1)}, bf16[512,512]{1,0:T(8,128)(2,1)}, u32[]{:S(2)}) copy-start(bf16[512,512]{1,0:T(8,128)(2,1)} %w_src.3) | copy-start | bytes 1572868
  1.7 14.3 %copy-start.6 = (bf16[227,512]{1,0:T(8,128)(2,1)S(1)}, bf16[227,512]{1,0:T(8,128)(2,1)}, u32[]{:S(2)}) copy-start(bf16[227,512]{1,0:T(8,128)(2,1)} %w_embed.1) | copy-start | bytes 697348
  1.7 14.3 %copy-start.7 = (s32[4,1024]{1,0:T(4,128)S(1)}, s32[4,1024]{1,0:T(4,128)}, u32[]{:S(2)}) copy-start(s32[4,1024]{1,0:T(4,128)} %dst.1) | copy-start | bytes 49156
  1.7 14.3 %copy-start.8 = (s32[4,1024]{1,0:T(4,128)S(1)}, s32[4,1024]{1,0:T(4,128)}, u32[]{:S(2)}) copy-start(s32[4,1024]{1,0:T(4,128)} %src.5) | copy-start | bytes 49156
  1.7 14.3 %copy-start.9 = (bf16[512]{0:T(512)(128)(2,1)S(1)}, bf16[512]{0:T(512)(128)(2,1)}, u32[]{:S(2)}) copy-start(bf16[512]{0:T(512)(128)(2,1)} %b_embed.1) | copy-start | bytes 3076
  1.7 14.3 %copy-start.10 = (bf16[512]{0:T(512)(128)(2,1)S(1)}, bf16[512]{0:T(512)(128)(2,1)}, u32[]{:S(2)}) copy-start(bf16[512]{0:T(512)(128)(2,1)} %b_hidden.1) | copy-start | bytes 3076
  1.8 14.3 %copy-start.12 = (s32[4]{0:T(128)S(1)}, s32[4]{0:T(128)}, u32[]{:S(2)}) copy-start(s32[4]{0:T(128)} %count.1) | copy-start | bytes 52
  30.2 2.8 %collective-permute-start = (bf16[512,512]{1,0:T(8,128)(2,1)S(1)}, bf16[512,512]{1,0:T(8,128)(2,1)S(1)}, u32[]{:S(2)}, u32[]{:S(2)}) collective-permute-start(bf16[512,512]{1,0:T(8,128)(2,1)S(1)} %get-tuple-element.36), channel_id=1, source_target_pairs={{0,1},{1,0},{2,3},{3,2},{4,5},{5,4},{6,7},{7,6},{8,9},{9,8},{10,11... | collective-permute-start | bytes 1572872 | tf_op jit(solution)/shard_map/ppermute | solution.py:457
  33.2 4.8 %copy-start.13 = (f32[512,512]{1,0:T(8,128)}, f32[512,512]{1,0:T(8,128)S(1)}, u32[]{:S(2)}) copy-start(f32[512,512]{1,0:T(8,128)S(1)} %convert_add_fusion) | copy-start | bytes 3145732
  33.2 6.4 %collective-permute-start.1 = (bf16[256,512]{1,0:T(8,128)(2,1)S(1)}, bf16[256,512]{1,0:T(8,128)(2,1)S(1)}, u32[]{:S(2)}, u32[]{:S(2)}) collective-permute-start(bf16[256,512]{1,0:T(8,128)(2,1)S(1)} %slice.55), channel_id=1, source_target_pairs={{0,2},{1,5},{2,0},{3,7},{4,6},{5,1},{6,4},{7,3},{8,10},{9,13},{10,... | collective-permute-start | bytes 786440 | tf_op jit(solution)/shard_map/ppermute | solution.py:457
  38.0 1.7 %slice-start = ((f32[512,512]{1,0:T(8,128)}), f32[256,512]{1,0:T(8,128)S(1)}, s32[]{:S(2)}) async-start(f32[512,512]{1,0:T(8,128)} %copy-done.13), calls=%async_computation.1 | async-start | bytes 1048576 | tf_op jit(solution)/shard_map/slice | solution.py:463
  38.0 1.8 %collective-permute-start.2 = (bf16[384,512]{1,0:T(8,128)(2,1)S(1)}, bf16[384,512]{1,0:T(8,128)(2,1)S(1)}, u32[]{:S(2)}, u32[]{:S(2)}) collective-permute-start(bf16[384,512]{1,0:T(8,128)(2,1)S(1)} %get-tuple-element.47), channel_id=1, source_target_pairs={{0,1},{1,0},{2,3},{3,2},{4,5},{5,4},{6,7},{7,6},{8,9},{9,8},{10,11... | collective-permute-start | bytes 1179656 | tf_op jit(solution)/shard_map/ppermute | solution.py:457
  40.0 5.7 %collective-permute-start.8 = (bf16[192,512]{1,0:T(8,128)(2,1)S(1)}, bf16[192,512]{1,0:T(8,128)(2,1)S(1)}, u32[]{:S(2)}, u32[]{:S(2)}) collective-permute-start(bf16[192,512]{1,0:T(8,128)(2,1)S(1)} %slice.56), channel_id=1, source_target_pairs={{0,4},{1,3},{2,6},{3,1},{4,0},{5,7},{6,2},{7,5},{8,12},{9,11},{10,... | collective-permute-start | bytes 589832 | tf_op jit(solution)/shard_map/ppermute | solution.py:457
  41.4 6.0 %collective-permute-start.3 = (bf16[128,512]{1,0:T(8,128)(2,1)S(1)}, bf16[128,512]{1,0:T(8,128)(2,1)S(1)}, u32[]{:S(2)}, u32[]{:S(2)}) collective-permute-start(bf16[128,512]{1,0:T(8,128)(2,1)S(1)} %slice.57), channel_id=1, source_target_pairs={{0,4},{1,3},{2,6},{3,1},{4,0},{5,7},{6,2},{7,5},{8,12},{9,11},{10,... | collective-permute-start | bytes 393224 | tf_op jit(solution)/shard_map/ppermute | solution.py:457
  45.8 4.7 %collective-permute-start.9 = (bf16[96,512]{1,0:T(8,128)(2,1)S(1)}, bf16[96,512]{1,0:T(8,128)(2,1)S(1)}, u32[]{:S(2)}, u32[]{:S(2)}) collective-permute-start(bf16[96,512]{1,0:T(8,128)(2,1)S(1)} %slice.58), channel_id=1, source_target_pairs={{0,2},{1,5},{2,0},{3,7},{4,6},{5,1},{6,4},{7,3},{8,10},{9,13},{10,... | collective-permute-start | bytes 294920 | tf_op jit(solution)/shard_map/ppermute | solution.py:457
  47.5 11.4 %collective-permute-start.4 = (bf16[128,512]{1,0:T(8,128)(2,1)S(1)}, bf16[128,512]{1,0:T(8,128)(2,1)S(1)}, u32[]{:S(2)}, u32[]{:S(2)}) collective-permute-start(bf16[128,512]{1,0:T(8,128)(2,1)S(1)} %fusion), channel_id=1, source_target_pairs={{0,8},{1,9},{2,10},{3,11},{4,12},{5,13},{6,14},{7,15},{8,0},{9,1},... | collective-permute-start | bytes 393224 | tf_op jit(solution)/shard_map/ppermute | solution.py:457
  50.5 9.4 %collective-permute-start.10 = (bf16[96,512]{1,0:T(8,128)(2,1)S(1)}, bf16[96,512]{1,0:T(8,128)(2,1)S(1)}, u32[]{:S(2)}, u32[]{:S(2)}) collective-permute-start(bf16[96,512]{1,0:T(8,128)(2,1)S(1)} %fusion.1), channel_id=1, source_target_pairs={{0,8},{1,9},{2,10},{3,11},{4,12},{5,13},{6,14},{7,15},{8,0},{9,1},... | collective-permute-start | bytes 294920 | tf_op jit(solution)/shard_map/ppermute | solution.py:457
  58.9 5.4 %collective-permute-start.5 = (bf16[128,512]{1,0:T(8,128)(2,1)S(1)}, bf16[128,512]{1,0:T(8,128)(2,1)S(1)}, u32[]{:S(2)}, u32[]{:S(2)}) collective-permute-start(bf16[128,512]{1,0:T(8,128)(2,1)S(1)} %add_convert_fusion), channel_id=1, source_target_pairs={{0,4},{1,3},{2,6},{3,1},{4,0},{5,7},{6,2},{7,5},{8,12},{9,11},{10,... | collective-permute-start | bytes 393224 | tf_op jit(solution)/shard_map/ppermute | solution.py:457
  59.9 5.9 %collective-permute-start.11 = (bf16[96,512]{1,0:T(8,128)(2,1)S(1)}, bf16[96,512]{1,0:T(8,128)(2,1)S(1)}, u32[]{:S(2)}, u32[]{:S(2)}) collective-permute-start(bf16[96,512]{1,0:T(8,128)(2,1)S(1)} %add_convert_fusion.1), channel_id=1, source_target_pairs={{0,2},{1,5},{2,0},{3,7},{4,6},{5,1},{6,4},{7,3},{8,10},{9,13},{10,... | collective-permute-start | bytes 294920 | tf_op jit(solution)/shard_map/ppermute | solution.py:457
  64.3 7.4 %collective-permute-start.6 = (bf16[256,512]{1,0:T(8,128)(2,1)S(1)}, bf16[256,512]{1,0:T(8,128)(2,1)S(1)}, u32[]{:S(2)}, u32[]{:S(2)}) collective-permute-start(bf16[256,512]{1,0:T(8,128)(2,1)S(1)} %pad_maximum_fusion.2), channel_id=1, source_target_pairs={{0,2},{1,5},{2,0},{3,7},{4,6},{5,1},{6,4},{7,3},{8,10},{9,13},{10,... | collective-permute-start | bytes 786440 | tf_op jit(solution)/shard_map/ppermute | solution.py:457
  65.9 5.9 %collective-permute-start.12 = (bf16[192,512]{1,0:T(8,128)(2,1)S(1)}, bf16[192,512]{1,0:T(8,128)(2,1)S(1)}, u32[]{:S(2)}, u32[]{:S(2)}) collective-permute-start(bf16[192,512]{1,0:T(8,128)(2,1)S(1)} %pad_maximum_fusion.3), channel_id=1, source_target_pairs={{0,4},{1,3},{2,6},{3,1},{4,0},{5,7},{6,2},{7,5},{8,12},{9,11},{10,... | collective-permute-start | bytes 589832 | tf_op jit(solution)/shard_map/ppermute | solution.py:457
  71.7 2.5 %collective-permute-start.7 = (bf16[512,512]{1,0:T(8,128)(2,1)S(1)}, bf16[512,512]{1,0:T(8,128)(2,1)S(1)}, u32[]{:S(2)}, u32[]{:S(2)}) collective-permute-start(bf16[512,512]{1,0:T(8,128)(2,1)S(1)} %pad_maximum_fusion.refs_0_), channel_id=1, source_target_pairs={{0,1},{1,0},{2,3},{3,2},{4,5},{5,4},{6,7},{7,6},{8,9},{9,8},{10,11... | collective-permute-start | bytes 1572872 | tf_op jit(solution)/shard_map/ppermute | solution.py:457
  71.9 2.4 %collective-permute-start.13 = (bf16[384,512]{1,0:T(8,128)(2,1)S(1)}, bf16[384,512]{1,0:T(8,128)(2,1)S(1)}, u32[]{:S(2)}, u32[]{:S(2)}) collective-permute-start(bf16[384,512]{1,0:T(8,128)(2,1)S(1)} %pad_maximum_fusion.1.refs_1_), channel_id=1, source_target_pairs={{0,1},{1,0},{2,3},{3,2},{4,5},{5,4},{6,7},{7,6},{8,9},{9,8},{10,11... | collective-permute-start | bytes 1179656 | tf_op jit(solution)/shard_map/ppermute | solution.py:457

commit v9 on v8

--- a/solution.py
+++ b/solution.py
@@ -114,7 +114,6 @@
     table,
     pair,
     wide,
-    wide_t,
     incoming,
     one_hot,
     one_hot_t,
@@ -133,17 +132,16 @@
     nodes = mesh.shape[0]
     block = nodes // blocks
     depth = table.shape[0]
-    step = 256
+    step = 512
 
     last = padded - 32
     wide[last:padded, :] = jnp.zeros((32, width), F32)
     wide[0:channels, :] = w_embed[...].astype(F32)
     wide[channels : channels + 1, :] = b_embed[...].astype(F32).reshape(1, width)
     w_pad[...] = wide[...].astype(BF16)
-    wide_t[last:padded, :] = jnp.zeros((32, own), F32)
-    wide_t[0:channels, :] = feat_t[...].astype(F32)
-    wide_t[channels : channels + 1, :] = jnp.ones((1, own), F32)
-    feat[0:own, :] = jnp.transpose(wide_t[...]).astype(BF16)
+    lane = lax.broadcasted_iota(jnp.int32, (own, 128), 1) + (padded - 128)
+    feat[0:own, padded - 128 : padded] = jnp.where(lane == channels, 1.0, 0.0).astype(BF16)
+    feat[0:own, 0:channels] = jnp.transpose(feat_t[...])
     for j in range(peers):
         incoming[j * peer_slots : (j + 1) * peer_slots, :] = feat_in[j].astype(F32)
     feat[own:slots, :] = incoming[...].astype(BF16)
@@ -420,7 +418,6 @@
             pltpu.VMEM((depth, width), BF16),
             pltpu.VMEM((2 * block, width), BF16),
             pltpu.VMEM((padded, width), F32),
-            pltpu.VMEM((padded, own), F32),
             pltpu.VMEM((more, padded), F32),
             pltpu.VMEM((edges, depth + block), BF16),
             pltpu.VMEM((block, edges), BF16),

time: 75.9 us -> 75.3 us (level)
  no operation moved by 1% of the time
where the time goes in v9:
time: 75.3 us; the launch traced here: 75.1 us
  Pallas kernels  24.6 us (33%)
  waiting for transfers between devices  24.1 us (32%)
  blocking collectives  13.9 us (18%)
  starting transfers between devices  9.47 us (13%)
  local copies, waits for them, and re-layouts  1.18 us (2%)
  between operations  1.15 us (2%)
    ppermute x14, waiting for transfers between devices, swap(): lax.ppermute(values, 'dom', [(d, d ^ 1 << bits[d % 2]) for d in range(dev...  24.1 us
    all_to_all x1, blocking collectives, shards(): lax.all_to_all(send, 'dom', split_axis=0, concat_axis=0, tiled=True)  13.9 us
    pallas_call x1, Pallas kernels, shards(): pl.pallas_call(functools.partial(forward_kernel, device_count), out_shape...  13.6 us
    ppermute x14, starting transfers between devices, swap(): lax.ppermute(values, 'dom', [(d, d ^ 1 << bits[d % 2]) for d in range(dev...  9.47 us
    pallas_call x1, Pallas kernels, shards(): pl.pallas_call(functools.partial(backward_kernel, channels, device_count)...  4.24 us
    pallas_call x2, Pallas kernels, unpack(): pl.pallas_call(functools.partial(unpack_kernel, device_count, chains, own...  2.67 us
    pallas_call x1, Pallas kernels, shards(): pl.pallas_call(scatter_kernel, out_shape=shape((slots, width), F32), in_s...  2.65 us
  transfers between devices with their start and end apart: 14, of which 8 were waited for; matrix products, arithmetic and copies ran while one was open for 0% of the time, Pallas kernels for 13%

profile of v9, /device:TPU:0, one launch (start us, length us, event | category | flops | bytes accessed | tf_op | source)
XLA Modules:
  0.0 75.1 jit_solution(4308478135011729683)
XLA Ops:
  0.7 0.6 copy-done.11
  1.3 0.4 copy-done.5
  1.8 0.3 pick_rows.1
  2.1 13.9 %all_to_all.5.feat_in = bf16[16,4,256]{2,1,0:T(4,128)(2,1)S(1)} all-to-all(bf16[16,4,256]{2,1,0:T(4,128)(2,1)S(1)} %pick_rows.1), channel_id=1, replica_groups=mesh['ens'=2,'dom'=16] {'dom'}, dimensions={0} | all-to-all | bytes 65536 | tf_op jit(solution)/shard_map/all_to_all | solution.py:395
  16.1 13.6 %forward_rows.1 = (bf16[512,512]{1,0:T(8,128)(2,1)S(1)}, bf16[4096,512]{1,0:T(8,128)(2,1)S(1)}, bf16[1088,512]{1,0:T(8,128)(2,1)S(1)}, bf16[1088,256]{1,0:T(8,12...) custom-call(s32[4]{0:T(128)S(1)} %copy-done.12, ...), custom_call_target="tpu_custom_call" | custom-call | flops 9714008064 | bytes 8388608 | tf_op jit(solution)/shard_map/forward_rows/pallas_call | solution.py:402
  29.7 2.6 %scatter_rows.1.slot_half = f32[1088,512]{1,0:T(8,128)S(1)} custom-call(s32[4,1024]{1,0:T(4,128)S(1)} %copy-done.8, bf16[4096,512]{1,0:T(8,128)(2,1)S(1)} %get-tuple-element.34.pgrad), custom_call_target="tpu_custom_call" | custom-call | flops 2281701376 | bytes 2097152 | tf_op jit(solution)/shard_map/scatter_rows/pallas_call | solution.py:477
  32.4 0.2 convert_add_fusion
  32.6 0.5 collective-permute-start.1
  33.1 4.2 %backward_rows.1 = (f32[384,512]{1,0:T(8,128)S(1)}, bf16[384,512]{1,0:T(8,128)(2,1)S(1)}) custom-call(s32[4,1024]{1,0:T(4,128)S(1)} %copy-done.8, bf16[4096,512]{1,0:T(8,128)(2,1)S(1)} %get-tuple-element.34.pgrad, f32[1088,512]{1,0:T(8,128)S(1)} %scatter_rows.1.slot_half, bf16[1088,512]{1,0:T(8,128)(2,1)S(1)} %get-tuple-element.42.latent, ...), custom_call_target="tpu_custom_call" | custom-call | flops 3992977408 | bytes 2097152 | tf_op jit(solution)/shard_map/backward_rows/pallas_call | solution.py:494
  37.4 0.2 collective-permute-start.2
  37.6 1.2 %mesh_rows.1 = bf16[512,512]{1,0:T(8,128)(2,1)} custom-call(bf16[512,512]{1,0:T(8,128)(2,1)S(1)} %copy-done, bf16[512,512]{1,0:T(8,128)(2,1)S(1)} %get-tuple-element.33.hid_sum, bf16[512,512]{1,0:T(8,128)(2,1)S(1)} %copy-done.1), custom_call_target="tpu_custom_call" | custom-call | flops 268435456 | bytes 2097152 | tf_op jit(solution)/shard_map/mesh_rows/pallas_call | solution.py:516
  38.8 0.2 collective-permute-done.1
  39.1 0.1 convert_add_fusion.2
  39.2 0.1 convert_add_fusion.1
  39.3 1.5 %collective-permute-start.8 = (bf16[192,512]{1,0:T(8,128)(2,1)S(1)}, bf16[192,512]{1,0:T(8,128)(2,1)S(1)}, u32[]{:S(2)}, u32[]{:S(2)}) collective-permute-start(bf16[192,512]{1,0:T(8,128)(2,1)S(1)} %slice.56), channel_id=1, source_target_pairs={{0,4},{1,3},{2,6},{3,1},{4,0},{5,7},{6,2},{7,5},{8,12},{9,11},{10,... | collective-permute-start | bytes 589832 | tf_op jit(solution)/shard_map/ppermute | solution.py:454
  40.8 0.6 collective-permute-start.3
  41.4 3.6 %collective-permute-done.8 = bf16[192,512]{1,0:T(8,128)(2,1)S(1)} collective-permute-done((bf16[192,512]{1,0:T(8,128)(2,1)S(1)}, bf16[192,512]{1,0:T(8,128)(2,1)S(1)}, u32[]{:S(2)}, u32[]{:S(2)}) %collective-permute-start.8) | collective-permute-done | bytes 196640 | tf_op jit(solution)/shard_map/ppermute | solution.py:454
  45.2 1.6 %collective-permute-start.9 = (bf16[96,512]{1,0:T(8,128)(2,1)S(1)}, bf16[96,512]{1,0:T(8,128)(2,1)S(1)}, u32[]{:S(2)}, u32[]{:S(2)}) collective-permute-start(bf16[96,512]{1,0:T(8,128)(2,1)S(1)} %slice.58), channel_id=1, source_target_pairs={{0,2},{1,5},{2,0},{3,7},{4,6},{5,1},{6,4},{7,3},{8,10},{9,13},{10,... | collective-permute-start | bytes 294920 | tf_op jit(solution)/shard_map/ppermute | solution.py:454
  46.8 0.6 collective-permute-start.4
  47.4 2.4 %collective-permute-done.9 = bf16[96,512]{1,0:T(8,128)(2,1)S(1)} collective-permute-done((bf16[96,512]{1,0:T(8,128)(2,1)S(1)}, bf16[96,512]{1,0:T(8,128)(2,1)S(1)}, u32[]{:S(2)}, u32[]{:S(2)}) %collective-permute-start.9) | collective-permute-done | bytes 98336 | tf_op jit(solution)/shard_map/ppermute | solution.py:454
  49.9 0.7 collective-permute-start.10
  50.6 7.7 %collective-permute-done.4 = bf16[128,512]{1,0:T(8,128)(2,1)S(1)} collective-permute-done((bf16[128,512]{1,0:T(8,128)(2,1)S(1)}, bf16[128,512]{1,0:T(8,128)(2,1)S(1)}, u32[]{:S(2)}, u32[]{:S(2)}) %collective-permute-start.4) | collective-permute-done | bytes 131104 | tf_op jit(solution)/shard_map/ppermute | solution.py:454
  58.4 0.9 %collective-permute-done.10 = bf16[96,512]{1,0:T(8,128)(2,1)S(1)} collective-permute-done((bf16[96,512]{1,0:T(8,128)(2,1)S(1)}, bf16[96,512]{1,0:T(8,128)(2,1)S(1)}, u32[]{:S(2)}, u32[]{:S(2)}) %collective-permute-start.10) | collective-permute-done | bytes 98336 | tf_op jit(solution)/shard_map/ppermute | solution.py:454
  59.3 1.5 %collective-permute-start.11 = (bf16[96,512]{1,0:T(8,128)(2,1)S(1)}, bf16[96,512]{1,0:T(8,128)(2,1)S(1)}, u32[]{:S(2)}, u32[]{:S(2)}) collective-permute-start(bf16[96,512]{1,0:T(8,128)(2,1)S(1)} %add_convert_fusion.1), channel_id=1, source_target_pairs={{0,2},{1,5},{2,0},{3,7},{4,6},{5,1},{6,4},{7,3},{8,10},{9,13},{10,... | collective-permute-start | bytes 294920 | tf_op jit(solution)/shard_map/ppermute | solution.py:454
  60.8 2.8 %collective-permute-done.5 = bf16[128,512]{1,0:T(8,128)(2,1)S(1)} collective-permute-done((bf16[128,512]{1,0:T(8,128)(2,1)S(1)}, bf16[128,512]{1,0:T(8,128)(2,1)S(1)}, u32[]{:S(2)}, u32[]{:S(2)}) %collective-permute-start.5) | collective-permute-done | bytes 131104 | tf_op jit(solution)/shard_map/ppermute | solution.py:454
  63.6 1.4 %collective-permute-start.6 = (bf16[256,512]{1,0:T(8,128)(2,1)S(1)}, bf16[256,512]{1,0:T(8,128)(2,1)S(1)}, u32[]{:S(2)}, u32[]{:S(2)}) collective-permute-start(bf16[256,512]{1,0:T(8,128)(2,1)S(1)} %pad_maximum_fusion.2), channel_id=1, source_target_pairs={{0,2},{1,5},{2,0},{3,7},{4,6},{5,1},{6,4},{7,3},{8,10},{9,13},{10,... | collective-permute-start | bytes 786440 | tf_op jit(solution)/shard_map/ppermute | solution.py:454
  65.0 0.2 collective-permute-start.12
  65.2 5.8 %collective-permute-done.6 = bf16[256,512]{1,0:T(8,128)(2,1)S(1)} collective-permute-done((bf16[256,512]{1,0:T(8,128)(2,1)S(1)}, bf16[256,512]{1,0:T(8,128)(2,1)S(1)}, u32[]{:S(2)}, u32[]{:S(2)}) %collective-permute-start.6) | collective-permute-done | bytes 262176 | tf_op jit(solution)/shard_map/ppermute | solution.py:454
  71.2 0.5 collective-permute-start.13
  71.7 1.3 %unpack_rows.2 = (f32[512,512]{1,0:T(8,128)}, f32[512,512]{1,0:T(8,128)}, f32[512,512]{1,0:T(8,128)}, f32[227,512]{1,0:T(8,128)}, f32[2,512]{1,0:T(2,128)}) custom-call(bf16[512,512]{1,0:T(8,128)(2,1)S(1)} %pad_maximum_fusion.refs_0_, bf16[384,512]{1,0:T(8,128)(2,1)S(1)} %pad_maximum_fusion.1.refs_1_), custom_call_target="tpu_custom_call" | custom-call | tf_op jit(solution)/shard_map/unpack_rows/pallas_call | solution.py:537
  73.1 0.5 collective-permute-done.13.refs_1_
  73.6 1.3 %unpack_rows.3 = (f32[512,512]{1,0:T(8,128)}, f32[512,512]{1,0:T(8,128)}, f32[512,512]{1,0:T(8,128)}, f32[227,512]{1,0:T(8,128)}, f32[2,512]{1,0:T(2,128)}) custom-call(bf16[512,512]{1,0:T(8,128)(2,1)S(1)} %collective-permute-done.7.refs_0_, ...), custom_call_target="tpu_custom_call", output_to_operand_aliasing={{0}: (2, {}), {1}: (3, {}), {2}: (4, {}), {3}: (5, {}), {4}... | custom-call | tf_op jit(solution)/shard_map/unpack_rows/pallas_call | solution.py:537
  (51 shorter events, 0.7 us)
Async XLA Ops:
  0.6 0.7 copy-start.11
  0.6 1.0 %copy-start.5 = (bf16[1024,227]{0,1:T(8,128)(2,1)S(1)}, bf16[1024,227]{0,1:T(8,128)(2,1)}, u32[]{:S(2)}) copy-start(bf16[1024,227]{0,1:T(8,128)(2,1)} %param.13) | copy-start | bytes 1394692
  1.7 14.3 %copy-start = (bf16[512,512]{1,0:T(8,128)(2,1)S(1)}, bf16[512,512]{1,0:T(8,128)(2,1)}, u32[]{:S(2)}) copy-start(bf16[512,512]{1,0:T(8,128)(2,1)} %mesh.3) | copy-start | bytes 1572868
  1.7 14.3 %copy-start.1 = (bf16[512,512]{1,0:T(8,128)(2,1)S(1)}, bf16[512,512]{1,0:T(8,128)(2,1)}, u32[]{:S(2)}) copy-start(bf16[512,512]{1,0:T(8,128)(2,1)} %w_out.3) | copy-start | bytes 1572868
  1.7 14.3 %copy-start.2 = (bf16[512,512]{1,0:T(8,128)(2,1)S(1)}, bf16[512,512]{1,0:T(8,128)(2,1)}, u32[]{:S(2)}) copy-start(bf16[512,512]{1,0:T(8,128)(2,1)} %w_dst.1) | copy-start | bytes 1572868
  1.7 14.3 %copy-start.3 = (bf16[512,512]{1,0:T(8,128)(2,1)S(1)}, bf16[512,512]{1,0:T(8,128)(2,1)}, u32[]{:S(2)}) copy-start(bf16[512,512]{1,0:T(8,128)(2,1)} %cot.1) | copy-start | bytes 1572868
  1.7 14.3 %copy-start.4 = (bf16[512,512]{1,0:T(8,128)(2,1)S(1)}, bf16[512,512]{1,0:T(8,128)(2,1)}, u32[]{:S(2)}) copy-start(bf16[512,512]{1,0:T(8,128)(2,1)} %w_src.3) | copy-start | bytes 1572868
  1.7 14.3 %copy-start.6 = (bf16[227,512]{1,0:T(8,128)(2,1)S(1)}, bf16[227,512]{1,0:T(8,128)(2,1)}, u32[]{:S(2)}) copy-start(bf16[227,512]{1,0:T(8,128)(2,1)} %w_embed.1) | copy-start | bytes 697348
  1.7 14.3 %copy-start.7 = (s32[4,1024]{1,0:T(4,128)S(1)}, s32[4,1024]{1,0:T(4,128)}, u32[]{:S(2)}) copy-start(s32[4,1024]{1,0:T(4,128)} %dst.1) | copy-start | bytes 49156
  1.7 14.3 %copy-start.8 = (s32[4,1024]{1,0:T(4,128)S(1)}, s32[4,1024]{1,0:T(4,128)}, u32[]{:S(2)}) copy-start(s32[4,1024]{1,0:T(4,128)} %src.5) | copy-start | bytes 49156
  1.7 14.3 %copy-start.9 = (bf16[512]{0:T(512)(128)(2,1)S(1)}, bf16[512]{0:T(512)(128)(2,1)}, u32[]{:S(2)}) copy-start(bf16[512]{0:T(512)(128)(2,1)} %b_embed.1) | copy-start | bytes 3076
  1.7 14.3 %copy-start.10 = (bf16[512]{0:T(512)(128)(2,1)S(1)}, bf16[512]{0:T(512)(128)(2,1)}, u32[]{:S(2)}) copy-start(bf16[512]{0:T(512)(128)(2,1)} %b_hidden.1) | copy-start | bytes 3076
  1.8 14.3 %copy-start.12 = (s32[4]{0:T(128)S(1)}, s32[4]{0:T(128)}, u32[]{:S(2)}) copy-start(s32[4]{0:T(128)} %count.1) | copy-start | bytes 52
  29.7 2.7 %collective-permute-start = (bf16[512,512]{1,0:T(8,128)(2,1)S(1)}, bf16[512,512]{1,0:T(8,128)(2,1)S(1)}, u32[]{:S(2)}, u32[]{:S(2)}) collective-permute-start(bf16[512,512]{1,0:T(8,128)(2,1)S(1)} %get-tuple-element.36), channel_id=1, source_target_pairs={{0,1},{1,0},{2,3},{3,2},{4,5},{5,4},{6,7},{7,6},{8,9},{9,8},{10,11... | collective-permute-start | bytes 1572872 | tf_op jit(solution)/shard_map/ppermute | solution.py:454
  32.6 4.8 %copy-start.13 = (f32[512,512]{1,0:T(8,128)}, f32[512,512]{1,0:T(8,128)S(1)}, u32[]{:S(2)}) copy-start(f32[512,512]{1,0:T(8,128)S(1)} %convert_add_fusion) | copy-start | bytes 3145732
  32.6 6.4 %collective-permute-start.1 = (bf16[256,512]{1,0:T(8,128)(2,1)S(1)}, bf16[256,512]{1,0:T(8,128)(2,1)S(1)}, u32[]{:S(2)}, u32[]{:S(2)}) collective-permute-start(bf16[256,512]{1,0:T(8,128)(2,1)S(1)} %slice.55), channel_id=1, source_target_pairs={{0,2},{1,5},{2,0},{3,7},{4,6},{5,1},{6,4},{7,3},{8,10},{9,13},{10,... | collective-permute-start | bytes 786440 | tf_op jit(solution)/shard_map/ppermute | solution.py:454
  37.4 1.7 %slice-start = ((f32[512,512]{1,0:T(8,128)}), f32[256,512]{1,0:T(8,128)S(1)}, s32[]{:S(2)}) async-start(f32[512,512]{1,0:T(8,128)} %copy-done.13), calls=%async_computation.1 | async-start | bytes 1048576 | tf_op jit(solution)/shard_map/slice | solution.py:460
  37.4 1.8 %collective-permute-start.2 = (bf16[384,512]{1,0:T(8,128)(2,1)S(1)}, bf16[384,512]{1,0:T(8,128)(2,1)S(1)}, u32[]{:S(2)}, u32[]{:S(2)}) collective-permute-start(bf16[384,512]{1,0:T(8,128)(2,1)S(1)} %get-tuple-element.47), channel_id=1, source_target_pairs={{0,1},{1,0},{2,3},{3,2},{4,5},{5,4},{6,7},{7,6},{8,9},{9,8},{10,11... | collective-permute-start | bytes 1179656 | tf_op jit(solution)/shard_map/ppermute | solution.py:454
  39.3 5.7 %collective-permute-start.8 = (bf16[192,512]{1,0:T(8,128)(2,1)S(1)}, bf16[192,512]{1,0:T(8,128)(2,1)S(1)}, u32[]{:S(2)}, u32[]{:S(2)}) collective-permute-start(bf16[192,512]{1,0:T(8,128)(2,1)S(1)} %slice.56), channel_id=1, source_target_pairs={{0,4},{1,3},{2,6},{3,1},{4,0},{5,7},{6,2},{7,5},{8,12},{9,11},{10,... | collective-permute-start | bytes 589832 | tf_op jit(solution)/shard_map/ppermute | solution.py:454
  40.8 6.0 %collective-permute-start.3 = (bf16[128,512]{1,0:T(8,128)(2,1)S(1)}, bf16[128,512]{1,0:T(8,128)(2,1)S(1)}, u32[]{:S(2)}, u32[]{:S(2)}) collective-permute-start(bf16[128,512]{1,0:T(8,128)(2,1)S(1)} %slice.57), channel_id=1, source_target_pairs={{0,4},{1,3},{2,6},{3,1},{4,0},{5,7},{6,2},{7,5},{8,12},{9,11},{10,... | collective-permute-start | bytes 393224 | tf_op jit(solution)/shard_map/ppermute | solution.py:454
  45.2 4.7 %collective-permute-start.9 = (bf16[96,512]{1,0:T(8,128)(2,1)S(1)}, bf16[96,512]{1,0:T(8,128)(2,1)S(1)}, u32[]{:S(2)}, u32[]{:S(2)}) collective-permute-start(bf16[96,512]{1,0:T(8,128)(2,1)S(1)} %slice.58), channel_id=1, source_target_pairs={{0,2},{1,5},{2,0},{3,7},{4,6},{5,1},{6,4},{7,3},{8,10},{9,13},{10,... | collective-permute-start | bytes 294920 | tf_op jit(solution)/shard_map/ppermute | solution.py:454
  46.8 11.4 %collective-permute-start.4 = (bf16[128,512]{1,0:T(8,128)(2,1)S(1)}, bf16[128,512]{1,0:T(8,128)(2,1)S(1)}, u32[]{:S(2)}, u32[]{:S(2)}) collective-permute-start(bf16[128,512]{1,0:T(8,128)(2,1)S(1)} %fusion), channel_id=1, source_target_pairs={{0,8},{1,9},{2,10},{3,11},{4,12},{5,13},{6,14},{7,15},{8,0},{9,1},... | collective-permute-start | bytes 393224 | tf_op jit(solution)/shard_map/ppermute | solution.py:454
  49.9 9.5 %collective-permute-start.10 = (bf16[96,512]{1,0:T(8,128)(2,1)S(1)}, bf16[96,512]{1,0:T(8,128)(2,1)S(1)}, u32[]{:S(2)}, u32[]{:S(2)}) collective-permute-start(bf16[96,512]{1,0:T(8,128)(2,1)S(1)} %fusion.1), channel_id=1, source_target_pairs={{0,8},{1,9},{2,10},{3,11},{4,12},{5,13},{6,14},{7,15},{8,0},{9,1},... | collective-permute-start | bytes 294920 | tf_op jit(solution)/shard_map/ppermute | solution.py:454
  58.3 5.3 %collective-permute-start.5 = (bf16[128,512]{1,0:T(8,128)(2,1)S(1)}, bf16[128,512]{1,0:T(8,128)(2,1)S(1)}, u32[]{:S(2)}, u32[]{:S(2)}) collective-permute-start(bf16[128,512]{1,0:T(8,128)(2,1)S(1)} %add_convert_fusion), channel_id=1, source_target_pairs={{0,4},{1,3},{2,6},{3,1},{4,0},{5,7},{6,2},{7,5},{8,12},{9,11},{10,... | collective-permute-start | bytes 393224 | tf_op jit(solution)/shard_map/ppermute | solution.py:454
  59.3 5.7 %collective-permute-start.11 = (bf16[96,512]{1,0:T(8,128)(2,1)S(1)}, bf16[96,512]{1,0:T(8,128)(2,1)S(1)}, u32[]{:S(2)}, u32[]{:S(2)}) collective-permute-start(bf16[96,512]{1,0:T(8,128)(2,1)S(1)} %add_convert_fusion.1), channel_id=1, source_target_pairs={{0,2},{1,5},{2,0},{3,7},{4,6},{5,1},{6,4},{7,3},{8,10},{9,13},{10,... | collective-permute-start | bytes 294920 | tf_op jit(solution)/shard_map/ppermute | solution.py:454
  63.6 7.4 %collective-permute-start.6 = (bf16[256,512]{1,0:T(8,128)(2,1)S(1)}, bf16[256,512]{1,0:T(8,128)(2,1)S(1)}, u32[]{:S(2)}, u32[]{:S(2)}) collective-permute-start(bf16[256,512]{1,0:T(8,128)(2,1)S(1)} %pad_maximum_fusion.2), channel_id=1, source_target_pairs={{0,2},{1,5},{2,0},{3,7},{4,6},{5,1},{6,4},{7,3},{8,10},{9,13},{10,... | collective-permute-start | bytes 786440 | tf_op jit(solution)/shard_map/ppermute | solution.py:454
  65.0 6.1 %collective-permute-start.12 = (bf16[192,512]{1,0:T(8,128)(2,1)S(1)}, bf16[192,512]{1,0:T(8,128)(2,1)S(1)}, u32[]{:S(2)}, u32[]{:S(2)}) collective-permute-start(bf16[192,512]{1,0:T(8,128)(2,1)S(1)} %pad_maximum_fusion.3), channel_id=1, source_target_pairs={{0,4},{1,3},{2,6},{3,1},{4,0},{5,7},{6,2},{7,5},{8,12},{9,11},{10,... | collective-permute-start | bytes 589832 | tf_op jit(solution)/shard_map/ppermute | solution.py:454
  71.1 2.5 %collective-permute-start.7 = (bf16[512,512]{1,0:T(8,128)(2,1)S(1)}, bf16[512,512]{1,0:T(8,128)(2,1)S(1)}, u32[]{:S(2)}, u32[]{:S(2)}) collective-permute-start(bf16[512,512]{1,0:T(8,128)(2,1)S(1)} %pad_maximum_fusion.refs_0_), channel_id=1, source_target_pairs={{0,1},{1,0},{2,3},{3,2},{4,5},{5,4},{6,7},{7,6},{8,9},{9,8},{10,11... | collective-permute-start | bytes 1572872 | tf_op jit(solution)/shard_map/ppermute | solution.py:454
  71.2 2.4 %collective-permute-start.13 = (bf16[384,512]{1,0:T(8,128)(2,1)S(1)}, bf16[384,512]{1,0:T(8,128)(2,1)S(1)}, u32[]{:S(2)}, u32[]{:S(2)}) collective-permute-start(bf16[384,512]{1,0:T(8,128)(2,1)S(1)} %pad_maximum_fusion.1.refs_1_), channel_id=1, source_target_pairs={{0,1},{1,0},{2,3},{3,2},{4,5},{5,4},{6,7},{7,6},{8,9},{9,8},{10,11... | collective-permute-start | bytes 1179656 | tf_op jit(solution)/shard_map/ppermute | solution.py:454

commit v10 on v9

--- a/solution.py
+++ b/solution.py
@@ -150,7 +150,7 @@
         pre = mm(feat[r:end, :], w_pad[...])
         sig = sigmoid(pre)
         lat = (pre * sig).astype(BF16)
-        latent[r:end, :] = lat
+        latent[:, r:end] = jnp.transpose(lat)
         slope[r:end, :] = sig * (1.0 + pre * (1.0 - sig))
         table[block + r : block + end, :] = halved(mm(lat, w_src[...]).astype(BF16))
     near[...] = halved(mm(mesh[...], w_dst[...]).astype(BF16))
@@ -264,7 +264,7 @@
     rest = src.shape[0] - half
     slot_sum = slot_half[...] + scatter_rows(src, pgrad, one_hot_t, half, rest)
     slot_grad = slot_sum.astype(BF16)
-    grads[0:width, :] = mm(latent[...], slot_grad, 0, 0)
+    grads[0:width, :] = mm(latent[...], slot_grad)
     buffer_grad = mm(slot_grad, w_src[...], 1, 1)
     embed = (buffer_grad * slope[...]).astype(BF16)
     grads[width : width + padded, :] = mm(feat[...], embed, 0, 0)
@@ -404,7 +404,7 @@
         out_shape=(
             shape((nodes, width), BF16),
             shape((blocks * edges, width), BF16),
-            shape((slots, width), BF16),
+            shape((width, slots), BF16),
             shape((slots, padded), BF16),
             shape((slots, width), F32),
             shape((8, width), F32),

time: 75.3 us -> 75.3 us (level)
  no operation moved by 1% of the time
where the time goes in v10:
time: 75.3 us; the launch traced here: 75.2 us
  Pallas kernels  24.7 us (33%)
  waiting for transfers between devices  24.2 us (32%)
  blocking collectives  13.9 us (18%)
  starting transfers between devices  9.46 us (13%)
  local copies, waits for them, and re-layouts  1.18 us (2%)
  between operations  1.17 us (2%)
    ppermute x14, waiting for transfers between devices, swap(): lax.ppermute(values, 'dom', [(d, d ^ 1 << bits[d % 2]) for d in range(dev...  24.2 us
    all_to_all x1, blocking collectives, shards(): lax.all_to_all(send, 'dom', split_axis=0, concat_axis=0, tiled=True)  13.9 us
    pallas_call x1, Pallas kernels, shards(): pl.pallas_call(functools.partial(forward_kernel, device_count), out_shape...  13.6 us
    ppermute x14, starting transfers between devices, swap(): lax.ppermute(values, 'dom', [(d, d ^ 1 << bits[d % 2]) for d in range(dev...  9.46 us
    pallas_call x1, Pallas kernels, shards(): pl.pallas_call(functools.partial(backward_kernel, channels, device_count)...  4.21 us
    pallas_call x2, Pallas kernels, unpack(): pl.pallas_call(functools.partial(unpack_kernel, device_count, chains, own...  2.67 us
    pallas_call x1, Pallas kernels, shards(): pl.pallas_call(scatter_kernel, out_shape=shape((slots, width), F32), in_s...  2.66 us
  transfers between devices with their start and end apart: 14, of which 8 were waited for; matrix products, arithmetic and copies ran while one was open for 0% of the time, Pallas kernels for 13%

profile of v10, /device:TPU:0, one launch (start us, length us, event | category | flops | bytes accessed | tf_op | source)
XLA Modules:
  0.0 75.2 jit_solution(2690157403184762108)
XLA Ops:
  0.7 0.6 copy-done.11
  1.3 0.4 copy-done.5
  1.8 0.3 pick_rows.1
  2.1 13.9 %all_to_all.5.feat_in = bf16[16,4,256]{2,1,0:T(4,128)(2,1)S(1)} all-to-all(bf16[16,4,256]{2,1,0:T(4,128)(2,1)S(1)} %pick_rows.1), channel_id=1, replica_groups=mesh['ens'=2,'dom'=16] {'dom'}, dimensions={0} | all-to-all | bytes 65536 | tf_op jit(solution)/shard_map/all_to_all | solution.py:395
  16.1 13.6 %forward_rows.1 = (bf16[512,512]{1,0:T(8,128)(2,1)S(1)}, bf16[4096,512]{1,0:T(8,128)(2,1)S(1)}, bf16[512,1088]{1,0:T(8,128)(2,1)S(1)}, bf16[1088,256]{1,0:T(8,12...) custom-call(s32[4]{0:T(128)S(1)} %copy-done.12, ...), custom_call_target="tpu_custom_call" | custom-call | flops 9714008064 | bytes 8388608 | tf_op jit(solution)/shard_map/forward_rows/pallas_call | solution.py:402
  29.7 0.1 collective-permute-start
  29.8 2.7 %scatter_rows.1.slot_half = f32[1088,512]{1,0:T(8,128)S(1)} custom-call(s32[4,1024]{1,0:T(4,128)S(1)} %copy-done.8, bf16[4096,512]{1,0:T(8,128)(2,1)S(1)} %get-tuple-element.34.pgrad), custom_call_target="tpu_custom_call" | custom-call | flops 2281701376 | bytes 2097152 | tf_op jit(solution)/shard_map/scatter_rows/pallas_call | solution.py:477
  32.4 0.2 convert_add_fusion
  32.6 0.5 collective-permute-start.1
  33.2 4.2 %backward_rows.1 = (f32[384,512]{1,0:T(8,128)S(1)}, bf16[384,512]{1,0:T(8,128)(2,1)S(1)}) custom-call(s32[4,1024]{1,0:T(4,128)S(1)} %copy-done.8, bf16[4096,512]{1,0:T(8,128)(2,1)S(1)} %get-tuple-element.34.pgrad, f32[1088,512]{1,0:T(8,128)S(1)} %scatter_rows.1.slot_half, bf16[512,1088]{1,0:T(8,128)(2,1)S(1)} %get-tuple-element.42.latent, ...), custom_call_target="tpu_custom_call" | custom-call | flops 3992977408 | bytes 2097152 | tf_op jit(solution)/shard_map/backward_rows/pallas_call | solution.py:494
  37.4 0.2 collective-permute-start.2
  37.6 1.2 %mesh_rows.1 = bf16[512,512]{1,0:T(8,128)(2,1)} custom-call(bf16[512,512]{1,0:T(8,128)(2,1)S(1)} %copy-done, bf16[512,512]{1,0:T(8,128)(2,1)S(1)} %get-tuple-element.33.hid_sum, bf16[512,512]{1,0:T(8,128)(2,1)S(1)} %copy-done.1), custom_call_target="tpu_custom_call" | custom-call | flops 268435456 | bytes 2097152 | tf_op jit(solution)/shard_map/mesh_rows/pallas_call | solution.py:516
  38.8 0.3 collective-permute-done.1
  39.1 0.1 convert_add_fusion.2
  39.2 0.1 convert_add_fusion.1
  39.4 1.5 %collective-permute-start.8 = (bf16[192,512]{1,0:T(8,128)(2,1)S(1)}, bf16[192,512]{1,0:T(8,128)(2,1)S(1)}, u32[]{:S(2)}, u32[]{:S(2)}) collective-permute-start(bf16[192,512]{1,0:T(8,128)(2,1)S(1)} %slice.56), channel_id=1, source_target_pairs={{0,4},{1,3},{2,6},{3,1},{4,0},{5,7},{6,2},{7,5},{8,12},{9,11},{10,... | collective-permute-start | bytes 589832 | tf_op jit(solution)/shard_map/ppermute | solution.py:454
  40.8 0.6 collective-permute-start.3
  41.5 3.6 %collective-permute-done.8 = bf16[192,512]{1,0:T(8,128)(2,1)S(1)} collective-permute-done((bf16[192,512]{1,0:T(8,128)(2,1)S(1)}, bf16[192,512]{1,0:T(8,128)(2,1)S(1)}, u32[]{:S(2)}, u32[]{:S(2)}) %collective-permute-start.8) | collective-permute-done | bytes 196640 | tf_op jit(solution)/shard_map/ppermute | solution.py:454
  45.2 1.6 %collective-permute-start.9 = (bf16[96,512]{1,0:T(8,128)(2,1)S(1)}, bf16[96,512]{1,0:T(8,128)(2,1)S(1)}, u32[]{:S(2)}, u32[]{:S(2)}) collective-permute-start(bf16[96,512]{1,0:T(8,128)(2,1)S(1)} %slice.58), channel_id=1, source_target_pairs={{0,2},{1,5},{2,0},{3,7},{4,6},{5,1},{6,4},{7,3},{8,10},{9,13},{10,... | collective-permute-start | bytes 294920 | tf_op jit(solution)/shard_map/ppermute | solution.py:454
  46.8 0.6 collective-permute-start.4
  47.4 2.5 %collective-permute-done.9 = bf16[96,512]{1,0:T(8,128)(2,1)S(1)} collective-permute-done((bf16[96,512]{1,0:T(8,128)(2,1)S(1)}, bf16[96,512]{1,0:T(8,128)(2,1)S(1)}, u32[]{:S(2)}, u32[]{:S(2)}) %collective-permute-start.9) | collective-permute-done | bytes 98336 | tf_op jit(solution)/shard_map/ppermute | solution.py:454
  49.9 0.7 collective-permute-start.10
  50.6 7.7 %collective-permute-done.4 = bf16[128,512]{1,0:T(8,128)(2,1)S(1)} collective-permute-done((bf16[128,512]{1,0:T(8,128)(2,1)S(1)}, bf16[128,512]{1,0:T(8,128)(2,1)S(1)}, u32[]{:S(2)}, u32[]{:S(2)}) %collective-permute-start.4) | collective-permute-done | bytes 131104 | tf_op jit(solution)/shard_map/ppermute | solution.py:454
  58.4 0.9 %collective-permute-done.10 = bf16[96,512]{1,0:T(8,128)(2,1)S(1)} collective-permute-done((bf16[96,512]{1,0:T(8,128)(2,1)S(1)}, bf16[96,512]{1,0:T(8,128)(2,1)S(1)}, u32[]{:S(2)}, u32[]{:S(2)}) %collective-permute-start.10) | collective-permute-done | bytes 98336 | tf_op jit(solution)/shard_map/ppermute | solution.py:454
  59.3 1.5 %collective-permute-start.11 = (bf16[96,512]{1,0:T(8,128)(2,1)S(1)}, bf16[96,512]{1,0:T(8,128)(2,1)S(1)}, u32[]{:S(2)}, u32[]{:S(2)}) collective-permute-start(bf16[96,512]{1,0:T(8,128)(2,1)S(1)} %add_convert_fusion.1), channel_id=1, source_target_pairs={{0,2},{1,5},{2,0},{3,7},{4,6},{5,1},{6,4},{7,3},{8,10},{9,13},{10,... | collective-permute-start | bytes 294920 | tf_op jit(solution)/shard_map/ppermute | solution.py:454
  60.8 2.9 %collective-permute-done.5 = bf16[128,512]{1,0:T(8,128)(2,1)S(1)} collective-permute-done((bf16[128,512]{1,0:T(8,128)(2,1)S(1)}, bf16[128,512]{1,0:T(8,128)(2,1)S(1)}, u32[]{:S(2)}, u32[]{:S(2)}) %collective-permute-start.5) | collective-permute-done | bytes 131104 | tf_op jit(solution)/shard_map/ppermute | solution.py:454
  63.7 1.5 %collective-permute-start.6 = (bf16[256,512]{1,0:T(8,128)(2,1)S(1)}, bf16[256,512]{1,0:T(8,128)(2,1)S(1)}, u32[]{:S(2)}, u32[]{:S(2)}) collective-permute-start(bf16[256,512]{1,0:T(8,128)(2,1)S(1)} %pad_maximum_fusion.2), channel_id=1, source_target_pairs={{0,2},{1,5},{2,0},{3,7},{4,6},{5,1},{6,4},{7,3},{8,10},{9,13},{10,... | collective-permute-start | bytes 786440 | tf_op jit(solution)/shard_map/ppermute | solution.py:454
  65.3 5.7 %collective-permute-done.6 = bf16[256,512]{1,0:T(8,128)(2,1)S(1)} collective-permute-done((bf16[256,512]{1,0:T(8,128)(2,1)S(1)}, bf16[256,512]{1,0:T(8,128)(2,1)S(1)}, u32[]{:S(2)}, u32[]{:S(2)}) %collective-permute-start.6) | collective-permute-done | bytes 262176 | tf_op jit(solution)/shard_map/ppermute | solution.py:454
  71.2 0.5 collective-permute-start.13
  71.8 1.3 %unpack_rows.2 = (f32[512,512]{1,0:T(8,128)}, f32[512,512]{1,0:T(8,128)}, f32[512,512]{1,0:T(8,128)}, f32[227,512]{1,0:T(8,128)}, f32[2,512]{1,0:T(2,128)}) custom-call(bf16[512,512]{1,0:T(8,128)(2,1)S(1)} %pad_maximum_fusion.refs_0_, bf16[384,512]{1,0:T(8,128)(2,1)S(1)} %pad_maximum_fusion.1.refs_1_), custom_call_target="tpu_custom_call" | custom-call | tf_op jit(solution)/shard_map/unpack_rows/pallas_call | solution.py:537
  73.1 0.5 collective-permute-done.13.refs_1_
  73.7 1.3 %unpack_rows.3 = (f32[512,512]{1,0:T(8,128)}, f32[512,512]{1,0:T(8,128)}, f32[512,512]{1,0:T(8,128)}, f32[227,512]{1,0:T(8,128)}, f32[2,512]{1,0:T(2,128)}) custom-call(bf16[512,512]{1,0:T(8,128)(2,1)S(1)} %collective-permute-done.7.refs_0_, ...), custom_call_target="tpu_custom_call", output_to_operand_aliasing={{0}: (2, {}), {1}: (3, {}), {2}: (4, {}), {3}: (5, {}), {4}... | custom-call | tf_op jit(solution)/shard_map/unpack_rows/pallas_call | solution.py:537
  (51 shorter events, 0.7 us)
Async XLA Ops:
  0.6 0.7 copy-start.11
  0.6 1.0 %copy-start.5 = (bf16[1024,227]{0,1:T(8,128)(2,1)S(1)}, bf16[1024,227]{0,1:T(8,128)(2,1)}, u32[]{:S(2)}) copy-start(bf16[1024,227]{0,1:T(8,128)(2,1)} %param.13) | copy-start | bytes 1394692
  1.7 14.3 %copy-start = (bf16[512,512]{1,0:T(8,128)(2,1)S(1)}, bf16[512,512]{1,0:T(8,128)(2,1)}, u32[]{:S(2)}) copy-start(bf16[512,512]{1,0:T(8,128)(2,1)} %mesh.3) | copy-start | bytes 1572868
  1.7 14.3 %copy-start.1 = (bf16[512,512]{1,0:T(8,128)(2,1)S(1)}, bf16[512,512]{1,0:T(8,128)(2,1)}, u32[]{:S(2)}) copy-start(bf16[512,512]{1,0:T(8,128)(2,1)} %w_out.3) | copy-start | bytes 1572868
  1.7 14.3 %copy-start.2 = (bf16[512,512]{1,0:T(8,128)(2,1)S(1)}, bf16[512,512]{1,0:T(8,128)(2,1)}, u32[]{:S(2)}) copy-start(bf16[512,512]{1,0:T(8,128)(2,1)} %w_dst.1) | copy-start | bytes 1572868
  1.7 14.3 %copy-start.3 = (bf16[512,512]{1,0:T(8,128)(2,1)S(1)}, bf16[512,512]{1,0:T(8,128)(2,1)}, u32[]{:S(2)}) copy-start(bf16[512,512]{1,0:T(8,128)(2,1)} %cot.1) | copy-start | bytes 1572868
  1.7 14.3 %copy-start.4 = (bf16[512,512]{1,0:T(8,128)(2,1)S(1)}, bf16[512,512]{1,0:T(8,128)(2,1)}, u32[]{:S(2)}) copy-start(bf16[512,512]{1,0:T(8,128)(2,1)} %w_src.3) | copy-start | bytes 1572868
  1.7 14.3 %copy-start.6 = (bf16[227,512]{1,0:T(8,128)(2,1)S(1)}, bf16[227,512]{1,0:T(8,128)(2,1)}, u32[]{:S(2)}) copy-start(bf16[227,512]{1,0:T(8,128)(2,1)} %w_embed.1) | copy-start | bytes 697348
  1.7 14.3 %copy-start.7 = (s32[4,1024]{1,0:T(4,128)S(1)}, s32[4,1024]{1,0:T(4,128)}, u32[]{:S(2)}) copy-start(s32[4,1024]{1,0:T(4,128)} %dst.1) | copy-start | bytes 49156
  1.7 14.3 %copy-start.8 = (s32[4,1024]{1,0:T(4,128)S(1)}, s32[4,1024]{1,0:T(4,128)}, u32[]{:S(2)}) copy-start(s32[4,1024]{1,0:T(4,128)} %src.5) | copy-start | bytes 49156
  1.7 14.3 %copy-start.9 = (bf16[512]{0:T(512)(128)(2,1)S(1)}, bf16[512]{0:T(512)(128)(2,1)}, u32[]{:S(2)}) copy-start(bf16[512]{0:T(512)(128)(2,1)} %b_embed.1) | copy-start | bytes 3076
  1.7 14.3 %copy-start.10 = (bf16[512]{0:T(512)(128)(2,1)S(1)}, bf16[512]{0:T(512)(128)(2,1)}, u32[]{:S(2)}) copy-start(bf16[512]{0:T(512)(128)(2,1)} %b_hidden.1) | copy-start | bytes 3076
  1.8 14.3 %copy-start.12 = (s32[4]{0:T(128)S(1)}, s32[4]{0:T(128)}, u32[]{:S(2)}) copy-start(s32[4]{0:T(128)} %count.1) | copy-start | bytes 52
  29.7 2.7 %collective-permute-start = (bf16[512,512]{1,0:T(8,128)(2,1)S(1)}, bf16[512,512]{1,0:T(8,128)(2,1)S(1)}, u32[]{:S(2)}, u32[]{:S(2)}) collective-permute-start(bf16[512,512]{1,0:T(8,128)(2,1)S(1)} %get-tuple-element.36), channel_id=1, source_target_pairs={{0,1},{1,0},{2,3},{3,2},{4,5},{5,4},{6,7},{7,6},{8,9},{9,8},{10,11... | collective-permute-start | bytes 1572872 | tf_op jit(solution)/shard_map/ppermute | solution.py:454
  32.6 4.8 %copy-start.13 = (f32[512,512]{1,0:T(8,128)}, f32[512,512]{1,0:T(8,128)S(1)}, u32[]{:S(2)}) copy-start(f32[512,512]{1,0:T(8,128)S(1)} %convert_add_fusion) | copy-start | bytes 3145732
  32.6 6.4 %collective-permute-start.1 = (bf16[256,512]{1,0:T(8,128)(2,1)S(1)}, bf16[256,512]{1,0:T(8,128)(2,1)S(1)}, u32[]{:S(2)}, u32[]{:S(2)}) collective-permute-start(bf16[256,512]{1,0:T(8,128)(2,1)S(1)} %slice.55), channel_id=1, source_target_pairs={{0,2},{1,5},{2,0},{3,7},{4,6},{5,1},{6,4},{7,3},{8,10},{9,13},{10,... | collective-permute-start | bytes 786440 | tf_op jit(solution)/shard_map/ppermute | solution.py:454
  37.4 1.7 %slice-start = ((f32[512,512]{1,0:T(8,128)}), f32[256,512]{1,0:T(8,128)S(1)}, s32[]{:S(2)}) async-start(f32[512,512]{1,0:T(8,128)} %copy-done.13), calls=%async_computation.1 | async-start | bytes 1048576 | tf_op jit(solution)/shard_map/slice | solution.py:460
  37.4 1.8 %collective-permute-start.2 = (bf16[384,512]{1,0:T(8,128)(2,1)S(1)}, bf16[384,512]{1,0:T(8,128)(2,1)S(1)}, u32[]{:S(2)}, u32[]{:S(2)}) collective-permute-start(bf16[384,512]{1,0:T(8,128)(2,1)S(1)} %get-tuple-element.47), channel_id=1, source_target_pairs={{0,1},{1,0},{2,3},{3,2},{4,5},{5,4},{6,7},{7,6},{8,9},{9,8},{10,11... | collective-permute-start | bytes 1179656 | tf_op jit(solution)/shard_map/ppermute | solution.py:454
  39.4 5.7 %collective-permute-start.8 = (bf16[192,512]{1,0:T(8,128)(2,1)S(1)}, bf16[192,512]{1,0:T(8,128)(2,1)S(1)}, u32[]{:S(2)}, u32[]{:S(2)}) collective-permute-start(bf16[192,512]{1,0:T(8,128)(2,1)S(1)} %slice.56), channel_id=1, source_target_pairs={{0,4},{1,3},{2,6},{3,1},{4,0},{5,7},{6,2},{7,5},{8,12},{9,11},{10,... | collective-permute-start | bytes 589832 | tf_op jit(solution)/shard_map/ppermute | solution.py:454
  40.8 6.0 %collective-permute-start.3 = (bf16[128,512]{1,0:T(8,128)(2,1)S(1)}, bf16[128,512]{1,0:T(8,128)(2,1)S(1)}, u32[]{:S(2)}, u32[]{:S(2)}) collective-permute-start(bf16[128,512]{1,0:T(8,128)(2,1)S(1)} %slice.57), channel_id=1, source_target_pairs={{0,4},{1,3},{2,6},{3,1},{4,0},{5,7},{6,2},{7,5},{8,12},{9,11},{10,... | collective-permute-start | bytes 393224 | tf_op jit(solution)/shard_map/ppermute | solution.py:454
  45.2 4.7 %collective-permute-start.9 = (bf16[96,512]{1,0:T(8,128)(2,1)S(1)}, bf16[96,512]{1,0:T(8,128)(2,1)S(1)}, u32[]{:S(2)}, u32[]{:S(2)}) collective-permute-start(bf16[96,512]{1,0:T(8,128)(2,1)S(1)} %slice.58), channel_id=1, source_target_pairs={{0,2},{1,5},{2,0},{3,7},{4,6},{5,1},{6,4},{7,3},{8,10},{9,13},{10,... | collective-permute-start | bytes 294920 | tf_op jit(solution)/shard_map/ppermute | solution.py:454
  46.8 11.4 %collective-permute-start.4 = (bf16[128,512]{1,0:T(8,128)(2,1)S(1)}, bf16[128,512]{1,0:T(8,128)(2,1)S(1)}, u32[]{:S(2)}, u32[]{:S(2)}) collective-permute-start(bf16[128,512]{1,0:T(8,128)(2,1)S(1)} %fusion), channel_id=1, source_target_pairs={{0,8},{1,9},{2,10},{3,11},{4,12},{5,13},{6,14},{7,15},{8,0},{9,1},... | collective-permute-start | bytes 393224 | tf_op jit(solution)/shard_map/ppermute | solution.py:454
  49.9 9.4 %collective-permute-start.10 = (bf16[96,512]{1,0:T(8,128)(2,1)S(1)}, bf16[96,512]{1,0:T(8,128)(2,1)S(1)}, u32[]{:S(2)}, u32[]{:S(2)}) collective-permute-start(bf16[96,512]{1,0:T(8,128)(2,1)S(1)} %fusion.1), channel_id=1, source_target_pairs={{0,8},{1,9},{2,10},{3,11},{4,12},{5,13},{6,14},{7,15},{8,0},{9,1},... | collective-permute-start | bytes 294920 | tf_op jit(solution)/shard_map/ppermute | solution.py:454
  58.3 5.4 %collective-permute-start.5 = (bf16[128,512]{1,0:T(8,128)(2,1)S(1)}, bf16[128,512]{1,0:T(8,128)(2,1)S(1)}, u32[]{:S(2)}, u32[]{:S(2)}) collective-permute-start(bf16[128,512]{1,0:T(8,128)(2,1)S(1)} %add_convert_fusion), channel_id=1, source_target_pairs={{0,4},{1,3},{2,6},{3,1},{4,0},{5,7},{6,2},{7,5},{8,12},{9,11},{10,... | collective-permute-start | bytes 393224 | tf_op jit(solution)/shard_map/ppermute | solution.py:454
  59.3 5.9 %collective-permute-start.11 = (bf16[96,512]{1,0:T(8,128)(2,1)S(1)}, bf16[96,512]{1,0:T(8,128)(2,1)S(1)}, u32[]{:S(2)}, u32[]{:S(2)}) collective-permute-start(bf16[96,512]{1,0:T(8,128)(2,1)S(1)} %add_convert_fusion.1), channel_id=1, source_target_pairs={{0,2},{1,5},{2,0},{3,7},{4,6},{5,1},{6,4},{7,3},{8,10},{9,13},{10,... | collective-permute-start | bytes 294920 | tf_op jit(solution)/shard_map/ppermute | solution.py:454
  63.7 7.4 %collective-permute-start.6 = (bf16[256,512]{1,0:T(8,128)(2,1)S(1)}, bf16[256,512]{1,0:T(8,128)(2,1)S(1)}, u32[]{:S(2)}, u32[]{:S(2)}) collective-permute-start(bf16[256,512]{1,0:T(8,128)(2,1)S(1)} %pad_maximum_fusion.2), channel_id=1, source_target_pairs={{0,2},{1,5},{2,0},{3,7},{4,6},{5,1},{6,4},{7,3},{8,10},{9,13},{10,... | collective-permute-start | bytes 786440 | tf_op jit(solution)/shard_map/ppermute | solution.py:454
  65.3 5.9 %collective-permute-start.12 = (bf16[192,512]{1,0:T(8,128)(2,1)S(1)}, bf16[192,512]{1,0:T(8,128)(2,1)S(1)}, u32[]{:S(2)}, u32[]{:S(2)}) collective-permute-start(bf16[192,512]{1,0:T(8,128)(2,1)S(1)} %pad_maximum_fusion.3), channel_id=1, source_target_pairs={{0,4},{1,3},{2,6},{3,1},{4,0},{5,7},{6,2},{7,5},{8,12},{9,11},{10,... | collective-permute-start | bytes 589832 | tf_op jit(solution)/shard_map/ppermute | solution.py:454
  71.1 2.5 %collective-permute-start.7 = (bf16[512,512]{1,0:T(8,128)(2,1)S(1)}, bf16[512,512]{1,0:T(8,128)(2,1)S(1)}, u32[]{:S(2)}, u32[]{:S(2)}) collective-permute-start(bf16[512,512]{1,0:T(8,128)(2,1)S(1)} %pad_maximum_fusion.refs_0_), channel_id=1, source_target_pairs={{0,1},{1,0},{2,3},{3,2},{4,5},{5,4},{6,7},{7,6},{8,9},{9,8},{10,11... | collective-permute-start | bytes 1572872 | tf_op jit(solution)/shard_map/ppermute | solution.py:454
  71.2 2.4 %collective-permute-start.13 = (bf16[384,512]{1,0:T(8,128)(2,1)S(1)}, bf16[384,512]{1,0:T(8,128)(2,1)S(1)}, u32[]{:S(2)}, u32[]{:S(2)}) collective-permute-start(bf16[384,512]{1,0:T(8,128)(2,1)S(1)} %pad_maximum_fusion.1.refs_1_), channel_id=1, source_target_pairs={{0,1},{1,0},{2,3},{3,2},{4,5},{5,4},{6,7},{7,6},{8,9},{9,8},{10,11... | collective-permute-start | bytes 1179656 | tf_op jit(solution)/shard_map/ppermute | solution.py:454
